TPU v7x, 512 devices: a whole 4x8x8 slice. The times are simulated.
512 devices in a mesh: blk: 64 (over y, z_lo, core), head: 8 (over z_hi, x).
Axes of the slice: x: 4, y: 8, z: 8 (z_hi: 2, z_lo: 4; z = z_hi * 4 + z_lo), core: 2. Of those that a mesh axis runs over, the one named last changes fastest.
Arguments:
- queries: bfloat16 [512, 8192], P('blk', 'head'), may hold values from -16 to 16
- keys: bfloat16 [131072, 1024], P('blk', 'head'), may hold values from -16 to 16
- values: bfloat16 [131072, 1024], P('blk', 'head'), may hold values from -24 to 24
- cutoffs: int32 [512], P('blk'), may hold values from 2 to 131072
- out_weight: bfloat16 [8192, 8192], P('head', 'blk'), may hold values from -0.0625 to 0.0625
Outputs:
- projected: float32 [512, 8192], P('head', 'blk')
All inputs are finite; a program needn't handle non-finite values.
Results may differ from a plain program's by a relative error of at most 0.0045.
Values may be sent and summed in bfloat16 or wider, within the bound.
No kernel may reach another device: no remote copies, remote signals or barrier semaphores. Data moves between devices by JAX's collectives and lax.ppermute only.
A program may use at most 128 MiB of HBM per device.

v0:
```python
import jax
import jax.numpy as jnp
from jax import lax
from jax.sharding import PartitionSpec as P

HEAD_DIM = 128


NEG = -1e30


def passed_along(x, axis, by):
    count = lax.axis_size(axis)
    return lax.ppermute(x, axis, [(i, (i + by) % count) for i in range(count)])


def attend(q_block, cut_block, start, k_local, v_local, m_old, total, acc):
    scale = q_block.shape[-1] ** (-0.5)
    scores = (
        jnp.einsum("rhgd,khd->rhgk", q_block, k_local, preferred_element_type=jnp.float32) * scale
    )
    places = start + jnp.arange(k_local.shape[0], dtype=jnp.int32)
    seen = (places[None, :] < cut_block[:, None])[:, None, None, :]
    scores = jnp.where(seen, scores, NEG)
    m_new = jnp.maximum(m_old, jnp.max(scores, axis=-1))
    weights = jnp.where(seen, jnp.exp(scores - m_new[..., None]), 0.0)
    fade = jnp.exp(m_old - m_new)
    total = total * fade + jnp.sum(weights, axis=-1)
    rounded = weights.astype(jnp.bfloat16)
    acc = acc * fade[..., None] + jnp.einsum(
        "rhgk,khd->rhgd", rounded, v_local, preferred_element_type=jnp.float32
    )
    return (m_new, total, acc)


def shards(queries, keys, values, cutoffs, out_weight):
    rows = queries.shape[0]
    length = keys.shape[0]
    kv_local = keys.shape[1] // HEAD_DIM
    group = queries.shape[1] // (kv_local * HEAD_DIM)
    q_local = queries.reshape(rows, kv_local, group, HEAD_DIM)
    k_local = keys.reshape(length, kv_local, HEAD_DIM)
    v_local = values.reshape(length, kv_local, HEAD_DIM)
    count = lax.axis_size("blk")
    mine = lax.axis_index("blk")
    k_start = mine * length
    all_cuts = lax.all_gather(cutoffs, "blk", axis=0, tiled=True)
    m_zero = jnp.full((rows, kv_local, group), NEG, jnp.float32)
    t_zero = jnp.zeros((rows, kv_local, group), jnp.float32)
    a_zero = jnp.zeros((rows, kv_local, group, HEAD_DIM), jnp.float32)

    def travel(step, carry):
        q_block, m_old, total, acc = carry
        source = (mine - step) % count
        cut_block = lax.dynamic_slice_in_dim(all_cuts, source * rows, rows, 0)
        state = attend(q_block, cut_block, k_start, k_local, v_local, m_old, total, acc)
        q_next = passed_along(q_block, "blk", 1)
        m_next, t_next, a_next = passed_along((state[0], state[1], state[2]), "blk", 1)
        return (q_next, m_next, t_next, a_next)

    unused, m_last, total, acc = lax.fori_loop(0, count, travel, (q_local, m_zero, t_zero, a_zero))
    attended = (
        (acc / total[..., None]).astype(jnp.bfloat16).reshape(rows, kv_local * group * HEAD_DIM)
    )
    whole = lax.all_gather(attended, "blk", axis=0, tiled=True)
    return lax.psum_scatter(
        jnp.dot(whole, out_weight, preferred_element_type=jnp.float32),
        "head",
        scatter_dimension=0,
        tiled=True,
    )


def solution(mesh):
    return jax.shard_map(
        shards,
        mesh=mesh,
        in_specs=(P("blk", "head"), P("blk", "head"), P("blk", "head"), P("blk"), P("head", "blk")),
        out_specs=P("head", "blk"),
        check_vma=False,
    )
```

profile of v0, /device:TPU:1, one launch (start us, length us, event | category | flops | bytes accessed | tf_op | source)
XLA Modules:
  0.0 1330.4 jit_solution(4593572808753695120)
XLA Ops:
  9.5 20.6 %all-reduce = s32[512]{0:T(512)S(1)} all-reduce(s32[512]{0:T(512)S(1)} %dynamic-update-slice), channel_id=1, replica_groups=mesh['blk'=64,'head'=8] {'blk'}, use_global_device_ids=true, to_apply=%add | all-reduce | flops 512 | bytes 4096
  30.2 1082.2 %while.21 = (s32[]{:T(128)}, bf16[8,1,8,128]{3,2,0,1:T(8,128)(2,1)S(1)}, f32[8,1,8]{2,0,1:T(8,128)S(1)}, f32[8,1,8]{2,0,1:T(8,128)S(1)}, f32[8,1,8,128]{3,2,0,1:...) while((s32[]{:T(128)}, ...), condition=%wide.region_3.4_spmd, body=%wide.region_0.3_spmd.sunk | while | flops 68323536 | bytes 5118560 | solution.py:61
  30.2 6.9 collective-permute-start
  54.1 4.9 collective-permute-start.3
  70.4 5.2 collective-permute-start.3
  126.5 4.4 collective-permute-done.2
  160.3 4.4 collective-permute-done.2
  194.2 4.4 collective-permute-done.2
  228.0 4.4 collective-permute-done.2
  261.9 4.4 collective-permute-done.2
  295.7 4.4 collective-permute-done.2
  329.5 4.4 collective-permute-done.2
  363.4 4.4 collective-permute-done.2
  397.2 4.4 collective-permute-done.2
  431.1 4.4 collective-permute-done.2
  498.8 4.4 collective-permute-done.2
  566.5 4.4 collective-permute-done.2
  634.1 4.4 collective-permute-done.2
  668.0 4.4 collective-permute-done.2
  701.8 4.4 collective-permute-done.2
  735.7 4.4 collective-permute-done.2
  769.5 4.4 collective-permute-done.2
  803.4 4.4 collective-permute-done.2
  837.2 4.4 collective-permute-done.2
  871.0 4.4 collective-permute-done.2
  904.9 4.4 collective-permute-done.2
  938.7 4.4 collective-permute-done.2
  972.6 4.4 collective-permute-done.2
  1006.4 4.4 collective-permute-done.2
  1074.1 4.4 collective-permute-done.2
  1113.2 122.0 %all-gather.2.cloned.1.call-done = bf16[512,1024]{1,0:T(8,128)(2,1)} async-done(((bf16[8,1024]{1,0:T(8,128)(2,1)}), bf16[512,1024]{1,0:T(8,128)(2,1)}) %all-gather.2.cloned.1.call-update) | async-done | bytes 1048592 | tf_op jit(solution)/shard_map/all_gather | solution.py:65
  1237.6 86.0 %reduce-scatter.2.cloned.1.call-done = f32[64,128]{1,0:T(8,128)} async-done(((f32[512,128]{1,0:T(8,128)}), f32[64,128]{1,0:T(8,128)}) %reduce-scatter.2.cloned.1.call-update) | async-done | bytes 32784 | tf_op jit(solution)/shard_map/reduce_scatter | solution.py:66
  (1272 shorter events, 952.5 us)
Async XLA Ops:
  6.5 1228.7 %all-gather.2.cloned.1.call-start = ((), (), s32[]{:S(2)}) async-start(), calls=%async_computation.1 | async-start | bytes 1064960 | tf_op jit(solution)/shard_map/all_gather | solution.py:65
  80.2 16.9 %collective-permute-start = (bf16[8,1,8,128]{3,2,0,1:T(8,128)(2,1)S(1)}, bf16[8,1,8,128]{3,2,0,1:T(8,128)(2,1)S(1)}, u32[]{:S(2)}, u32[]{:S(2)}) collective-permute-start(bf16[8,1,8,128]{3,2,0,1:T(8,128)(2,1)S(1)} %copy.19), channel_id=1, source_target_pairs={{0,8},{8,16},{16,24},{24,32},{32,40},{40,48},{48,56},{56,64},{64,7... | collective-permute-start | bytes 49160 | tf_op jit(solution)/shard_map/while/body/eval_jaxpr/ppermute | solution.py:14
  114.0 16.9 %collective-permute-start = (bf16[8,1,8,128]{3,2,0,1:T(8,128)(2,1)S(1)}, bf16[8,1,8,128]{3,2,0,1:T(8,128)(2,1)S(1)}, u32[]{:S(2)}, u32[]{:S(2)}) collective-permute-start(bf16[8,1,8,128]{3,2,0,1:T(8,128)(2,1)S(1)} %copy.19), channel_id=1, source_target_pairs={{0,8},{8,16},{16,24},{24,32},{32,40},{40,48},{48,56},{56,64},{64,7... | collective-permute-start | bytes 49160 | tf_op jit(solution)/shard_map/while/body/eval_jaxpr/ppermute | solution.py:14
  147.8 16.9 %collective-permute-start = (bf16[8,1,8,128]{3,2,0,1:T(8,128)(2,1)S(1)}, bf16[8,1,8,128]{3,2,0,1:T(8,128)(2,1)S(1)}, u32[]{:S(2)}, u32[]{:S(2)}) collective-permute-start(bf16[8,1,8,128]{3,2,0,1:T(8,128)(2,1)S(1)} %copy.19), channel_id=1, source_target_pairs={{0,8},{8,16},{16,24},{24,32},{32,40},{40,48},{48,56},{56,64},{64,7... | collective-permute-start | bytes 49160 | tf_op jit(solution)/shard_map/while/body/eval_jaxpr/ppermute | solution.py:14
  181.7 16.9 %collective-permute-start = (bf16[8,1,8,128]{3,2,0,1:T(8,128)(2,1)S(1)}, bf16[8,1,8,128]{3,2,0,1:T(8,128)(2,1)S(1)}, u32[]{:S(2)}, u32[]{:S(2)}) collective-permute-start(bf16[8,1,8,128]{3,2,0,1:T(8,128)(2,1)S(1)} %copy.19), channel_id=1, source_target_pairs={{0,8},{8,16},{16,24},{24,32},{32,40},{40,48},{48,56},{56,64},{64,7... | collective-permute-start | bytes 49160 | tf_op jit(solution)/shard_map/while/body/eval_jaxpr/ppermute | solution.py:14
  215.5 16.9 %collective-permute-start = (bf16[8,1,8,128]{3,2,0,1:T(8,128)(2,1)S(1)}, bf16[8,1,8,128]{3,2,0,1:T(8,128)(2,1)S(1)}, u32[]{:S(2)}, u32[]{:S(2)}) collective-permute-start(bf16[8,1,8,128]{3,2,0,1:T(8,128)(2,1)S(1)} %copy.19), channel_id=1, source_target_pairs={{0,8},{8,16},{16,24},{24,32},{32,40},{40,48},{48,56},{56,64},{64,7... | collective-permute-start | bytes 49160 | tf_op jit(solution)/shard_map/while/body/eval_jaxpr/ppermute | solution.py:14
  249.4 16.9 %collective-permute-start = (bf16[8,1,8,128]{3,2,0,1:T(8,128)(2,1)S(1)}, bf16[8,1,8,128]{3,2,0,1:T(8,128)(2,1)S(1)}, u32[]{:S(2)}, u32[]{:S(2)}) collective-permute-start(bf16[8,1,8,128]{3,2,0,1:T(8,128)(2,1)S(1)} %copy.19), channel_id=1, source_target_pairs={{0,8},{8,16},{16,24},{24,32},{32,40},{40,48},{48,56},{56,64},{64,7... | collective-permute-start | bytes 49160 | tf_op jit(solution)/shard_map/while/body/eval_jaxpr/ppermute | solution.py:14
  283.2 16.9 %collective-permute-start = (bf16[8,1,8,128]{3,2,0,1:T(8,128)(2,1)S(1)}, bf16[8,1,8,128]{3,2,0,1:T(8,128)(2,1)S(1)}, u32[]{:S(2)}, u32[]{:S(2)}) collective-permute-start(bf16[8,1,8,128]{3,2,0,1:T(8,128)(2,1)S(1)} %copy.19), channel_id=1, source_target_pairs={{0,8},{8,16},{16,24},{24,32},{32,40},{40,48},{48,56},{56,64},{64,7... | collective-permute-start | bytes 49160 | tf_op jit(solution)/shard_map/while/body/eval_jaxpr/ppermute | solution.py:14
  317.1 16.9 %collective-permute-start = (bf16[8,1,8,128]{3,2,0,1:T(8,128)(2,1)S(1)}, bf16[8,1,8,128]{3,2,0,1:T(8,128)(2,1)S(1)}, u32[]{:S(2)}, u32[]{:S(2)}) collective-permute-start(bf16[8,1,8,128]{3,2,0,1:T(8,128)(2,1)S(1)} %copy.19), channel_id=1, source_target_pairs={{0,8},{8,16},{16,24},{24,32},{32,40},{40,48},{48,56},{56,64},{64,7... | collective-permute-start | bytes 49160 | tf_op jit(solution)/shard_map/while/body/eval_jaxpr/ppermute | solution.py:14
  350.9 16.9 %collective-permute-start = (bf16[8,1,8,128]{3,2,0,1:T(8,128)(2,1)S(1)}, bf16[8,1,8,128]{3,2,0,1:T(8,128)(2,1)S(1)}, u32[]{:S(2)}, u32[]{:S(2)}) collective-permute-start(bf16[8,1,8,128]{3,2,0,1:T(8,128)(2,1)S(1)} %copy.19), channel_id=1, source_target_pairs={{0,8},{8,16},{16,24},{24,32},{32,40},{40,48},{48,56},{56,64},{64,7... | collective-permute-start | bytes 49160 | tf_op jit(solution)/shard_map/while/body/eval_jaxpr/ppermute | solution.py:14
  384.8 16.9 %collective-permute-start = (bf16[8,1,8,128]{3,2,0,1:T(8,128)(2,1)S(1)}, bf16[8,1,8,128]{3,2,0,1:T(8,128)(2,1)S(1)}, u32[]{:S(2)}, u32[]{:S(2)}) collective-permute-start(bf16[8,1,8,128]{3,2,0,1:T(8,128)(2,1)S(1)} %copy.19), channel_id=1, source_target_pairs={{0,8},{8,16},{16,24},{24,32},{32,40},{40,48},{48,56},{56,64},{64,7... | collective-permute-start | bytes 49160 | tf_op jit(solution)/shard_map/while/body/eval_jaxpr/ppermute | solution.py:14
  418.6 16.9 %collective-permute-start = (bf16[8,1,8,128]{3,2,0,1:T(8,128)(2,1)S(1)}, bf16[8,1,8,128]{3,2,0,1:T(8,128)(2,1)S(1)}, u32[]{:S(2)}, u32[]{:S(2)}) collective-permute-start(bf16[8,1,8,128]{3,2,0,1:T(8,128)(2,1)S(1)} %copy.19), channel_id=1, source_target_pairs={{0,8},{8,16},{16,24},{24,32},{32,40},{40,48},{48,56},{56,64},{64,7... | collective-permute-start | bytes 49160 | tf_op jit(solution)/shard_map/while/body/eval_jaxpr/ppermute | solution.py:14
  452.4 16.9 %collective-permute-start = (bf16[8,1,8,128]{3,2,0,1:T(8,128)(2,1)S(1)}, bf16[8,1,8,128]{3,2,0,1:T(8,128)(2,1)S(1)}, u32[]{:S(2)}, u32[]{:S(2)}) collective-permute-start(bf16[8,1,8,128]{3,2,0,1:T(8,128)(2,1)S(1)} %copy.19), channel_id=1, source_target_pairs={{0,8},{8,16},{16,24},{24,32},{32,40},{40,48},{48,56},{56,64},{64,7... | collective-permute-start | bytes 49160 | tf_op jit(solution)/shard_map/while/body/eval_jaxpr/ppermute | solution.py:14
  486.3 16.9 %collective-permute-start = (bf16[8,1,8,128]{3,2,0,1:T(8,128)(2,1)S(1)}, bf16[8,1,8,128]{3,2,0,1:T(8,128)(2,1)S(1)}, u32[]{:S(2)}, u32[]{:S(2)}) collective-permute-start(bf16[8,1,8,128]{3,2,0,1:T(8,128)(2,1)S(1)} %copy.19), channel_id=1, source_target_pairs={{0,8},{8,16},{16,24},{24,32},{32,40},{40,48},{48,56},{56,64},{64,7... | collective-permute-start | bytes 49160 | tf_op jit(solution)/shard_map/while/body/eval_jaxpr/ppermute | solution.py:14
  520.1 16.9 %collective-permute-start = (bf16[8,1,8,128]{3,2,0,1:T(8,128)(2,1)S(1)}, bf16[8,1,8,128]{3,2,0,1:T(8,128)(2,1)S(1)}, u32[]{:S(2)}, u32[]{:S(2)}) collective-permute-start(bf16[8,1,8,128]{3,2,0,1:T(8,128)(2,1)S(1)} %copy.19), channel_id=1, source_target_pairs={{0,8},{8,16},{16,24},{24,32},{32,40},{40,48},{48,56},{56,64},{64,7... | collective-permute-start | bytes 49160 | tf_op jit(solution)/shard_map/while/body/eval_jaxpr/ppermute | solution.py:14
  554.0 16.9 %collective-permute-start = (bf16[8,1,8,128]{3,2,0,1:T(8,128)(2,1)S(1)}, bf16[8,1,8,128]{3,2,0,1:T(8,128)(2,1)S(1)}, u32[]{:S(2)}, u32[]{:S(2)}) collective-permute-start(bf16[8,1,8,128]{3,2,0,1:T(8,128)(2,1)S(1)} %copy.19), channel_id=1, source_target_pairs={{0,8},{8,16},{16,24},{24,32},{32,40},{40,48},{48,56},{56,64},{64,7... | collective-permute-start | bytes 49160 | tf_op jit(solution)/shard_map/while/body/eval_jaxpr/ppermute | solution.py:14
  587.8 16.9 %collective-permute-start = (bf16[8,1,8,128]{3,2,0,1:T(8,128)(2,1)S(1)}, bf16[8,1,8,128]{3,2,0,1:T(8,128)(2,1)S(1)}, u32[]{:S(2)}, u32[]{:S(2)}) collective-permute-start(bf16[8,1,8,128]{3,2,0,1:T(8,128)(2,1)S(1)} %copy.19), channel_id=1, source_target_pairs={{0,8},{8,16},{16,24},{24,32},{32,40},{40,48},{48,56},{56,64},{64,7... | collective-permute-start | bytes 49160 | tf_op jit(solution)/shard_map/while/body/eval_jaxpr/ppermute | solution.py:14
  621.7 16.9 %collective-permute-start = (bf16[8,1,8,128]{3,2,0,1:T(8,128)(2,1)S(1)}, bf16[8,1,8,128]{3,2,0,1:T(8,128)(2,1)S(1)}, u32[]{:S(2)}, u32[]{:S(2)}) collective-permute-start(bf16[8,1,8,128]{3,2,0,1:T(8,128)(2,1)S(1)} %copy.19), channel_id=1, source_target_pairs={{0,8},{8,16},{16,24},{24,32},{32,40},{40,48},{48,56},{56,64},{64,7... | collective-permute-start | bytes 49160 | tf_op jit(solution)/shard_map/while/body/eval_jaxpr/ppermute | solution.py:14
  655.5 16.9 %collective-permute-start = (bf16[8,1,8,128]{3,2,0,1:T(8,128)(2,1)S(1)}, bf16[8,1,8,128]{3,2,0,1:T(8,128)(2,1)S(1)}, u32[]{:S(2)}, u32[]{:S(2)}) collective-permute-start(bf16[8,1,8,128]{3,2,0,1:T(8,128)(2,1)S(1)} %copy.19), channel_id=1, source_target_pairs={{0,8},{8,16},{16,24},{24,32},{32,40},{40,48},{48,56},{56,64},{64,7... | collective-permute-start | bytes 49160 | tf_op jit(solution)/shard_map/while/body/eval_jaxpr/ppermute | solution.py:14
  689.4 16.9 %collective-permute-start = (bf16[8,1,8,128]{3,2,0,1:T(8,128)(2,1)S(1)}, bf16[8,1,8,128]{3,2,0,1:T(8,128)(2,1)S(1)}, u32[]{:S(2)}, u32[]{:S(2)}) collective-permute-start(bf16[8,1,8,128]{3,2,0,1:T(8,128)(2,1)S(1)} %copy.19), channel_id=1, source_target_pairs={{0,8},{8,16},{16,24},{24,32},{32,40},{40,48},{48,56},{56,64},{64,7... | collective-permute-start | bytes 49160 | tf_op jit(solution)/shard_map/while/body/eval_jaxpr/ppermute | solution.py:14
  723.2 16.9 %collective-permute-start = (bf16[8,1,8,128]{3,2,0,1:T(8,128)(2,1)S(1)}, bf16[8,1,8,128]{3,2,0,1:T(8,128)(2,1)S(1)}, u32[]{:S(2)}, u32[]{:S(2)}) collective-permute-start(bf16[8,1,8,128]{3,2,0,1:T(8,128)(2,1)S(1)} %copy.19), channel_id=1, source_target_pairs={{0,8},{8,16},{16,24},{24,32},{32,40},{40,48},{48,56},{56,64},{64,7... | collective-permute-start | bytes 49160 | tf_op jit(solution)/shard_map/while/body/eval_jaxpr/ppermute | solution.py:14
  757.0 16.9 %collective-permute-start = (bf16[8,1,8,128]{3,2,0,1:T(8,128)(2,1)S(1)}, bf16[8,1,8,128]{3,2,0,1:T(8,128)(2,1)S(1)}, u32[]{:S(2)}, u32[]{:S(2)}) collective-permute-start(bf16[8,1,8,128]{3,2,0,1:T(8,128)(2,1)S(1)} %copy.19), channel_id=1, source_target_pairs={{0,8},{8,16},{16,24},{24,32},{32,40},{40,48},{48,56},{56,64},{64,7... | collective-permute-start | bytes 49160 | tf_op jit(solution)/shard_map/while/body/eval_jaxpr/ppermute | solution.py:14
  790.9 16.9 %collective-permute-start = (bf16[8,1,8,128]{3,2,0,1:T(8,128)(2,1)S(1)}, bf16[8,1,8,128]{3,2,0,1:T(8,128)(2,1)S(1)}, u32[]{:S(2)}, u32[]{:S(2)}) collective-permute-start(bf16[8,1,8,128]{3,2,0,1:T(8,128)(2,1)S(1)} %copy.19), channel_id=1, source_target_pairs={{0,8},{8,16},{16,24},{24,32},{32,40},{40,48},{48,56},{56,64},{64,7... | collective-permute-start | bytes 49160 | tf_op jit(solution)/shard_map/while/body/eval_jaxpr/ppermute | solution.py:14
  824.7 16.9 %collective-permute-start = (bf16[8,1,8,128]{3,2,0,1:T(8,128)(2,1)S(1)}, bf16[8,1,8,128]{3,2,0,1:T(8,128)(2,1)S(1)}, u32[]{:S(2)}, u32[]{:S(2)}) collective-permute-start(bf16[8,1,8,128]{3,2,0,1:T(8,128)(2,1)S(1)} %copy.19), channel_id=1, source_target_pairs={{0,8},{8,16},{16,24},{24,32},{32,40},{40,48},{48,56},{56,64},{64,7... | collective-permute-start | bytes 49160 | tf_op jit(solution)/shard_map/while/body/eval_jaxpr/ppermute | solution.py:14
  858.6 16.9 %collective-permute-start = (bf16[8,1,8,128]{3,2,0,1:T(8,128)(2,1)S(1)}, bf16[8,1,8,128]{3,2,0,1:T(8,128)(2,1)S(1)}, u32[]{:S(2)}, u32[]{:S(2)}) collective-permute-start(bf16[8,1,8,128]{3,2,0,1:T(8,128)(2,1)S(1)} %copy.19), channel_id=1, source_target_pairs={{0,8},{8,16},{16,24},{24,32},{32,40},{40,48},{48,56},{56,64},{64,7... | collective-permute-start | bytes 49160 | tf_op jit(solution)/shard_map/while/body/eval_jaxpr/ppermute | solution.py:14
  892.4 16.9 %collective-permute-start = (bf16[8,1,8,128]{3,2,0,1:T(8,128)(2,1)S(1)}, bf16[8,1,8,128]{3,2,0,1:T(8,128)(2,1)S(1)}, u32[]{:S(2)}, u32[]{:S(2)}) collective-permute-start(bf16[8,1,8,128]{3,2,0,1:T(8,128)(2,1)S(1)} %copy.19), channel_id=1, source_target_pairs={{0,8},{8,16},{16,24},{24,32},{32,40},{40,48},{48,56},{56,64},{64,7... | collective-permute-start | bytes 49160 | tf_op jit(solution)/shard_map/while/body/eval_jaxpr/ppermute | solution.py:14
  926.3 16.9 %collective-permute-start = (bf16[8,1,8,128]{3,2,0,1:T(8,128)(2,1)S(1)}, bf16[8,1,8,128]{3,2,0,1:T(8,128)(2,1)S(1)}, u32[]{:S(2)}, u32[]{:S(2)}) collective-permute-start(bf16[8,1,8,128]{3,2,0,1:T(8,128)(2,1)S(1)} %copy.19), channel_id=1, source_target_pairs={{0,8},{8,16},{16,24},{24,32},{32,40},{40,48},{48,56},{56,64},{64,7... | collective-permute-start | bytes 49160 | tf_op jit(solution)/shard_map/while/body/eval_jaxpr/ppermute | solution.py:14
  960.1 16.9 %collective-permute-start = (bf16[8,1,8,128]{3,2,0,1:T(8,128)(2,1)S(1)}, bf16[8,1,8,128]{3,2,0,1:T(8,128)(2,1)S(1)}, u32[]{:S(2)}, u32[]{:S(2)}) collective-permute-start(bf16[8,1,8,128]{3,2,0,1:T(8,128)(2,1)S(1)} %copy.19), channel_id=1, source_target_pairs={{0,8},{8,16},{16,24},{24,32},{32,40},{40,48},{48,56},{56,64},{64,7... | collective-permute-start | bytes 49160 | tf_op jit(solution)/shard_map/while/body/eval_jaxpr/ppermute | solution.py:14
  994.0 16.9 %collective-permute-start = (bf16[8,1,8,128]{3,2,0,1:T(8,128)(2,1)S(1)}, bf16[8,1,8,128]{3,2,0,1:T(8,128)(2,1)S(1)}, u32[]{:S(2)}, u32[]{:S(2)}) collective-permute-start(bf16[8,1,8,128]{3,2,0,1:T(8,128)(2,1)S(1)} %copy.19), channel_id=1, source_target_pairs={{0,8},{8,16},{16,24},{24,32},{32,40},{40,48},{48,56},{56,64},{64,7... | collective-permute-start | bytes 49160 | tf_op jit(solution)/shard_map/while/body/eval_jaxpr/ppermute | solution.py:14
  1027.8 16.9 %collective-permute-start = (bf16[8,1,8,128]{3,2,0,1:T(8,128)(2,1)S(1)}, bf16[8,1,8,128]{3,2,0,1:T(8,128)(2,1)S(1)}, u32[]{:S(2)}, u32[]{:S(2)}) collective-permute-start(bf16[8,1,8,128]{3,2,0,1:T(8,128)(2,1)S(1)} %copy.19), channel_id=1, source_target_pairs={{0,8},{8,16},{16,24},{24,32},{32,40},{40,48},{48,56},{56,64},{64,7... | collective-permute-start | bytes 49160 | tf_op jit(solution)/shard_map/while/body/eval_jaxpr/ppermute | solution.py:14
  1061.6 16.9 %collective-permute-start = (bf16[8,1,8,128]{3,2,0,1:T(8,128)(2,1)S(1)}, bf16[8,1,8,128]{3,2,0,1:T(8,128)(2,1)S(1)}, u32[]{:S(2)}, u32[]{:S(2)}) collective-permute-start(bf16[8,1,8,128]{3,2,0,1:T(8,128)(2,1)S(1)} %copy.19), channel_id=1, source_target_pairs={{0,8},{8,16},{16,24},{24,32},{32,40},{40,48},{48,56},{56,64},{64,7... | collective-permute-start | bytes 49160 | tf_op jit(solution)/shard_map/while/body/eval_jaxpr/ppermute | solution.py:14
  1113.1 210.5 %reduce-scatter.2.cloned.1.call-start = ((), (), s32[]{:S(2)}) async-start(), calls=%async_computation.2 | async-start | bytes 294912 | tf_op jit(solution)/shard_map/reduce_scatter | solution.py:66
  (293 other events, 3851.9 us)
Sparse Core Ops, SparseCore 0:
  1113.2 121.9 all-gather.1
  1239.7 83.8 reduce-scatter.1
where the time goes:
time: 1340 us; the launch traced here: 1330 us
  waiting for transfers between devices  627 us (47%)
  starting transfers between devices  514 us (38%)
  matrix products  116 us (9%)
  other arithmetic  23.7 us (2%)
  blocking collectives  20.6 us (2%)
  between operations  14.2 us (1%)
    ppermute x256, starting transfers between devices, passed_along(): return lax.ppermute(x, axis, [(i, (i + by) % count) for i in range(count)])  514 us
    ppermute x256, waiting for transfers between devices, passed_along(): return lax.ppermute(x, axis, [(i, (i + by) % count) for i in range(count)])  419 us
    all_gather x1, waiting for transfers between devices, shards(): whole = lax.all_gather(attended, 'blk', axis=0, tiled=True)  122 us
    dot_general x64, matrix products, attend(): jnp.einsum('rhgd,khd->rhgk', q_block, k_local, preferred_element_type=jnp...  94.4 us
    reduce_scatter x1, waiting for transfers between devices, shards(): lax.psum_scatter(jnp.dot(whole, out_weight, preferred_element_type=jnp.fl...  86 us
  transfers between devices with their start and end apart: 258, of which 125 were waited for; matrix products, arithmetic and copies ran while one was open for 11% of the time, Pallas kernels for 0%

commit v1 on v0

v1 whole, which is shorter than its diff:
```python
import functools
import math

import jax
import jax.numpy as jnp
from jax import lax
from jax.experimental import pallas as pl
from jax.experimental.pallas import tpu as pltpu
from jax.sharding import Mesh
from jax.sharding import PartitionSpec as P

HEAD_DIM = 128
GROUP = 8
LANES = 128
WIDTH = GROUP * HEAD_DIM
PACKED = WIDTH + LANES
NEG = -1e30
FLOOR = -1e20
SCALE = math.log2(math.e) / math.sqrt(HEAD_DIM)
ROW_BLOCK = 32
KEY_CHUNK = 2048
VMEM = 32 * 2**20

AXES = ("y", "z", "c", "w", "x")
SIZES = (8, 4, 2, 2, 4)
BLK = ("y", "z", "c")
HEAD = ("w", "x")
CHIPS = ("y", "z")
SWAP = ((0, 1), (1, 0))


def attend_kernel(q_ref, k_mine, v_mine, k_other, v_other, o_ref):
    length = k_mine.shape[0]
    rows = q_ref.shape[0]
    many = GROUP * rows
    me = lax.axis_index("y") * 4 + lax.axis_index("z")
    core = lax.axis_index("c")
    start_mine = (me * 2 + core) * length
    start_other = (me * 2 + 1 - core) * length
    packed = q_ref[...]
    queries = jnp.concatenate(
        [packed[:, h * HEAD_DIM : (h + 1) * HEAD_DIM] for h in range(GROUP)], axis=0
    )
    digits = packed[:, WIDTH:].astype(jnp.float32)
    cut = (digits[:, 0:1] + 64.0 * digits[:, 1:2] + 4096.0 * digits[:, 2:3]).astype(jnp.int32)
    cut = jnp.concatenate([cut] * GROUP, axis=0)
    places = lax.broadcasted_iota(jnp.int32, (many, KEY_CHUNK), 1)
    ones = jnp.ones((KEY_CHUNK, LANES), jnp.bfloat16)
    chunks = [
        (keys, values, start + at, at)
        for keys, values, start in (
            (k_mine, v_mine, start_mine),
            (k_other, v_other, start_other),
        )
        for at in range(0, length, KEY_CHUNK)
    ]

    def scores_of(chunk):
        keys, _, start, at = chunk
        scores = lax.dot_general(
            queries,
            keys[at : at + KEY_CHUNK, :],
            (((1,), (1,)), ((), ())),
            preferred_element_type=jnp.float32,
        )
        return jnp.where(places < cut - start, scores, NEG)

    m_old = jnp.full((many, 1), FLOOR, jnp.float32)
    acc = jnp.zeros((many, HEAD_DIM + LANES), jnp.float32)
    scores = scores_of(chunks[0])
    for n, (_, values, _, at) in enumerate(chunks):
        later = scores_of(chunks[n + 1]) if n + 1 < len(chunks) else None
        m_new = jnp.maximum(m_old, jnp.max(scores, axis=1, keepdims=True))
        fade = jnp.exp2((m_old - m_new) * SCALE)
        weights = jnp.exp2(scores * SCALE - m_new * SCALE).astype(jnp.bfloat16)
        wide = jnp.concatenate([values[at : at + KEY_CHUNK, :], ones], axis=1)
        acc = acc * fade + jnp.dot(weights, wide, preferred_element_type=jnp.float32)
        m_old, scores = m_new, later
    total = acc[:, HEAD_DIM : HEAD_DIM + 1]
    some = jnp.maximum(total, 1e-30)
    mixed = (acc[:, :HEAD_DIM] / some).astype(jnp.bfloat16)
    level = jnp.where(total > 0.0, m_old * SCALE + jnp.log2(some), NEG)
    high = level.astype(jnp.bfloat16).astype(jnp.float32)
    middle = (level - high).astype(jnp.bfloat16).astype(jnp.float32)
    low = (level - high) - middle
    lane = lax.broadcasted_iota(jnp.int32, (rows, LANES), 1)
    stats = jnp.zeros((rows, LANES), jnp.float32)
    for h in range(GROUP):
        mine = slice(h * rows, (h + 1) * rows)
        o_ref[:, h * HEAD_DIM : (h + 1) * HEAD_DIM] = mixed[mine]
        for i, part in enumerate((high, middle, low)):
            stats = jnp.where(lane == 3 * h + i, part[mine], stats)
    o_ref[:, WIDTH:] = stats.astype(jnp.bfloat16)


def attend(packed, k_mine, v_mine, k_other, v_other):
    rows = packed.shape[0]
    whole = pl.BlockSpec(k_mine.shape, lambda i: (0, 0))
    block = pl.BlockSpec((ROW_BLOCK, PACKED), lambda i: (i, 0))
    return pl.pallas_call(
        attend_kernel,
        grid=(rows // ROW_BLOCK,),
        in_specs=[block, whole, whole, whole, whole],
        out_specs=block,
        out_shape=jax.ShapeDtypeStruct((rows, PACKED), jnp.bfloat16),
        compiler_params=pltpu.CompilerParams(vmem_limit_bytes=VMEM),
        name="attend",
    )(packed, k_mine, v_mine, k_other, v_other)


def repeated(o_ref, at, block):
    twice = jnp.concatenate([block, block], axis=0)
    for top in range(0, o_ref.shape[0], twice.shape[0]):
        o_ref[top : top + twice.shape[0], at : at + block.shape[1]] = twice


def pack_kernel(q_ref, cut_ref, o_ref):
    rows = q_ref.shape[0]
    lane = lax.broadcasted_iota(jnp.int32, (rows, LANES), 1)
    row = lax.broadcasted_iota(jnp.int32, (rows, LANES), 0)
    cut = jnp.zeros((rows, LANES), jnp.int32)
    for r in range(rows):
        cut = jnp.where(row == r, cut_ref[r], cut)
    digits = jnp.where(lane == 0, cut & 63, jnp.where(lane == 1, (cut >> 6) & 63, cut >> 12))
    digits = digits.astype(jnp.float32).astype(jnp.bfloat16)
    repeated(o_ref, 0, q_ref[...])
    repeated(o_ref, WIDTH, digits)


def pack(queries, cutoffs, receivers):
    rows = queries.shape[0]
    return pl.pallas_call(
        pack_kernel,
        in_specs=[
            pl.BlockSpec(memory_space=pltpu.VMEM),
            pl.BlockSpec(memory_space=pltpu.SMEM),
        ],
        out_shape=jax.ShapeDtypeStruct((receivers * rows, PACKED), jnp.bfloat16),
        name="pack",
    )(queries, cutoffs)


def combine_kernel(p_ref, o_ref):
    rows = 8
    sources = p_ref.shape[0] // rows
    levels = []
    for n in range(sources // 2):
        stats = p_ref[2 * n * rows : 2 * (n + 1) * rows, WIDTH:].astype(jnp.float32)
        level = stats + jnp.roll(stats, -1, axis=1) + jnp.roll(stats, -2, axis=1)
        levels += [level[:rows], level[rows:]]
    top = functools.reduce(jnp.maximum, levels)
    shares = [jnp.exp2(level - top) for level in levels]
    total = 1.0 / functools.reduce(jnp.add, shares)
    shares = [share * total for share in shares]
    sums = [jnp.zeros((rows, HEAD_DIM), jnp.float32) for _ in range(GROUP)]
    for n in range(sources // 2):
        for h in range(GROUP):
            part = p_ref[2 * n * rows : 2 * (n + 1) * rows, h * HEAD_DIM : (h + 1) * HEAD_DIM]
            part = part.astype(jnp.float32)
            sums[h] = sums[h] + part[:rows] * shares[2 * n][:, 3 * h : 3 * h + 1]
            sums[h] = sums[h] + part[rows:] * shares[2 * n + 1][:, 3 * h : 3 * h + 1]
    for h in range(GROUP):
        repeated(o_ref, h * HEAD_DIM, sums[h].astype(jnp.bfloat16))


def combine(parts):
    return pl.pallas_call(
        combine_kernel,
        out_shape=jax.ShapeDtypeStruct((parts.shape[0], WIDTH), jnp.bfloat16),
        name="combine",
    )(parts)


def project_kernel(a_ref, w_mine, w_other, o_ref):
    rows = a_ref.shape[0]
    core = lax.axis_index("c")
    attended = a_ref[...]
    for place, weight in ((core, w_mine), (1 - core, w_other)):
        at = pl.multiple_of(place * rows, rows)
        o_ref[pl.ds(at, rows), :] = jnp.dot(
            attended, weight[...], preferred_element_type=jnp.float32
        )


def project(attended, w_mine, w_other):
    rows = attended.shape[0]
    return pl.pallas_call(
        project_kernel,
        out_shape=jax.ShapeDtypeStruct((2 * rows, w_mine.shape[1]), jnp.float32),
        name="project",
    )(attended, w_mine, w_other)


def exchange(x, axis):
    return lax.all_to_all(x, axis, 0, 0, tiled=True)


def shards(queries, keys, values, cutoffs, out_weight):
    rows = queries.shape[0]
    chips = SIZES[0] * SIZES[1]
    k_other = lax.ppermute(keys, "c", SWAP)
    v_other = lax.ppermute(values, "c", SWAP)
    w_other = lax.ppermute(out_weight, "c", SWAP)
    packed = exchange(pack(queries, cutoffs, chips), CHIPS)
    parts = exchange(attend(packed, keys, values, k_other, v_other), CHIPS)
    attended = exchange(combine(parts), CHIPS)
    sums = exchange(project(attended, out_weight, w_other), ("c",) + HEAD)
    heads = SIZES[3] * SIZES[4]
    sums = sums.reshape(2, heads, SIZES[1], rows, LANES).sum(axis=1)
    return sums.transpose(1, 0, 2, 3).reshape(2 * SIZES[1] * rows, LANES)


def solution(mesh):
    fine = Mesh(mesh.devices.reshape(SIZES), AXES)
    return jax.shard_map(
        shards,
        mesh=fine,
        in_specs=(P(BLK, HEAD), P(BLK, HEAD), P(BLK, HEAD), P(BLK), P(HEAD, BLK)),
        out_specs=P(HEAD, BLK),
        check_vma=False,
    )
```

time: 1340 us -> 124 us (0.09)
  waiting for transfers between devices: 627 us -> 27.5 us
  starting transfers between devices: 514 us -> 26.7 us
  matrix products: 116 us -> 0 us
  blocking collectives: 20.6 us -> 47.8 us
  other arithmetic: 23.7 us -> 0.02 us
  Pallas kernels: 0 us -> 19.7 us
  between operations: 14.2 us -> 0.09 us
    ppermute x256 -> x3, starting transfers between devices: 514 us -> 7.51 us  [the longest x1 2.86 us: shards(): k_other = lax.ppermute(keys, 'c', SWAP)]
    ppermute x256 -> x3, waiting for transfers between devices: 419 us -> 3.01 us  [the longest x1 1.87 us: shards(): v_other = lax.ppermute(values, 'c', SWAP)]
    all_gather x1 -> x0, waiting for transfers between devices: 122 us -> none  [shards(): whole = lax.all_gather(attended, 'blk', axis=0, tiled=True)]
    dot_general x129 -> x0, matrix products: 116 us -> none  [the longest x64 94.4 us: attend(): jnp.einsum('rhgd,khd->rhgk', q_block, k_local, preferred_element_type=jnp...]
    reduce_scatter x1 -> x0, waiting for transfers between devices: 86 us -> none  [shards(): lax.psum_scatter(jnp.dot(whole, out_weight, preferred_element_type=jnp.fl...]
    all_to_all x0 -> x2, blocking collectives: none -> 47.8 us  [exchange(): return lax.all_to_all(x, axis, 0, 0, tiled=True)]
    all_to_all x0 -> x2, waiting for transfers between devices: none -> 24.5 us  [exchange(): return lax.all_to_all(x, axis, 0, 0, tiled=True)]
    unnamed x1 -> x0, blocking collectives: 20.6 us -> none
  transfers between devices with their start and end apart: 258 -> 5, of which waited for: 125 -> 4; matrix products, arithmetic and copies ran while one was open for 11% -> 0% of each run, Pallas kernels for 0% -> 0%
where the time goes in v1:
time: 124 us; the launch traced here: 123 us
  blocking collectives  47.8 us (39%)
  waiting for transfers between devices  27.5 us (22%)
  starting transfers between devices  26.7 us (22%)
  Pallas kernels  19.7 us (16%)
  local copies, waits for them, and re-layouts  1.43 us (1%)
    all_to_all x2, blocking collectives, exchange(): return lax.all_to_all(x, axis, 0, 0, tiled=True)  47.8 us
    all_to_all x2, waiting for transfers between devices, exchange(): return lax.all_to_all(x, axis, 0, 0, tiled=True)  24.5 us
    all_to_all x2, starting transfers between devices, exchange(): return lax.all_to_all(x, axis, 0, 0, tiled=True)  19.2 us
    pallas_call x1, Pallas kernels, attend(): pl.pallas_call(attend_kernel, grid=(rows // ROW_BLOCK,), in_specs=[block,...  13.1 us
    ppermute x1, starting transfers between devices, shards(): k_other = lax.ppermute(keys, 'c', SWAP)  2.86 us
    ppermute x1, starting transfers between devices, shards(): w_other = lax.ppermute(out_weight, 'c', SWAP)  2.72 us
    pallas_call x1, Pallas kernels, combine(): pl.pallas_call(combine_kernel, out_shape=jax.ShapeDtypeStruct((parts.shap...  2.6 us
  transfers between devices with their start and end apart: 5, of which 4 were waited for; matrix products, arithmetic and copies ran while one was open for 0% of the time, Pallas kernels for 0%

profile of v1, /device:TPU:1, one launch (start us, length us, event | category | flops | bytes accessed | tf_op | source)
XLA Modules:
  0.0 123.2 jit_solution(363122472806737773)
XLA Ops:
  0.0 1.7 %pack.1 = bf16[256,1152]{1,0:T(8,128)(2,1)} custom-call(bf16[8,1024]{1,0:T(8,128)(2,1)} %q_ref.1, s32[8]{0:T(128)} %cut_ref.1), custom_call_target="tpu_custom_call" | custom-call | tf_op jit(solution)/shard_map/pack/pallas_call | solution.py:132
  1.7 0.0 copy-start
  1.7 0.0 copy-start.1
  1.7 13.6 %all-to-all-start = ((bf16[32,8,1152]{2,1,0:T(8,128)(2,1)}), bf16[32,8,1152]{2,1,0:T(8,128)(2,1)S(1)}, u32[]{:S(2)}, u32[]{:S(2)}) async-start(bf16[32,8,1152]{2,1,0:T(8,128)(2,1)} %bitcast.12), calls=%async_computation | async-start | bytes 1179648 | tf_op jit(solution)/shard_map/all_to_all | solution.py:195
  15.3 0.0 copy-done
  15.3 2.9 %collective-permute-start = (bf16[2048,128]{1,0:T(8,128)(2,1)S(1)}, bf16[2048,128]{1,0:T(8,128)(2,1)S(1)}, u32[]{:S(2)}, u32[]{:S(2)}) collective-permute-start(bf16[2048,128]{1,0:T(8,128)(2,1)S(1)} %copy-done), channel_id=1, source_target_pairs={{0,8},{8,0},{1,9},{9,1},{2,10},{10,2},{3,11},{11,3},{4,12},{12,4},... | collective-permute-start | bytes 1572872 | tf_op jit(solution)/shard_map/ppermute | solution.py:201
  18.1 0.0 copy-done.1
  18.2 1.9 %collective-permute-start.1 = (bf16[2048,128]{1,0:T(8,128)(2,1)S(1)}, bf16[2048,128]{1,0:T(8,128)(2,1)S(1)}, u32[]{:S(2)}, u32[]{:S(2)}) collective-permute-start(bf16[2048,128]{1,0:T(8,128)(2,1)S(1)} %copy-done.1), channel_id=1, source_target_pairs={{0,8},{8,0},{1,9},{9,1},{2,10},{10,2},{3,11},{11,3},{4,12},{12,4},... | collective-permute-start | bytes 1572872 | tf_op jit(solution)/shard_map/ppermute | solution.py:202
  20.1 0.0 collective-permute-done.k_other
  20.1 1.9 %collective-permute-done.1.v_other = bf16[2048,128]{1,0:T(8,128)(2,1)S(1)} collective-permute-done((bf16[2048,128]{1,0:T(8,128)(2,1)S(1)}, bf16[2048,128]{1,0:T(8,128)(2,1)S(1)}, u32[]{:S(2)}, u32[]{:S(2)}) %collective-permute-start.1) | collective-permute-done | bytes 524320 | tf_op jit(solution)/shard_map/ppermute | solution.py:202
  22.0 11.4 %all-to-all-done = bf16[32,8,1152]{2,1,0:T(8,128)(2,1)S(1)} async-done(((bf16[32,8,1152]{2,1,0:T(8,128)(2,1)}), bf16[32,8,1152]{2,1,0:T(8,128)(2,1)S(1)}, u32[]{:S(2)}, u32[]{:S(2)}) %all-to-all-start) | async-done | bytes 589856 | tf_op jit(solution)/shard_map/all_to_all | solution.py:195
  33.3 13.1 %attend.1 = bf16[256,1152]{1,0:T(8,128)(2,1)S(1)} custom-call(bf16[256,1152]{1,0:T(8,128)(2,1)S(1)} %bitcast.10, bf16[2048,128]{1,0:T(8,128)(2,1)S(1)} %copy-done, bf16[2048,128]{1,0:T(8,128)(2,1)S(1)} %copy-done.1, bf16[2048,128]{1,0:T(8,128)(2,1)S(1)} %collective-permute-done.k_other, bf16[2048,128]{1,0:T(8,128)(2,1)S(1)} %collective-permute-done.1.v_other), custom_call_target="tpu_custom_call" | custom-call | tf_op jit(solution)/shard_map/attend/pallas_call | solution.py:100
  46.5 23.7 %all_to_all.42 = bf16[32,8,1152]{2,1,0:T(8,128)(2,1)} all-to-all(bf16[32,8,1152]{2,1,0:T(8,128)(2,1)S(1)} %bitcast.11), channel_id=1, replica_groups=mesh['y'=8,'z'=4,'c'=2,'w'=2,'x'=4] {'y','z'}, dimensions={0} | all-to-all | bytes 1179648 | tf_op jit(solution)/shard_map/all_to_all | solution.py:195
  70.1 2.6 %combine.1 = bf16[256,1024]{1,0:T(8,128)(2,1)} custom-call(bf16[256,1152]{1,0:T(8,128)(2,1)} %bitcast.13), custom_call_target="tpu_custom_call" | custom-call | tf_op jit(solution)/shard_map/combine/pallas_call | solution.py:167
  72.7 0.0 copy-start.3
  72.7 5.6 %all-to-all-start.2 = ((bf16[32,8,1024]{2,1,0:T(8,128)(2,1)}), bf16[32,8,1024]{2,1,0:T(8,128)(2,1)S(1)}, u32[]{:S(2)}, u32[]{:S(2)}) async-start(bf16[32,8,1024]{2,1,0:T(8,128)(2,1)} %bitcast.15), calls=%async_computation.2 | async-start | bytes 1048576 | tf_op jit(solution)/shard_map/all_to_all | solution.py:195
  78.4 0.0 copy-done.3
  78.4 2.7 %collective-permute-start.2 = (bf16[1024,128]{1,0:T(8,128)(2,1)S(1)}, bf16[1024,128]{1,0:T(8,128)(2,1)S(1)}, u32[]{:S(2)}, u32[]{:S(2)}) collective-permute-start(bf16[1024,128]{1,0:T(8,128)(2,1)S(1)} %copy-done.3), channel_id=1, source_target_pairs={{0,8},{8,0},{1,9},{9,1},{2,10},{10,2},{3,11},{11,3},{4,12},{12,4},... | collective-permute-start | bytes 786440 | tf_op jit(solution)/shard_map/ppermute | solution.py:203
  81.1 1.1 collective-permute-done.2.w_other
  82.2 0.0 copy-start.4
  82.2 13.1 %all-to-all-done.2 = bf16[32,8,1024]{2,1,0:T(8,128)(2,1)S(1)} async-done(((bf16[32,8,1024]{2,1,0:T(8,128)(2,1)}), bf16[32,8,1024]{2,1,0:T(8,128)(2,1)S(1)}, u32[]{:S(2)}, u32[]{:S(2)}) %all-to-all-start.2) | async-done | bytes 524320 | tf_op jit(solution)/shard_map/all_to_all | solution.py:195
  95.4 0.0 copy-start.2
  95.4 0.0 copy-done.4
  95.4 0.8 copy-done.2
  96.2 2.3 %project.1 = f32[512,128]{1,0:T(8,128)} custom-call(bf16[256,1024]{1,0:T(8,128)(2,1)} %bitcast.14, bf16[1024,128]{1,0:T(8,128)(2,1)} %w_mine.1, bf16[1024,128]{1,0:T(8,128)(2,1)} %copy-done.4), custom_call_target="tpu_custom_call" | custom-call | tf_op jit(solution)/shard_map/project/pallas_call | solution.py:187
  98.5 24.1 %all_to_all.43 = f32[16,32,128]{2,1,0:T(8,128)S(1)} all-to-all(f32[16,32,128]{2,1,0:T(8,128)} %bitcast.16), channel_id=1, replica_groups=mesh['y'=8,'z'=4,'c'=2,'w'=2,'x'=4] {'c','w','x'}, dimensions={0} | all-to-all | bytes 524288 | tf_op jit(solution)/shard_map/all_to_all | solution.py:195
  122.6 0.6 copy.6
  (1 shorter events, 0.0 us)
Async XLA Ops:
  1.7 13.6 %copy-start = (bf16[2048,128]{1,0:T(8,128)(2,1)S(1)}, bf16[2048,128]{1,0:T(8,128)(2,1)}, u32[]{:S(2)}) copy-start(bf16[2048,128]{1,0:T(8,128)(2,1)} %k_mine.1) | copy-start | bytes 1572868
  1.7 16.5 %copy-start.1 = (bf16[2048,128]{1,0:T(8,128)(2,1)S(1)}, bf16[2048,128]{1,0:T(8,128)(2,1)}, u32[]{:S(2)}) copy-start(bf16[2048,128]{1,0:T(8,128)(2,1)} %v_mine.1) | copy-start | bytes 1572868
  1.7 31.7 %all-to-all-start = ((bf16[32,8,1152]{2,1,0:T(8,128)(2,1)}), bf16[32,8,1152]{2,1,0:T(8,128)(2,1)S(1)}, u32[]{:S(2)}, u32[]{:S(2)}) async-start(bf16[32,8,1152]{2,1,0:T(8,128)(2,1)} %bitcast.12), calls=%async_computation | async-start | bytes 1179648 | tf_op jit(solution)/shard_map/all_to_all | solution.py:195
  15.3 4.8 %collective-permute-start = (bf16[2048,128]{1,0:T(8,128)(2,1)S(1)}, bf16[2048,128]{1,0:T(8,128)(2,1)S(1)}, u32[]{:S(2)}, u32[]{:S(2)}) collective-permute-start(bf16[2048,128]{1,0:T(8,128)(2,1)S(1)} %copy-done), channel_id=1, source_target_pairs={{0,8},{8,0},{1,9},{9,1},{2,10},{10,2},{3,11},{11,3},{4,12},{12,4},... | collective-permute-start | bytes 1572872 | tf_op jit(solution)/shard_map/ppermute | solution.py:201
  18.2 3.8 %collective-permute-start.1 = (bf16[2048,128]{1,0:T(8,128)(2,1)S(1)}, bf16[2048,128]{1,0:T(8,128)(2,1)S(1)}, u32[]{:S(2)}, u32[]{:S(2)}) collective-permute-start(bf16[2048,128]{1,0:T(8,128)(2,1)S(1)} %copy-done.1), channel_id=1, source_target_pairs={{0,8},{8,0},{1,9},{9,1},{2,10},{10,2},{3,11},{11,3},{4,12},{12,4},... | collective-permute-start | bytes 1572872 | tf_op jit(solution)/shard_map/ppermute | solution.py:202
  72.7 5.6 %copy-start.3 = (bf16[1024,128]{1,0:T(8,128)(2,1)S(1)}, bf16[1024,128]{1,0:T(8,128)(2,1)}, u32[]{:S(2)}) copy-start(bf16[1024,128]{1,0:T(8,128)(2,1)} %w_mine.1) | copy-start | bytes 786436
  72.7 22.6 %all-to-all-start.2 = ((bf16[32,8,1024]{2,1,0:T(8,128)(2,1)}), bf16[32,8,1024]{2,1,0:T(8,128)(2,1)S(1)}, u32[]{:S(2)}, u32[]{:S(2)}) async-start(bf16[32,8,1024]{2,1,0:T(8,128)(2,1)} %bitcast.15), calls=%async_computation.2 | async-start | bytes 1048576 | tf_op jit(solution)/shard_map/all_to_all | solution.py:195
  78.4 3.9 %collective-permute-start.2 = (bf16[1024,128]{1,0:T(8,128)(2,1)S(1)}, bf16[1024,128]{1,0:T(8,128)(2,1)S(1)}, u32[]{:S(2)}, u32[]{:S(2)}) collective-permute-start(bf16[1024,128]{1,0:T(8,128)(2,1)S(1)} %copy-done.3), channel_id=1, source_target_pairs={{0,8},{8,0},{1,9},{9,1},{2,10},{10,2},{3,11},{11,3},{4,12},{12,4},... | collective-permute-start | bytes 786440 | tf_op jit(solution)/shard_map/ppermute | solution.py:203
  82.2 13.1 %copy-start.4 = (bf16[1024,128]{1,0:T(8,128)(2,1)}, bf16[1024,128]{1,0:T(8,128)(2,1)S(1)}, u32[]{:S(2)}) copy-start(bf16[1024,128]{1,0:T(8,128)(2,1)S(1)} %collective-permute-done.2.w_other) | copy-start | bytes 786436
  95.4 0.8 copy-start.2

commit v2 on v1

--- a/solution.py
+++ b/solution.py
@@ -19,13 +19,16 @@
 SCALE = math.log2(math.e) / math.sqrt(HEAD_DIM)
 ROW_BLOCK = 32
 KEY_CHUNK = 2048
-VMEM = 32 * 2**20
-
-AXES = ("y", "z", "c", "w", "x")
-SIZES = (8, 4, 2, 2, 4)
-BLK = ("y", "z", "c")
+VMEM = 24 * 2**20
+SMALL = 8 * 2**20
+
+AXES = ("y", "zh", "zl", "c", "w", "x")
+SIZES = (8, 2, 2, 2, 2, 4)
+BLK = ("y", "zh", "zl", "c")
 HEAD = ("w", "x")
-CHIPS = ("y", "z")
+CHIPS = ("y", "zh", "zl")
+FAR = ("y", "zh")
+NEAR = ("zl", "c")
 SWAP = ((0, 1), (1, 0))
 
 
@@ -33,7 +36,7 @@
     length = k_mine.shape[0]
     rows = q_ref.shape[0]
     many = GROUP * rows
-    me = lax.axis_index("y") * 4 + lax.axis_index("z")
+    me = lax.axis_index("y") * 4 + lax.axis_index("zh") * 2 + lax.axis_index("zl")
     core = lax.axis_index("c")
     start_mine = (me * 2 + core) * length
     start_other = (me * 2 + 1 - core) * length
@@ -163,32 +166,62 @@
         repeated(o_ref, h * HEAD_DIM, sums[h].astype(jnp.bfloat16))
 
 
-def combine(parts):
+def combine(parts, receivers):
     return pl.pallas_call(
         combine_kernel,
-        out_shape=jax.ShapeDtypeStruct((parts.shape[0], WIDTH), jnp.bfloat16),
+        out_shape=jax.ShapeDtypeStruct((8 * receivers, WIDTH), jnp.bfloat16),
+        compiler_params=pltpu.CompilerParams(vmem_limit_bytes=SMALL),
         name="combine",
     )(parts)
 
 
-def project_kernel(a_ref, w_mine, w_other, o_ref):
+def project_kernel(a_ref, w_ref, w_core, w_chip, w_both, o_ref):
     rows = a_ref.shape[0]
+    chip = lax.axis_index("zl")
     core = lax.axis_index("c")
     attended = a_ref[...]
-    for place, weight in ((core, w_mine), (1 - core, w_other)):
-        at = pl.multiple_of(place * rows, rows)
-        o_ref[pl.ds(at, rows), :] = jnp.dot(
-            attended, weight[...], preferred_element_type=jnp.float32
-        )
-
-
-def project(attended, w_mine, w_other):
+    for there, that, weight in (
+        (chip, core, w_ref),
+        (chip, 1 - core, w_core),
+        (1 - chip, core, w_chip),
+        (1 - chip, 1 - core, w_both),
+    ):
+        at = pl.multiple_of((there * 2 + that) * rows, rows)
+        part = jnp.dot(attended, weight[...], preferred_element_type=jnp.float32)
+        o_ref[pl.ds(at, rows), :] = part.astype(o_ref.dtype)
+
+
+def project(attended, *weights):
     rows = attended.shape[0]
     return pl.pallas_call(
         project_kernel,
-        out_shape=jax.ShapeDtypeStruct((2 * rows, w_mine.shape[1]), jnp.float32),
+        out_shape=jax.ShapeDtypeStruct((len(weights) * rows, LANES), jnp.bfloat16),
+        compiler_params=pltpu.CompilerParams(vmem_limit_bytes=SMALL),
         name="project",
-    )(attended, w_mine, w_other)
+    )(attended, *weights)
+
+
+def total_kernel(s_ref, o_ref):
+    near, heads, rows = 4, 8, 16
+    half = rows // 2
+    for n in range(near):
+        parts = [
+            s_ref[(n * heads + h) * rows : (n * heads + h + 1) * rows, :].astype(jnp.float32)
+            for h in range(heads)
+        ]
+        total = functools.reduce(jnp.add, parts)
+        for z in range(2):
+            at = (z * near + n) * half
+            o_ref[at : at + half, :] = total[z * half : (z + 1) * half]
+
+
+def total_of(sums):
+    return pl.pallas_call(
+        total_kernel,
+        out_shape=jax.ShapeDtypeStruct((64, LANES), jnp.float32),
+        compiler_params=pltpu.CompilerParams(vmem_limit_bytes=SMALL),
+        name="total",
+    )(sums)
 
 
 def exchange(x, axis):
@@ -196,18 +229,18 @@
 
 
 def shards(queries, keys, values, cutoffs, out_weight):
-    rows = queries.shape[0]
-    chips = SIZES[0] * SIZES[1]
+    chips = SIZES[0] * SIZES[1] * SIZES[2]
+    far = SIZES[0] * SIZES[1]
     k_other = lax.ppermute(keys, "c", SWAP)
     v_other = lax.ppermute(values, "c", SWAP)
-    w_other = lax.ppermute(out_weight, "c", SWAP)
+    w_core = lax.ppermute(out_weight, "c", SWAP)
+    w_chip = lax.ppermute(out_weight, "zl", SWAP)
+    w_both = lax.ppermute(w_chip, "c", SWAP)
     packed = exchange(pack(queries, cutoffs, chips), CHIPS)
     parts = exchange(attend(packed, keys, values, k_other, v_other), CHIPS)
-    attended = exchange(combine(parts), CHIPS)
-    sums = exchange(project(attended, out_weight, w_other), ("c",) + HEAD)
-    heads = SIZES[3] * SIZES[4]
-    sums = sums.reshape(2, heads, SIZES[1], rows, LANES).sum(axis=1)
-    return sums.transpose(1, 0, 2, 3).reshape(2 * SIZES[1] * rows, LANES)
+    attended = exchange(combine(parts, far), FAR)
+    sums = project(attended, out_weight, w_core, w_chip, w_both)
+    return total_of(exchange(sums, NEAR + HEAD))
 
 
 def solution(mesh):

time: 124 us -> 112 us (0.903)
  blocking collectives: 47.8 us -> 23.6 us
  starting transfers between devices: 26.7 us -> 37 us
  waiting for transfers between devices: 27.5 us -> 32.9 us
  Pallas kernels: 19.7 us -> 17.8 us
  local copies, waits for them, and re-layouts: 1.43 us -> 0.01 us
    all_to_all x2 -> x1, blocking collectives: 47.8 us -> 23.6 us  [exchange(): return lax.all_to_all(x, axis, 0, 0, tiled=True)]
    ppermute x1 -> x3, starting transfers between devices: 2.72 us -> 9.07 us  [the longest x1 4.01 us: shards(): w_core = lax.ppermute(out_weight, 'c', SWAP)]
    all_to_all x2 -> x3, waiting for transfers between devices: 24.5 us -> 29.5 us  [exchange(): return lax.all_to_all(x, axis, 0, 0, tiled=True)]
    all_to_all x2 -> x3, starting transfers between devices: 19.2 us -> 23.2 us  [exchange(): return lax.all_to_all(x, axis, 0, 0, tiled=True)]
    pallas_call x2 -> x3, Pallas kernels: 4.91 us -> 2.43 us  [the longest x1 1.38 us: combine(): pl.pallas_call(combine_kernel, out_shape=jax.ShapeDtypeStruct((8 * receiv...]
  transfers between devices with their start and end apart: 5 -> 8, of which waited for: 4 -> 5; matrix products, arithmetic and copies ran while one was open for 0% -> 0% of each run, Pallas kernels for 0% -> 1%
where the time goes in v2:
time: 112 us; the launch traced here: 111 us
  starting transfers between devices  37 us (33%)
  waiting for transfers between devices  32.9 us (29%)
  blocking collectives  23.6 us (21%)
  Pallas kernels  17.8 us (16%)
    all_to_all x3, waiting for transfers between devices, exchange(): return lax.all_to_all(x, axis, 0, 0, tiled=True)  29.5 us
    all_to_all x1, blocking collectives, exchange(): return lax.all_to_all(x, axis, 0, 0, tiled=True)  23.6 us
    all_to_all x3, starting transfers between devices, exchange(): return lax.all_to_all(x, axis, 0, 0, tiled=True)  23.2 us
    pallas_call x1, Pallas kernels, attend(): pl.pallas_call(attend_kernel, grid=(rows // ROW_BLOCK,), in_specs=[block,...  13.8 us
    ppermute x1, starting transfers between devices, shards(): w_core = lax.ppermute(out_weight, 'c', SWAP)  4.01 us
    ppermute x1, starting transfers between devices, shards(): w_chip = lax.ppermute(out_weight, 'zl', SWAP)  3.14 us
    ppermute x1, starting transfers between devices, shards(): k_other = lax.ppermute(keys, 'c', SWAP)  2.86 us
  transfers between devices with their start and end apart: 8, of which 5 were waited for; matrix products, arithmetic and copies ran while one was open for 0% of the time, Pallas kernels for 1%

profile of v2, /device:TPU:1, one launch (start us, length us, event | category | flops | bytes accessed | tf_op | source)
XLA Modules:
  0.0 111.4 jit_solution(5899567390142592376)
XLA Ops:
  0.0 1.7 %pack.1 = bf16[256,1152]{1,0:T(8,128)(2,1)} custom-call(bf16[8,1024]{1,0:T(8,128)(2,1)} %q_ref.1, s32[8]{0:T(128)} %cut_ref.1), custom_call_target="tpu_custom_call" | custom-call | tf_op jit(solution)/shard_map/pack/pallas_call | solution.py:135
  1.7 0.0 copy-start
  1.7 0.0 copy-start.1
  1.7 13.6 %all-to-all-start = ((bf16[32,8,1152]{2,1,0:T(8,128)(2,1)}), bf16[32,8,1152]{2,1,0:T(8,128)(2,1)S(1)}, u32[]{:S(2)}, u32[]{:S(2)}) async-start(bf16[32,8,1152]{2,1,0:T(8,128)(2,1)} %bitcast.13), calls=%async_computation | async-start | bytes 1179648 | tf_op jit(solution)/shard_map/all_to_all | solution.py:228
  15.3 0.0 copy-done
  15.3 2.9 %collective-permute-start = (bf16[2048,128]{1,0:T(8,128)(2,1)S(1)}, bf16[2048,128]{1,0:T(8,128)(2,1)S(1)}, u32[]{:S(2)}, u32[]{:S(2)}) collective-permute-start(bf16[2048,128]{1,0:T(8,128)(2,1)S(1)} %copy-done), channel_id=1, source_target_pairs={{0,8},{8,0},{1,9},{9,1},{2,10},{10,2},{3,11},{11,3},{4,12},{12,4},... | collective-permute-start | bytes 1572872 | tf_op jit(solution)/shard_map/ppermute | solution.py:234
  18.1 0.0 copy-done.1
  18.2 1.9 %collective-permute-start.1 = (bf16[2048,128]{1,0:T(8,128)(2,1)S(1)}, bf16[2048,128]{1,0:T(8,128)(2,1)S(1)}, u32[]{:S(2)}, u32[]{:S(2)}) collective-permute-start(bf16[2048,128]{1,0:T(8,128)(2,1)S(1)} %copy-done.1), channel_id=1, source_target_pairs={{0,8},{8,0},{1,9},{9,1},{2,10},{10,2},{3,11},{11,3},{4,12},{12,4},... | collective-permute-start | bytes 1572872 | tf_op jit(solution)/shard_map/ppermute | solution.py:235
  20.1 0.0 collective-permute-done.k_other
  20.1 1.9 %collective-permute-done.1.v_other = bf16[2048,128]{1,0:T(8,128)(2,1)S(1)} collective-permute-done((bf16[2048,128]{1,0:T(8,128)(2,1)S(1)}, bf16[2048,128]{1,0:T(8,128)(2,1)S(1)}, u32[]{:S(2)}, u32[]{:S(2)}) %collective-permute-start.1) | collective-permute-done | bytes 524320 | tf_op jit(solution)/shard_map/ppermute | solution.py:235
  22.0 11.4 %all-to-all-done = bf16[32,8,1152]{2,1,0:T(8,128)(2,1)S(1)} async-done(((bf16[32,8,1152]{2,1,0:T(8,128)(2,1)}), bf16[32,8,1152]{2,1,0:T(8,128)(2,1)S(1)}, u32[]{:S(2)}, u32[]{:S(2)}) %all-to-all-start) | async-done | bytes 589856 | tf_op jit(solution)/shard_map/all_to_all | solution.py:228
  33.3 13.8 %attend.1 = bf16[256,1152]{1,0:T(8,128)(2,1)} custom-call(bf16[256,1152]{1,0:T(8,128)(2,1)S(1)} %bitcast.8, bf16[2048,128]{1,0:T(8,128)(2,1)S(1)} %copy-done, bf16[2048,128]{1,0:T(8,128)(2,1)S(1)} %copy-done.1, bf16[2048,128]{1,0:T(8,128)(2,1)S(1)} %collective-permute-done.k_other, bf16[2048,128]{1,0:T(8,128)(2,1)S(1)} %collective-permute-done.1.v_other), custom_call_target="tpu_custom_call" | custom-call | tf_op jit(solution)/shard_map/attend/pallas_call | solution.py:103
  47.1 0.0 copy-start.2
  47.1 5.7 %all-to-all-start.1 = ((bf16[32,8,1152]{2,1,0:T(8,128)(2,1)}), bf16[32,8,1152]{2,1,0:T(8,128)(2,1)S(1)}, u32[]{:S(2)}, u32[]{:S(2)}) async-start(bf16[32,8,1152]{2,1,0:T(8,128)(2,1)} %bitcast.2), calls=%async_computation.1 | async-start | bytes 1179648 | tf_op jit(solution)/shard_map/all_to_all | solution.py:228
  52.8 0.0 copy-done.2
  52.8 3.1 %collective-permute-start.3 = (bf16[1024,128]{1,0:T(8,128)(2,1)S(1)}, bf16[1024,128]{1,0:T(8,128)(2,1)S(1)}, u32[]{:S(2)}, u32[]{:S(2)}) collective-permute-start(bf16[1024,128]{1,0:T(8,128)(2,1)S(1)} %copy-done.2), channel_id=1, source_target_pairs={{0,16},{16,0},{1,17},{17,1},{2,18},{18,2},{3,19},{19,3},{4,20},{20... | collective-permute-start | bytes 786440 | tf_op jit(solution)/shard_map/ppermute | solution.py:237
  56.0 15.1 %all-to-all-done.1 = bf16[32,8,1152]{2,1,0:T(8,128)(2,1)S(1)} async-done(((bf16[32,8,1152]{2,1,0:T(8,128)(2,1)}), bf16[32,8,1152]{2,1,0:T(8,128)(2,1)S(1)}, u32[]{:S(2)}, u32[]{:S(2)}) %all-to-all-start.1) | async-done | bytes 589856 | tf_op jit(solution)/shard_map/all_to_all | solution.py:228
  71.0 1.4 %combine.1 = bf16[128,1024]{1,0:T(8,128)(2,1)} custom-call(bf16[256,1152]{1,0:T(8,128)(2,1)S(1)} %bitcast.9), custom_call_target="tpu_custom_call" | custom-call | tf_op jit(solution)/shard_map/combine/pallas_call | solution.py:170
  72.4 3.9 %all-to-all-start.2 = ((bf16[16,8,1024]{2,1,0:T(8,128)(2,1)}), bf16[16,8,1024]{2,1,0:T(8,128)(2,1)S(1)}, u32[]{:S(2)}, u32[]{:S(2)}) async-start(bf16[16,8,1024]{2,1,0:T(8,128)(2,1)} %bitcast.4), calls=%async_computation.2 | async-start | bytes 524288 | tf_op jit(solution)/shard_map/all_to_all | solution.py:228
  76.3 4.0 %collective-permute-start.2 = (bf16[1024,128]{1,0:T(8,128)(2,1)S(1)}, bf16[1024,128]{1,0:T(8,128)(2,1)S(1)}, u32[]{:S(2)}, u32[]{:S(2)}) collective-permute-start(bf16[1024,128]{1,0:T(8,128)(2,1)S(1)} %copy-done.2), channel_id=1, source_target_pairs={{0,8},{8,0},{1,9},{9,1},{2,10},{10,2},{3,11},{11,3},{4,12},{12,4},... | collective-permute-start | bytes 786440 | tf_op jit(solution)/shard_map/ppermute | solution.py:236
  80.3 0.0 collective-permute-done.3.w_chip
  80.3 1.9 %collective-permute-start.4 = (bf16[1024,128]{1,0:T(8,128)(2,1)S(1)}, bf16[1024,128]{1,0:T(8,128)(2,1)S(1)}, u32[]{:S(2)}, u32[]{:S(2)}) collective-permute-start(bf16[1024,128]{1,0:T(8,128)(2,1)S(1)} %collective-permute-done.3.w_chip), channel_id=1, source_target_pairs={{0,8},{8,0},{1,9},{9,1},{2,10},{10,2},{3,11},{11,3},{4,12},{12,4},... | collective-permute-start | bytes 786440 | tf_op jit(solution)/shard_map/ppermute | solution.py:238
  82.2 0.0 collective-permute-done.2.w_core
  82.2 1.5 %collective-permute-done.4.w_both = bf16[1024,128]{1,0:T(8,128)(2,1)S(1)} collective-permute-done((bf16[1024,128]{1,0:T(8,128)(2,1)S(1)}, bf16[1024,128]{1,0:T(8,128)(2,1)S(1)}, u32[]{:S(2)}, u32[]{:S(2)}) %collective-permute-start.4) | collective-permute-done | bytes 262176 | tf_op jit(solution)/shard_map/ppermute | solution.py:238
  83.7 3.1 %all-to-all-done.2 = bf16[16,8,1024]{2,1,0:T(8,128)(2,1)S(1)} async-done(((bf16[16,8,1024]{2,1,0:T(8,128)(2,1)}), bf16[16,8,1024]{2,1,0:T(8,128)(2,1)S(1)}, u32[]{:S(2)}, u32[]{:S(2)}) %all-to-all-start.2) | async-done | bytes 262176 | tf_op jit(solution)/shard_map/all_to_all | solution.py:228
  86.8 0.4 project.1
  87.2 23.6 %all_to_all.44 = bf16[32,16,128]{2,1,0:T(8,128)(2,1)S(1)} all-to-all(bf16[32,16,128]{2,1,0:T(8,128)(2,1)S(1)} %bitcast.12), channel_id=1, replica_groups=mesh['y'=8,'zh'=2,'zl'=2,'c'=2,'w'=2,'x'=4] {'zl','c','w','x'}, dimensions={0} | all-to-all | bytes 262144 | tf_op jit(solution)/shard_map/all_to_all | solution.py:228
  110.8 0.6 total.1
Async XLA Ops:
  1.7 13.6 %copy-start = (bf16[2048,128]{1,0:T(8,128)(2,1)S(1)}, bf16[2048,128]{1,0:T(8,128)(2,1)}, u32[]{:S(2)}) copy-start(bf16[2048,128]{1,0:T(8,128)(2,1)} %k_mine.1) | copy-start | bytes 1572868
  1.7 16.5 %copy-start.1 = (bf16[2048,128]{1,0:T(8,128)(2,1)S(1)}, bf16[2048,128]{1,0:T(8,128)(2,1)}, u32[]{:S(2)}) copy-start(bf16[2048,128]{1,0:T(8,128)(2,1)} %v_mine.1) | copy-start | bytes 1572868
  1.7 31.7 %all-to-all-start = ((bf16[32,8,1152]{2,1,0:T(8,128)(2,1)}), bf16[32,8,1152]{2,1,0:T(8,128)(2,1)S(1)}, u32[]{:S(2)}, u32[]{:S(2)}) async-start(bf16[32,8,1152]{2,1,0:T(8,128)(2,1)} %bitcast.13), calls=%async_computation | async-start | bytes 1179648 | tf_op jit(solution)/shard_map/all_to_all | solution.py:228
  15.3 4.8 %collective-permute-start = (bf16[2048,128]{1,0:T(8,128)(2,1)S(1)}, bf16[2048,128]{1,0:T(8,128)(2,1)S(1)}, u32[]{:S(2)}, u32[]{:S(2)}) collective-permute-start(bf16[2048,128]{1,0:T(8,128)(2,1)S(1)} %copy-done), channel_id=1, source_target_pairs={{0,8},{8,0},{1,9},{9,1},{2,10},{10,2},{3,11},{11,3},{4,12},{12,4},... | collective-permute-start | bytes 1572872 | tf_op jit(solution)/shard_map/ppermute | solution.py:234
  18.2 3.8 %collective-permute-start.1 = (bf16[2048,128]{1,0:T(8,128)(2,1)S(1)}, bf16[2048,128]{1,0:T(8,128)(2,1)S(1)}, u32[]{:S(2)}, u32[]{:S(2)}) collective-permute-start(bf16[2048,128]{1,0:T(8,128)(2,1)S(1)} %copy-done.1), channel_id=1, source_target_pairs={{0,8},{8,0},{1,9},{9,1},{2,10},{10,2},{3,11},{11,3},{4,12},{12,4},... | collective-permute-start | bytes 1572872 | tf_op jit(solution)/shard_map/ppermute | solution.py:235
  47.1 5.7 %copy-start.2 = (bf16[1024,128]{1,0:T(8,128)(2,1)S(1)}, bf16[1024,128]{1,0:T(8,128)(2,1)}, u32[]{:S(2)}) copy-start(bf16[1024,128]{1,0:T(8,128)(2,1)} %w_ref.1) | copy-start | bytes 786436
  47.1 23.9 %all-to-all-start.1 = ((bf16[32,8,1152]{2,1,0:T(8,128)(2,1)}), bf16[32,8,1152]{2,1,0:T(8,128)(2,1)S(1)}, u32[]{:S(2)}, u32[]{:S(2)}) async-start(bf16[32,8,1152]{2,1,0:T(8,128)(2,1)} %bitcast.2), calls=%async_computation.1 | async-start | bytes 1179648 | tf_op jit(solution)/shard_map/all_to_all | solution.py:228
  52.8 27.5 %collective-permute-start.3 = (bf16[1024,128]{1,0:T(8,128)(2,1)S(1)}, bf16[1024,128]{1,0:T(8,128)(2,1)S(1)}, u32[]{:S(2)}, u32[]{:S(2)}) collective-permute-start(bf16[1024,128]{1,0:T(8,128)(2,1)S(1)} %copy-done.2), channel_id=1, source_target_pairs={{0,16},{16,0},{1,17},{17,1},{2,18},{18,2},{3,19},{19,3},{4,20},{20... | collective-permute-start | bytes 786440 | tf_op jit(solution)/shard_map/ppermute | solution.py:237
  72.4 14.4 %all-to-all-start.2 = ((bf16[16,8,1024]{2,1,0:T(8,128)(2,1)}), bf16[16,8,1024]{2,1,0:T(8,128)(2,1)S(1)}, u32[]{:S(2)}, u32[]{:S(2)}) async-start(bf16[16,8,1024]{2,1,0:T(8,128)(2,1)} %bitcast.4), calls=%async_computation.2 | async-start | bytes 524288 | tf_op jit(solution)/shard_map/all_to_all | solution.py:228
  76.3 6.0 %collective-permute-start.2 = (bf16[1024,128]{1,0:T(8,128)(2,1)S(1)}, bf16[1024,128]{1,0:T(8,128)(2,1)S(1)}, u32[]{:S(2)}, u32[]{:S(2)}) collective-permute-start(bf16[1024,128]{1,0:T(8,128)(2,1)S(1)} %copy-done.2), channel_id=1, source_target_pairs={{0,8},{8,0},{1,9},{9,1},{2,10},{10,2},{3,11},{11,3},{4,12},{12,4},... | collective-permute-start | bytes 786440 | tf_op jit(solution)/shard_map/ppermute | solution.py:236
  80.3 3.4 %collective-permute-start.4 = (bf16[1024,128]{1,0:T(8,128)(2,1)S(1)}, bf16[1024,128]{1,0:T(8,128)(2,1)S(1)}, u32[]{:S(2)}, u32[]{:S(2)}) collective-permute-start(bf16[1024,128]{1,0:T(8,128)(2,1)S(1)} %collective-permute-done.3.w_chip), channel_id=1, source_target_pairs={{0,8},{8,0},{1,9},{9,1},{2,10},{10,2},{3,11},{11,3},{4,12},{12,4},... | collective-permute-start | bytes 786440 | tf_op jit(solution)/shard_map/ppermute | solution.py:238

commit v3 on v2

v3 whole, which is shorter than its diff:
```python
import functools
import math

import jax
import jax.numpy as jnp
from jax import lax
from jax.experimental import pallas as pl
from jax.experimental.pallas import tpu as pltpu
from jax.sharding import Mesh
from jax.sharding import PartitionSpec as P

HEAD_DIM = 128
GROUP = 8
LANES = 128
WIDTH = GROUP * HEAD_DIM
PACKED = WIDTH + LANES
NEG = -1e30
FLOOR = -1e20
SCALE = math.log2(math.e) / math.sqrt(HEAD_DIM)
ROW_BLOCK = 64
PROBE = 128
LEAP = 400.0
VMEM = 24 * 2**20
SMALL = 8 * 2**20

AXES = ("y", "zh", "zl", "c", "w", "x")
SIZES = (8, 2, 2, 2, 2, 4)
BLK = ("y", "zh", "zl", "c")
HEAD = ("w", "x")
FAR = ("y", "zh")
NEAR = ("zl", "c")
SWAP = ((0, 1), (1, 0))


def split(x):
    high = x.astype(jnp.bfloat16).astype(jnp.float32)
    middle = (x - high).astype(jnp.bfloat16).astype(jnp.float32)
    return high, middle, x - high - middle


def attend_kernel(chunk, whose, q_ref, k_mine, v_mine, k_other, v_other, o_ref):
    pairs = ((k_mine, v_mine), (k_other, v_other))
    rows = o_ref.shape[0]
    many = GROUP * ROW_BLOCK
    length = k_mine.shape[0]
    chip = lax.axis_index("zl")
    core = lax.axis_index("c")
    me = lax.axis_index("y") * 8 + lax.axis_index("zh") * 4 + chip * 2
    starts = ((me + core) * length, (me + 1 - core) * length)
    base = (1 - chip if whose else chip) * rows

    def load(i):
        packed = q_ref[pl.ds(pl.multiple_of(base + i * ROW_BLOCK, ROW_BLOCK), ROW_BLOCK), :]
        queries = jnp.concatenate(
            [packed[:, h * HEAD_DIM : (h + 1) * HEAD_DIM] for h in range(GROUP)], axis=0
        )
        digits = packed[:, WIDTH:].astype(jnp.float32)
        cut = digits[:, 0:1] + 64.0 * digits[:, 1:2] + 4096.0 * digits[:, 2:3]
        cut = jnp.concatenate([cut.astype(jnp.int32)] * GROUP, axis=0)
        return queries, cut

    def scores_of(queries, cut, n, at, size):
        scores = lax.dot_general(
            queries,
            pairs[n][0][at : at + size, :],
            (((1,), (1,)), ((), ())),
            preferred_element_type=jnp.float32,
        )
        places = lax.broadcasted_iota(jnp.int32, (many, size), 1)
        return jnp.where(places < cut - (starts[n] + at), scores, NEG)

    def weighed(acc, scores, level, n, at, size):
        weights = jnp.exp2(scores * SCALE - level * SCALE).astype(jnp.bfloat16)
        wide = [pairs[n][1][at : at + size, :], jnp.ones((size, LANES), jnp.bfloat16)]
        wide = jnp.concatenate(wide, axis=1)
        return acc + jnp.dot(weights, wide, preferred_element_type=jnp.float32)

    def store(i, level, acc):
        level = jnp.broadcast_to(level, (many, LANES))
        here = pl.ds(pl.multiple_of(i * ROW_BLOCK, ROW_BLOCK), ROW_BLOCK)
        total = acc[:, HEAD_DIM:]
        some = jnp.maximum(total, 1e-30)
        mixed = (acc[:, :HEAD_DIM] / some).astype(jnp.bfloat16)
        level = jnp.where(total > 0.0, level * SCALE + jnp.log2(some), NEG)
        high, middle, low = split(level)
        lane = lax.broadcasted_iota(jnp.int32, (ROW_BLOCK, LANES), 1)
        stats = jnp.zeros((ROW_BLOCK, LANES), jnp.float32)
        for h in range(GROUP):
            mine = slice(h * ROW_BLOCK, (h + 1) * ROW_BLOCK)
            o_ref[here, h * HEAD_DIM : (h + 1) * HEAD_DIM] = mixed[mine]
            part = jnp.where(lane < 8, high[mine], jnp.where(lane < 16, middle[mine], low[mine]))
            stats = jnp.where((lane & 7) == h, part, stats)
        o_ref[here, WIDTH:] = jnp.where(lane < 24, stats, 0.0).astype(jnp.bfloat16)

    def quick(i, leap):
        queries, cut = load(i)
        acc = jnp.zeros((many, HEAD_DIM + LANES), jnp.float32)
        level = jnp.full((many, 1), FLOOR, jnp.float32)
        for n in range(len(pairs)):
            probe = scores_of(queries, cut, n, 0, PROBE)
            level = jnp.maximum(level, jnp.max(probe, axis=1, keepdims=True))
        most = jnp.full((many, LANES), FLOOR, jnp.float32)
        for n in range(len(pairs)):
            for at in range(0, length, chunk):
                scores = scores_of(queries, cut, n, at, chunk)
                for t in range(0, chunk, LANES):
                    most = jnp.maximum(most, scores[:, t : t + LANES])
                acc = weighed(acc, scores, level, n, at, chunk)
        store(i, level, acc)
        return jnp.maximum(leap, most - level)

    leap = jnp.full((many, LANES), FLOOR, jnp.float32)
    leap = lax.fori_loop(0, rows // ROW_BLOCK, quick, leap)

    @pl.when(jnp.max(leap) > LEAP)
    def _():
        def exact(i, unused):
            queries, cut = load(i)
            acc = jnp.zeros((many, HEAD_DIM + LANES), jnp.float32)
            level = jnp.full((many, 1), FLOOR, jnp.float32)
            for n in range(len(pairs)):
                scores = scores_of(queries, cut, n, 0, length)
                higher = jnp.maximum(level, jnp.max(scores, axis=1, keepdims=True))
                acc = weighed(acc * jnp.exp2((level - higher) * SCALE), scores, higher, n, 0, length)
                level = higher
            store(i, level, acc)
            return unused

        lax.fori_loop(0, rows // ROW_BLOCK, exact, 0)


def attend(packed, whose, *pairs):
    rows = packed.shape[0] // 2
    vmem = pl.BlockSpec(memory_space=pltpu.VMEM)
    work = 4 * rows * GROUP * pairs[0].shape[0] * HEAD_DIM
    return pl.pallas_call(
        functools.partial(attend_kernel, 256, whose),
        in_specs=[vmem] * (1 + len(pairs)),
        out_specs=vmem,
        out_shape=jax.ShapeDtypeStruct((rows, PACKED), jnp.bfloat16),
        compiler_params=pltpu.CompilerParams(vmem_limit_bytes=VMEM),
        cost_estimate=pl.CostEstimate(
            flops=4 * work, bytes_accessed=2**21, transcendentals=work // 256
        ),
        name="attend",
    )(packed, *pairs)


def level_of(stats):
    stats = stats.astype(jnp.float32)
    return stats + jnp.roll(stats, -8, axis=1) + jnp.roll(stats, -16, axis=1)


def merge_kernel(a_ref, b_ref, o_ref):
    rows = 64
    lane = lax.broadcasted_iota(jnp.int32, (rows, LANES), 1)
    for at in range(0, o_ref.shape[0], rows):
        here = slice(at, at + rows)
        levels = [level_of(ref[here, WIDTH:]) for ref in (a_ref, b_ref)]
        top = jnp.maximum(*levels)
        shares = [jnp.exp2(level - top) for level in levels]
        total = shares[0] + shares[1]
        shares = [share / total for share in shares]
        for h in range(GROUP):
            head = slice(h * HEAD_DIM, (h + 1) * HEAD_DIM)
            mixed = a_ref[here, head].astype(jnp.float32) * shares[0][:, h : h + 1]
            mixed = mixed + b_ref[here, head].astype(jnp.float32) * shares[1][:, h : h + 1]
            o_ref[here, head] = mixed.astype(jnp.bfloat16)
        high, middle, low = split(top + jnp.log2(total))
        stats = jnp.where(
            lane < 8,
            high,
            jnp.where(lane < 16, jnp.roll(middle, 8, axis=1), jnp.roll(low, 16, axis=1)),
        )
        o_ref[here, WIDTH:] = jnp.where(lane < 24, stats, 0.0).astype(jnp.bfloat16)


def merge(a, b):
    return pl.pallas_call(
        merge_kernel,
        out_shape=jax.ShapeDtypeStruct(a.shape, a.dtype),
        compiler_params=pltpu.CompilerParams(vmem_limit_bytes=SMALL),
        name="merge",
    )(a, b)


def repeated(o_ref, at, block):
    twice = jnp.concatenate([block, block], axis=0)
    for top in range(0, o_ref.shape[0], twice.shape[0]):
        o_ref[top : top + twice.shape[0], at : at + block.shape[1]] = twice


def pack_kernel(q_ref, cut_ref, o_ref):
    rows = q_ref.shape[0]
    lane = lax.broadcasted_iota(jnp.int32, (rows, LANES), 1)
    row = lax.broadcasted_iota(jnp.int32, (rows, LANES), 0)
    cut = jnp.zeros((rows, LANES), jnp.int32)
    for r in range(rows):
        cut = jnp.where(row == r, cut_ref[r], cut)
    digits = jnp.where(lane == 0, cut & 63, jnp.where(lane == 1, (cut >> 6) & 63, cut >> 12))
    digits = digits.astype(jnp.float32).astype(jnp.bfloat16)
    repeated(o_ref, 0, q_ref[...])
    repeated(o_ref, WIDTH, digits)


def pack(queries, cutoffs, receivers):
    rows = queries.shape[0]
    return pl.pallas_call(
        pack_kernel,
        in_specs=[
            pl.BlockSpec(memory_space=pltpu.VMEM),
            pl.BlockSpec(memory_space=pltpu.SMEM),
        ],
        out_shape=jax.ShapeDtypeStruct((receivers * rows, PACKED), jnp.bfloat16),
        name="pack",
    )(queries, cutoffs)


def combine_kernel(p_ref, o_ref):
    rows = 8
    sources = p_ref.shape[0] // rows
    levels = []
    for n in range(sources // 2):
        level = level_of(p_ref[2 * n * rows : 2 * (n + 1) * rows, WIDTH:])
        levels += [level[:rows], level[rows:]]
    top = functools.reduce(jnp.maximum, levels)
    shares = [jnp.exp2(level - top) for level in levels]
    total = 1.0 / functools.reduce(jnp.add, shares)
    shares = [share * total for share in shares]
    sums = [jnp.zeros((rows, HEAD_DIM), jnp.float32) for _ in range(GROUP)]
    for n in range(sources // 2):
        for h in range(GROUP):
            part = p_ref[2 * n * rows : 2 * (n + 1) * rows, h * HEAD_DIM : (h + 1) * HEAD_DIM]
            part = part.astype(jnp.float32)
            sums[h] = sums[h] + part[:rows] * shares[2 * n][:, h : h + 1]
            sums[h] = sums[h] + part[rows:] * shares[2 * n + 1][:, h : h + 1]
    for h in range(GROUP):
        repeated(o_ref, h * HEAD_DIM, sums[h].astype(jnp.bfloat16))


def combine(parts, receivers):
    return pl.pallas_call(
        combine_kernel,
        out_shape=jax.ShapeDtypeStruct((8 * receivers, WIDTH), jnp.bfloat16),
        compiler_params=pltpu.CompilerParams(vmem_limit_bytes=SMALL),
        name="combine",
    )(parts)


def project_kernel(a_ref, w_ref, w_core, w_chip, w_both, o_ref):
    rows = a_ref.shape[0]
    chip = lax.axis_index("zl")
    core = lax.axis_index("c")
    attended = a_ref[...]
    for there, that, weight in (
        (chip, core, w_ref),
        (chip, 1 - core, w_core),
        (1 - chip, core, w_chip),
        (1 - chip, 1 - core, w_both),
    ):
        at = pl.multiple_of((there * 2 + that) * rows, rows)
        part = jnp.dot(attended, weight[...], preferred_element_type=jnp.float32)
        o_ref[pl.ds(at, rows), :] = part.astype(o_ref.dtype)


def project(attended, *weights):
    rows = attended.shape[0]
    return pl.pallas_call(
        project_kernel,
        out_shape=jax.ShapeDtypeStruct((len(weights) * rows, LANES), jnp.bfloat16),
        compiler_params=pltpu.CompilerParams(vmem_limit_bytes=SMALL),
        name="project",
    )(attended, *weights)


def total_kernel(s_ref, o_ref):
    near, heads, rows = 4, 8, 16
    half = rows // 2
    for n in range(near):
        parts = [
            s_ref[(n * heads + h) * rows : (n * heads + h + 1) * rows, :].astype(jnp.float32)
            for h in range(heads)
        ]
        total = functools.reduce(jnp.add, parts)
        for z in range(2):
            at = (z * near + n) * half
            o_ref[at : at + half, :] = total[z * half : (z + 1) * half]


def total_of(sums):
    return pl.pallas_call(
        total_kernel,
        out_shape=jax.ShapeDtypeStruct((64, LANES), jnp.float32),
        compiler_params=pltpu.CompilerParams(vmem_limit_bytes=SMALL),
        name="total",
    )(sums)


def exchange(x, axis):
    return lax.all_to_all(x, axis, 0, 0, tiled=True)


def shards(queries, keys, values, cutoffs, out_weight):
    far = SIZES[0] * SIZES[1]
    k_other = lax.ppermute(keys, "c", SWAP)
    v_other = lax.ppermute(values, "c", SWAP)
    packed = exchange(pack(queries, cutoffs, 2 * far), ("zl",) + FAR)
    pairs = (keys, values, k_other, v_other)
    away = lax.ppermute(attend(packed, 1, *pairs), "zl", SWAP)
    parts = exchange(merge(attend(packed, 0, *pairs), away), FAR)
    w_core = lax.ppermute(out_weight, "c", SWAP)
    w_chip = lax.ppermute(out_weight, "zl", SWAP)
    w_both = lax.ppermute(w_chip, "c", SWAP)
    attended = exchange(combine(parts, far), FAR)
    sums = project(attended, out_weight, w_core, w_chip, w_both)
    return total_of(exchange(sums, NEAR + HEAD))


def solution(mesh):
    fine = Mesh(mesh.devices.reshape(SIZES), AXES)
    return jax.shard_map(
        shards,
        mesh=fine,
        in_specs=(P(BLK, HEAD), P(BLK, HEAD), P(BLK, HEAD), P(BLK), P(HEAD, BLK)),
        out_specs=P(HEAD, BLK),
        check_vma=False,
    )
```

time: 112 us -> 107 us (0.955)
  waiting for transfers between devices: 32.9 us -> 23.4 us
  starting transfers between devices: 37 us -> 40.5 us
  blocking collectives: 23.6 us -> 24.8 us
    all_to_all x3, waiting for transfers between devices: 29.5 us -> 20 us  [exchange(): return lax.all_to_all(x, axis, 0, 0, tiled=True)]
    ppermute x0 -> x1, starting transfers between devices: none -> 1.92 us  [shards(): away = lax.ppermute(attend(packed, 1, *pairs), 'zl', SWAP)]
    ppermute x1, starting transfers between devices: 4.01 us -> 5.65 us  [shards(): w_core = lax.ppermute(out_weight, 'c', SWAP)]
    all_to_all x1, blocking collectives: 23.6 us -> 24.8 us  [exchange(): return lax.all_to_all(x, axis, 0, 0, tiled=True)]
    pallas_call x1 -> x3, Pallas kernels: 13.8 us -> 13.3 us  [the longest x2 12 us: attend(): pl.pallas_call(functools.partial(attend_kernel, 256, whose), in_specs=[vm...]
  transfers between devices with their start and end apart: 8 -> 9, of which waited for: 5 -> 5; matrix products, arithmetic and copies ran while one was open for 0% -> 0% of each run, Pallas kernels for 1% -> 7%
where the time goes in v3:
time: 107 us; the launch traced here: 106 us
  starting transfers between devices  40.5 us (38%)
  blocking collectives  24.8 us (23%)
  waiting for transfers between devices  23.4 us (22%)
  Pallas kernels  17.2 us (16%)
    all_to_all x1, blocking collectives, exchange(): return lax.all_to_all(x, axis, 0, 0, tiled=True)  24.8 us
    all_to_all x3, starting transfers between devices, exchange(): return lax.all_to_all(x, axis, 0, 0, tiled=True)  23.2 us
    all_to_all x3, waiting for transfers between devices, exchange(): return lax.all_to_all(x, axis, 0, 0, tiled=True)  20 us
    pallas_call x2, Pallas kernels, attend(): pl.pallas_call(functools.partial(attend_kernel, 256, whose), in_specs=[vm...  12 us
    ppermute x1, starting transfers between devices, shards(): w_core = lax.ppermute(out_weight, 'c', SWAP)  5.65 us
    ppermute x1, starting transfers between devices, shards(): w_chip = lax.ppermute(out_weight, 'zl', SWAP)  3.02 us
    ppermute x1, starting transfers between devices, shards(): k_other = lax.ppermute(keys, 'c', SWAP)  2.86 us
  transfers between devices with their start and end apart: 9, of which 5 were waited for; matrix products, arithmetic and copies ran while one was open for 0% of the time, Pallas kernels for 7%

profile of v3, /device:TPU:1, one launch (start us, length us, event | category | flops | bytes accessed | tf_op | source)
XLA Modules:
  0.0 106.1 jit_solution(17638420152046825265)
XLA Ops:
  0.0 1.7 %pack.1 = bf16[256,1152]{1,0:T(8,128)(2,1)} custom-call(bf16[8,1024]{1,0:T(8,128)(2,1)} %q_ref.1, s32[8]{0:T(128)} %cut_ref.1), custom_call_target="tpu_custom_call" | custom-call | tf_op jit(solution)/shard_map/pack/pallas_call | solution.py:208
  1.7 0.0 copy-start.1
  1.7 0.0 copy-start.2
  1.7 13.6 %all-to-all-start = ((bf16[32,8,1152]{2,1,0:T(8,128)(2,1)}), bf16[32,8,1152]{2,1,0:T(8,128)(2,1)S(1)}, u32[]{:S(2)}, u32[]{:S(2)}) async-start(bf16[32,8,1152]{2,1,0:T(8,128)(2,1)} %bitcast.14), calls=%async_computation | async-start | bytes 1179648 | tf_op jit(solution)/shard_map/all_to_all | solution.py:300
  15.3 0.0 copy-done.1
  15.3 2.9 %collective-permute-start = (bf16[2048,128]{1,0:T(8,128)(2,1)S(1)}, bf16[2048,128]{1,0:T(8,128)(2,1)S(1)}, u32[]{:S(2)}, u32[]{:S(2)}) collective-permute-start(bf16[2048,128]{1,0:T(8,128)(2,1)S(1)} %copy-done.1), channel_id=1, source_target_pairs={{0,8},{8,0},{1,9},{9,1},{2,10},{10,2},{3,11},{11,3},{4,12},{12,4},... | collective-permute-start | bytes 1572872 | tf_op jit(solution)/shard_map/ppermute | solution.py:305
  18.2 0.0 copy-done.2
  18.2 1.9 %collective-permute-start.1 = (bf16[2048,128]{1,0:T(8,128)(2,1)S(1)}, bf16[2048,128]{1,0:T(8,128)(2,1)S(1)}, u32[]{:S(2)}, u32[]{:S(2)}) collective-permute-start(bf16[2048,128]{1,0:T(8,128)(2,1)S(1)} %copy-done.2), channel_id=1, source_target_pairs={{0,8},{8,0},{1,9},{9,1},{2,10},{10,2},{3,11},{11,3},{4,12},{12,4},... | collective-permute-start | bytes 1572872 | tf_op jit(solution)/shard_map/ppermute | solution.py:306
  20.1 0.0 collective-permute-done.k_other
  20.1 1.9 %collective-permute-done.1.v_other = bf16[2048,128]{1,0:T(8,128)(2,1)S(1)} collective-permute-done((bf16[2048,128]{1,0:T(8,128)(2,1)S(1)}, bf16[2048,128]{1,0:T(8,128)(2,1)S(1)}, u32[]{:S(2)}, u32[]{:S(2)}) %collective-permute-start.1) | collective-permute-done | bytes 524320 | tf_op jit(solution)/shard_map/ppermute | solution.py:306
  22.0 10.5 %all-to-all-done = bf16[32,8,1152]{2,1,0:T(8,128)(2,1)S(1)} async-done(((bf16[32,8,1152]{2,1,0:T(8,128)(2,1)}), bf16[32,8,1152]{2,1,0:T(8,128)(2,1)S(1)}, u32[]{:S(2)}, u32[]{:S(2)}) %all-to-all-start) | async-done | bytes 589856 | tf_op jit(solution)/shard_map/all_to_all | solution.py:300
  32.5 5.9 %attend.3 = bf16[128,1152]{1,0:T(8,128)(2,1)S(1)} custom-call(bf16[256,1152]{1,0:T(8,128)(2,1)S(1)} %bitcast.10, bf16[2048,128]{1,0:T(8,128)(2,1)S(1)} %copy-done.1, bf16[2048,128]{1,0:T(8,128)(2,1)S(1)} %copy-done.2, bf16[2048,128]{1,0:T(8,128)(2,1)S(1)} %collective-permute-done.k_other, bf16[2048,128]{1,0:T(8,128)(2,1)S(1)} %collective-permute-done.1.v_other), custom_call_target="tpu_custom_call" | custom-call | flops 4294967296 | bytes 2097152 | tf_op jit(solution)/shard_map/attend/pallas_call | solution.py:136
  38.4 1.9 %collective-permute-start.2 = (bf16[128,1152]{1,0:T(8,128)(2,1)S(1)}, bf16[128,1152]{1,0:T(8,128)(2,1)S(1)}, u32[]{:S(2)}, u32[]{:S(2)}) collective-permute-start(bf16[128,1152]{1,0:T(8,128)(2,1)S(1)} %attend.3), channel_id=1, source_target_pairs={{0,16},{16,0},{1,17},{17,1},{2,18},{18,2},{3,19},{19,3},{4,20},{20... | collective-permute-start | bytes 884744 | tf_op jit(solution)/shard_map/ppermute | solution.py:309
  40.3 6.1 %attend.2.a_ref = bf16[128,1152]{1,0:T(8,128)(2,1)S(1)} custom-call(bf16[256,1152]{1,0:T(8,128)(2,1)S(1)} %bitcast.11, bf16[2048,128]{1,0:T(8,128)(2,1)S(1)} %copy-done.1, bf16[2048,128]{1,0:T(8,128)(2,1)S(1)} %copy-done.2, bf16[2048,128]{1,0:T(8,128)(2,1)S(1)} %collective-permute-done.k_other, bf16[2048,128]{1,0:T(8,128)(2,1)S(1)} %collective-permute-done.1.v_other), custom_call_target="tpu_custom_call" | custom-call | flops 4294967296 | bytes 2097152 | tf_op jit(solution)/shard_map/attend/pallas_call | solution.py:136
  46.4 0.0 collective-permute-done.2.b_ref
  46.4 1.4 %merge.1 = bf16[128,1152]{1,0:T(8,128)(2,1)} custom-call(bf16[128,1152]{1,0:T(8,128)(2,1)S(1)} %attend.2.a_ref, bf16[128,1152]{1,0:T(8,128)(2,1)S(1)} %collective-permute-done.2.b_ref), custom_call_target="tpu_custom_call" | custom-call | tf_op jit(solution)/shard_map/merge/pallas_call | solution.py:179
  47.8 0.0 copy-start
  47.8 6.1 %all-to-all-start.1 = ((bf16[16,8,1152]{2,1,0:T(8,128)(2,1)}), bf16[16,8,1152]{2,1,0:T(8,128)(2,1)S(1)}, u32[]{:S(2)}, u32[]{:S(2)}) async-start(bf16[16,8,1152]{2,1,0:T(8,128)(2,1)} %bitcast.2), calls=%async_computation.1 | async-start | bytes 589824 | tf_op jit(solution)/shard_map/all_to_all | solution.py:300
  53.9 0.0 copy-done
  53.9 3.0 %collective-permute-start.4 = (bf16[1024,128]{1,0:T(8,128)(2,1)S(1)}, bf16[1024,128]{1,0:T(8,128)(2,1)S(1)}, u32[]{:S(2)}, u32[]{:S(2)}) collective-permute-start(bf16[1024,128]{1,0:T(8,128)(2,1)S(1)} %copy-done), channel_id=1, source_target_pairs={{0,16},{16,0},{1,17},{17,1},{2,18},{18,2},{3,19},{19,3},{4,20},{20... | collective-permute-start | bytes 786440 | tf_op jit(solution)/shard_map/ppermute | solution.py:312
  57.0 8.0 %all-to-all-done.1 = bf16[16,8,1152]{2,1,0:T(8,128)(2,1)S(1)} async-done(((bf16[16,8,1152]{2,1,0:T(8,128)(2,1)}), bf16[16,8,1152]{2,1,0:T(8,128)(2,1)S(1)}, u32[]{:S(2)}, u32[]{:S(2)}) %all-to-all-start.1) | async-done | bytes 294944 | tf_op jit(solution)/shard_map/all_to_all | solution.py:300
  65.0 1.1 %combine.1 = bf16[128,1024]{1,0:T(8,128)(2,1)} custom-call(bf16[128,1152]{1,0:T(8,128)(2,1)S(1)} %bitcast.8), custom_call_target="tpu_custom_call" | custom-call | tf_op jit(solution)/shard_map/combine/pallas_call | solution.py:242
  66.1 3.5 %all-to-all-start.2 = ((bf16[16,8,1024]{2,1,0:T(8,128)(2,1)}), bf16[16,8,1024]{2,1,0:T(8,128)(2,1)S(1)}, u32[]{:S(2)}, u32[]{:S(2)}) async-start(bf16[16,8,1024]{2,1,0:T(8,128)(2,1)} %bitcast.4), calls=%async_computation.2 | async-start | bytes 524288 | tf_op jit(solution)/shard_map/all_to_all | solution.py:300
  69.6 5.6 %collective-permute-start.3 = (bf16[1024,128]{1,0:T(8,128)(2,1)S(1)}, bf16[1024,128]{1,0:T(8,128)(2,1)S(1)}, u32[]{:S(2)}, u32[]{:S(2)}) collective-permute-start(bf16[1024,128]{1,0:T(8,128)(2,1)S(1)} %copy-done), channel_id=1, source_target_pairs={{0,8},{8,0},{1,9},{9,1},{2,10},{10,2},{3,11},{11,3},{4,12},{12,4},... | collective-permute-start | bytes 786440 | tf_op jit(solution)/shard_map/ppermute | solution.py:311
  75.3 0.0 collective-permute-done.4.w_chip
  75.3 1.9 %collective-permute-start.5 = (bf16[1024,128]{1,0:T(8,128)(2,1)S(1)}, bf16[1024,128]{1,0:T(8,128)(2,1)S(1)}, u32[]{:S(2)}, u32[]{:S(2)}) collective-permute-start(bf16[1024,128]{1,0:T(8,128)(2,1)S(1)} %collective-permute-done.4.w_chip), channel_id=1, source_target_pairs={{0,8},{8,0},{1,9},{9,1},{2,10},{10,2},{3,11},{11,3},{4,12},{12,4},... | collective-permute-start | bytes 786440 | tf_op jit(solution)/shard_map/ppermute | solution.py:313
  77.2 0.0 collective-permute-done.3.w_core
  77.2 1.5 %collective-permute-done.5.w_both = bf16[1024,128]{1,0:T(8,128)(2,1)S(1)} collective-permute-done((bf16[1024,128]{1,0:T(8,128)(2,1)S(1)}, bf16[1024,128]{1,0:T(8,128)(2,1)S(1)}, u32[]{:S(2)}, u32[]{:S(2)}) %collective-permute-start.5) | collective-permute-done | bytes 262176 | tf_op jit(solution)/shard_map/ppermute | solution.py:313
  78.7 1.4 %all-to-all-done.2 = bf16[16,8,1024]{2,1,0:T(8,128)(2,1)S(1)} async-done(((bf16[16,8,1024]{2,1,0:T(8,128)(2,1)}), bf16[16,8,1024]{2,1,0:T(8,128)(2,1)S(1)}, u32[]{:S(2)}, u32[]{:S(2)}) %all-to-all-start.2) | async-done | bytes 262176 | tf_op jit(solution)/shard_map/all_to_all | solution.py:300
  80.2 0.4 project.1
  80.6 24.8 %all_to_all.44 = bf16[32,16,128]{2,1,0:T(8,128)(2,1)S(1)} all-to-all(bf16[32,16,128]{2,1,0:T(8,128)(2,1)S(1)} %bitcast.13), channel_id=1, replica_groups=mesh['y'=8,'zh'=2,'zl'=2,'c'=2,'w'=2,'x'=4] {'zl','c','w','x'}, dimensions={0} | all-to-all | bytes 262144 | tf_op jit(solution)/shard_map/all_to_all | solution.py:300
  105.4 0.6 total.1
Async XLA Ops:
  1.7 13.6 %copy-start.1 = (bf16[2048,128]{1,0:T(8,128)(2,1)S(1)}, bf16[2048,128]{1,0:T(8,128)(2,1)}, u32[]{:S(2)}) copy-start(bf16[2048,128]{1,0:T(8,128)(2,1)} %k_mine.3) | copy-start | bytes 1572868
  1.7 16.5 %copy-start.2 = (bf16[2048,128]{1,0:T(8,128)(2,1)S(1)}, bf16[2048,128]{1,0:T(8,128)(2,1)}, u32[]{:S(2)}) copy-start(bf16[2048,128]{1,0:T(8,128)(2,1)} %v_mine.3) | copy-start | bytes 1572868
  1.7 30.8 %all-to-all-start = ((bf16[32,8,1152]{2,1,0:T(8,128)(2,1)}), bf16[32,8,1152]{2,1,0:T(8,128)(2,1)S(1)}, u32[]{:S(2)}, u32[]{:S(2)}) async-start(bf16[32,8,1152]{2,1,0:T(8,128)(2,1)} %bitcast.14), calls=%async_computation | async-start | bytes 1179648 | tf_op jit(solution)/shard_map/all_to_all | solution.py:300
  15.3 4.8 %collective-permute-start = (bf16[2048,128]{1,0:T(8,128)(2,1)S(1)}, bf16[2048,128]{1,0:T(8,128)(2,1)S(1)}, u32[]{:S(2)}, u32[]{:S(2)}) collective-permute-start(bf16[2048,128]{1,0:T(8,128)(2,1)S(1)} %copy-done.1), channel_id=1, source_target_pairs={{0,8},{8,0},{1,9},{9,1},{2,10},{10,2},{3,11},{11,3},{4,12},{12,4},... | collective-permute-start | bytes 1572872 | tf_op jit(solution)/shard_map/ppermute | solution.py:305
  18.2 3.8 %collective-permute-start.1 = (bf16[2048,128]{1,0:T(8,128)(2,1)S(1)}, bf16[2048,128]{1,0:T(8,128)(2,1)S(1)}, u32[]{:S(2)}, u32[]{:S(2)}) collective-permute-start(bf16[2048,128]{1,0:T(8,128)(2,1)S(1)} %copy-done.2), channel_id=1, source_target_pairs={{0,8},{8,0},{1,9},{9,1},{2,10},{10,2},{3,11},{11,3},{4,12},{12,4},... | collective-permute-start | bytes 1572872 | tf_op jit(solution)/shard_map/ppermute | solution.py:306
  38.4 8.0 %collective-permute-start.2 = (bf16[128,1152]{1,0:T(8,128)(2,1)S(1)}, bf16[128,1152]{1,0:T(8,128)(2,1)S(1)}, u32[]{:S(2)}, u32[]{:S(2)}) collective-permute-start(bf16[128,1152]{1,0:T(8,128)(2,1)S(1)} %attend.3), channel_id=1, source_target_pairs={{0,16},{16,0},{1,17},{17,1},{2,18},{18,2},{3,19},{19,3},{4,20},{20... | collective-permute-start | bytes 884744 | tf_op jit(solution)/shard_map/ppermute | solution.py:309
  47.8 6.1 %copy-start = (bf16[1024,128]{1,0:T(8,128)(2,1)S(1)}, bf16[1024,128]{1,0:T(8,128)(2,1)}, u32[]{:S(2)}) copy-start(bf16[1024,128]{1,0:T(8,128)(2,1)} %w_ref.1) | copy-start | bytes 786436
  47.8 17.2 %all-to-all-start.1 = ((bf16[16,8,1152]{2,1,0:T(8,128)(2,1)}), bf16[16,8,1152]{2,1,0:T(8,128)(2,1)S(1)}, u32[]{:S(2)}, u32[]{:S(2)}) async-start(bf16[16,8,1152]{2,1,0:T(8,128)(2,1)} %bitcast.2), calls=%async_computation.1 | async-start | bytes 589824 | tf_op jit(solution)/shard_map/all_to_all | solution.py:300
  53.9 21.4 %collective-permute-start.4 = (bf16[1024,128]{1,0:T(8,128)(2,1)S(1)}, bf16[1024,128]{1,0:T(8,128)(2,1)S(1)}, u32[]{:S(2)}, u32[]{:S(2)}) collective-permute-start(bf16[1024,128]{1,0:T(8,128)(2,1)S(1)} %copy-done), channel_id=1, source_target_pairs={{0,16},{16,0},{1,17},{17,1},{2,18},{18,2},{3,19},{19,3},{4,20},{20... | collective-permute-start | bytes 786440 | tf_op jit(solution)/shard_map/ppermute | solution.py:312
  66.1 14.1 %all-to-all-start.2 = ((bf16[16,8,1024]{2,1,0:T(8,128)(2,1)}), bf16[16,8,1024]{2,1,0:T(8,128)(2,1)S(1)}, u32[]{:S(2)}, u32[]{:S(2)}) async-start(bf16[16,8,1024]{2,1,0:T(8,128)(2,1)} %bitcast.4), calls=%async_computation.2 | async-start | bytes 524288 | tf_op jit(solution)/shard_map/all_to_all | solution.py:300
  69.6 7.6 %collective-permute-start.3 = (bf16[1024,128]{1,0:T(8,128)(2,1)S(1)}, bf16[1024,128]{1,0:T(8,128)(2,1)S(1)}, u32[]{:S(2)}, u32[]{:S(2)}) collective-permute-start(bf16[1024,128]{1,0:T(8,128)(2,1)S(1)} %copy-done), channel_id=1, source_target_pairs={{0,8},{8,0},{1,9},{9,1},{2,10},{10,2},{3,11},{11,3},{4,12},{12,4},... | collective-permute-start | bytes 786440 | tf_op jit(solution)/shard_map/ppermute | solution.py:311
  75.3 3.4 %collective-permute-start.5 = (bf16[1024,128]{1,0:T(8,128)(2,1)S(1)}, bf16[1024,128]{1,0:T(8,128)(2,1)S(1)}, u32[]{:S(2)}, u32[]{:S(2)}) collective-permute-start(bf16[1024,128]{1,0:T(8,128)(2,1)S(1)} %collective-permute-done.4.w_chip), channel_id=1, source_target_pairs={{0,8},{8,0},{1,9},{9,1},{2,10},{10,2},{3,11},{11,3},{4,12},{12,4},... | collective-permute-start | bytes 786440 | tf_op jit(solution)/shard_map/ppermute | solution.py:313

commit v4 on v3

--- a/solution.py
+++ b/solution.py
@@ -18,8 +18,7 @@
 FLOOR = -1e20
 SCALE = math.log2(math.e) / math.sqrt(HEAD_DIM)
 ROW_BLOCK = 64
-PROBE = 128
-LEAP = 400.0
+REACH = 470.0
 VMEM = 24 * 2**20
 SMALL = 8 * 2**20
 
@@ -69,19 +68,18 @@
         places = lax.broadcasted_iota(jnp.int32, (many, size), 1)
         return jnp.where(places < cut - (starts[n] + at), scores, NEG)
 
-    def weighed(acc, scores, level, n, at, size):
-        weights = jnp.exp2(scores * SCALE - level * SCALE).astype(jnp.bfloat16)
+    def weighed(acc, weights, n, at, size):
         wide = [pairs[n][1][at : at + size, :], jnp.ones((size, LANES), jnp.bfloat16)]
         wide = jnp.concatenate(wide, axis=1)
+        weights = weights.astype(jnp.bfloat16)
         return acc + jnp.dot(weights, wide, preferred_element_type=jnp.float32)
 
-    def store(i, level, acc):
-        level = jnp.broadcast_to(level, (many, LANES))
+    def store(i, acc, level=0.0):
         here = pl.ds(pl.multiple_of(i * ROW_BLOCK, ROW_BLOCK), ROW_BLOCK)
         total = acc[:, HEAD_DIM:]
         some = jnp.maximum(total, 1e-30)
         mixed = (acc[:, :HEAD_DIM] / some).astype(jnp.bfloat16)
-        level = jnp.where(total > 0.0, level * SCALE + jnp.log2(some), NEG)
+        level = jnp.where(total > 0.0, jnp.log2(some) + level * SCALE, NEG)
         high, middle, low = split(level)
         lane = lax.broadcasted_iota(jnp.int32, (ROW_BLOCK, LANES), 1)
         stats = jnp.zeros((ROW_BLOCK, LANES), jnp.float32)
@@ -92,27 +90,25 @@
             stats = jnp.where((lane & 7) == h, part, stats)
         o_ref[here, WIDTH:] = jnp.where(lane < 24, stats, 0.0).astype(jnp.bfloat16)
 
-    def quick(i, leap):
+    def quick(i, unsafe):
         queries, cut = load(i)
         acc = jnp.zeros((many, HEAD_DIM + LANES), jnp.float32)
-        level = jnp.full((many, 1), FLOOR, jnp.float32)
-        for n in range(len(pairs)):
-            probe = scores_of(queries, cut, n, 0, PROBE)
-            level = jnp.maximum(level, jnp.max(probe, axis=1, keepdims=True))
-        most = jnp.full((many, LANES), FLOOR, jnp.float32)
+        most = jnp.full((many, LANES), NEG, jnp.float32)
         for n in range(len(pairs)):
             for at in range(0, length, chunk):
                 scores = scores_of(queries, cut, n, at, chunk)
                 for t in range(0, chunk, LANES):
                     most = jnp.maximum(most, scores[:, t : t + LANES])
-                acc = weighed(acc, scores, level, n, at, chunk)
-        store(i, level, acc)
-        return jnp.maximum(leap, most - level)
-
-    leap = jnp.full((many, LANES), FLOOR, jnp.float32)
-    leap = lax.fori_loop(0, rows // ROW_BLOCK, quick, leap)
-
-    @pl.when(jnp.max(leap) > LEAP)
+                acc = weighed(acc, jnp.exp2(scores * SCALE), n, at, chunk)
+        store(i, acc)
+        most = jnp.max(most, axis=1, keepdims=True)
+        far = jnp.where(most > FLOOR, jnp.abs(most), 0.0)
+        return jnp.maximum(unsafe, far)
+
+    unsafe = jnp.zeros((many, 1), jnp.float32)
+    unsafe = lax.fori_loop(0, rows // ROW_BLOCK, quick, unsafe)
+
+    @pl.when(jnp.logical_not(jnp.max(unsafe) < REACH))
     def _():
         def exact(i, unused):
             queries, cut = load(i)
@@ -121,9 +117,10 @@
             for n in range(len(pairs)):
                 scores = scores_of(queries, cut, n, 0, length)
                 higher = jnp.maximum(level, jnp.max(scores, axis=1, keepdims=True))
-                acc = weighed(acc * jnp.exp2((level - higher) * SCALE), scores, higher, n, 0, length)
+                acc = acc * jnp.exp2((level - higher) * SCALE)
+                acc = weighed(acc, jnp.exp2(scores * SCALE - higher * SCALE), n, 0, length)
                 level = higher
-            store(i, level, acc)
+            store(i, acc, level)
             return unused
 
         lax.fori_loop(0, rows // ROW_BLOCK, exact, 0)

time: 107 us -> 121 us (1.13)
  starting transfers between devices: 40.5 us -> 56.6 us
  waiting for transfers between devices: 23.4 us -> 21.7 us
  blocking collectives: 24.8 us -> 26.2 us
    ppermute x1, starting transfers between devices: 5.65 us -> 21.2 us  [shards(): w_core = lax.ppermute(out_weight, 'c', SWAP)]
    all_to_all x3, waiting for transfers between devices: 20 us -> 18.3 us  [exchange(): return lax.all_to_all(x, axis, 0, 0, tiled=True)]
    all_to_all x1, blocking collectives: 24.8 us -> 26.2 us  [exchange(): return lax.all_to_all(x, axis, 0, 0, tiled=True)]
  transfers between devices with their start and end apart: 9 -> 9, of which waited for: 5 -> 4; matrix products, arithmetic and copies ran while one was open for 0% -> 0% of each run, Pallas kernels for 7% -> 6%
where the time goes in v4:
time: 121 us
  starting transfers between devices  56.6 us (47%)
  blocking collectives  26.2 us (22%)
  waiting for transfers between devices  21.7 us (18%)
  Pallas kernels  16.1 us (13%)
    all_to_all x1, blocking collectives, exchange(): return lax.all_to_all(x, axis, 0, 0, tiled=True)  26.2 us
    all_to_all x3, starting transfers between devices, exchange(): return lax.all_to_all(x, axis, 0, 0, tiled=True)  23.8 us
    ppermute x1, starting transfers between devices, shards(): w_core = lax.ppermute(out_weight, 'c', SWAP)  21.2 us
    all_to_all x3, waiting for transfers between devices, exchange(): return lax.all_to_all(x, axis, 0, 0, tiled=True)  18.3 us
    pallas_call x2, Pallas kernels, attend(): pl.pallas_call(functools.partial(attend_kernel, 256, whose), in_specs=[vm...  10.8 us
    ppermute x1, starting transfers between devices, shards(): w_chip = lax.ppermute(out_weight, 'zl', SWAP)  3.03 us
    ppermute x1, starting transfers between devices, shards(): k_other = lax.ppermute(keys, 'c', SWAP)  2.86 us
  transfers between devices with their start and end apart: 9, of which 4 were waited for; matrix products, arithmetic and copies ran while one was open for 0% of the time, Pallas kernels for 6%

profile of v4, /device:TPU:1, one launch (start us, length us, event | category | flops | bytes accessed | tf_op | source)
XLA Modules:
  0.0 120.8 jit_solution(7708715947377904092)
XLA Ops:
  0.0 1.7 %pack.1 = bf16[256,1152]{1,0:T(8,128)(2,1)} custom-call(bf16[8,1024]{1,0:T(8,128)(2,1)} %q_ref.1, s32[8]{0:T(128)} %cut_ref.1), custom_call_target="tpu_custom_call" | custom-call | tf_op jit(solution)/shard_map/pack/pallas_call | solution.py:205
  1.7 0.0 copy-start.1
  1.7 0.0 copy-start.2
  1.7 13.6 %all-to-all-start = ((bf16[32,8,1152]{2,1,0:T(8,128)(2,1)}), bf16[32,8,1152]{2,1,0:T(8,128)(2,1)S(1)}, u32[]{:S(2)}, u32[]{:S(2)}) async-start(bf16[32,8,1152]{2,1,0:T(8,128)(2,1)} %bitcast.14), calls=%async_computation | async-start | bytes 1179648 | tf_op jit(solution)/shard_map/all_to_all | solution.py:297
  15.3 0.0 copy-done.1
  15.3 2.9 %collective-permute-start = (bf16[2048,128]{1,0:T(8,128)(2,1)S(1)}, bf16[2048,128]{1,0:T(8,128)(2,1)S(1)}, u32[]{:S(2)}, u32[]{:S(2)}) collective-permute-start(bf16[2048,128]{1,0:T(8,128)(2,1)S(1)} %copy-done.1), channel_id=1, source_target_pairs={{0,8},{8,0},{1,9},{9,1},{2,10},{10,2},{3,11},{11,3},{4,12},{12,4},... | collective-permute-start | bytes 1572872 | tf_op jit(solution)/shard_map/ppermute | solution.py:302
  18.2 0.0 copy-done.2
  18.2 1.9 %collective-permute-start.1 = (bf16[2048,128]{1,0:T(8,128)(2,1)S(1)}, bf16[2048,128]{1,0:T(8,128)(2,1)S(1)}, u32[]{:S(2)}, u32[]{:S(2)}) collective-permute-start(bf16[2048,128]{1,0:T(8,128)(2,1)S(1)} %copy-done.2), channel_id=1, source_target_pairs={{0,8},{8,0},{1,9},{9,1},{2,10},{10,2},{3,11},{11,3},{4,12},{12,4},... | collective-permute-start | bytes 1572872 | tf_op jit(solution)/shard_map/ppermute | solution.py:303
  20.1 0.0 collective-permute-done.k_other
  20.1 1.9 %collective-permute-done.1.v_other = bf16[2048,128]{1,0:T(8,128)(2,1)S(1)} collective-permute-done((bf16[2048,128]{1,0:T(8,128)(2,1)S(1)}, bf16[2048,128]{1,0:T(8,128)(2,1)S(1)}, u32[]{:S(2)}, u32[]{:S(2)}) %collective-permute-start.1) | collective-permute-done | bytes 524320 | tf_op jit(solution)/shard_map/ppermute | solution.py:303
  22.0 10.5 %all-to-all-done = bf16[32,8,1152]{2,1,0:T(8,128)(2,1)S(1)} async-done(((bf16[32,8,1152]{2,1,0:T(8,128)(2,1)}), bf16[32,8,1152]{2,1,0:T(8,128)(2,1)S(1)}, u32[]{:S(2)}, u32[]{:S(2)}) %all-to-all-start) | async-done | bytes 589856 | tf_op jit(solution)/shard_map/all_to_all | solution.py:297
  32.5 5.3 %attend.3 = bf16[128,1152]{1,0:T(8,128)(2,1)S(1)} custom-call(bf16[256,1152]{1,0:T(8,128)(2,1)S(1)} %bitcast.10, bf16[2048,128]{1,0:T(8,128)(2,1)S(1)} %copy-done.1, bf16[2048,128]{1,0:T(8,128)(2,1)S(1)} %copy-done.2, bf16[2048,128]{1,0:T(8,128)(2,1)S(1)} %collective-permute-done.k_other, bf16[2048,128]{1,0:T(8,128)(2,1)S(1)} %collective-permute-done.1.v_other), custom_call_target="tpu_custom_call" | custom-call | flops 4294967296 | bytes 2097152 | tf_op jit(solution)/shard_map/attend/pallas_call | solution.py:133
  37.8 1.9 %collective-permute-start.2 = (bf16[128,1152]{1,0:T(8,128)(2,1)S(1)}, bf16[128,1152]{1,0:T(8,128)(2,1)S(1)}, u32[]{:S(2)}, u32[]{:S(2)}) collective-permute-start(bf16[128,1152]{1,0:T(8,128)(2,1)S(1)} %attend.3), channel_id=1, source_target_pairs={{0,16},{16,0},{1,17},{17,1},{2,18},{18,2},{3,19},{19,3},{4,20},{20... | collective-permute-start | bytes 884744 | tf_op jit(solution)/shard_map/ppermute | solution.py:306
  39.8 5.5 %attend.2.a_ref = bf16[128,1152]{1,0:T(8,128)(2,1)S(1)} custom-call(bf16[256,1152]{1,0:T(8,128)(2,1)S(1)} %bitcast.11, bf16[2048,128]{1,0:T(8,128)(2,1)S(1)} %copy-done.1, bf16[2048,128]{1,0:T(8,128)(2,1)S(1)} %copy-done.2, bf16[2048,128]{1,0:T(8,128)(2,1)S(1)} %collective-permute-done.k_other, bf16[2048,128]{1,0:T(8,128)(2,1)S(1)} %collective-permute-done.1.v_other), custom_call_target="tpu_custom_call" | custom-call | flops 4294967296 | bytes 2097152 | tf_op jit(solution)/shard_map/attend/pallas_call | solution.py:133
  45.3 0.0 collective-permute-done.2.b_ref
  45.3 1.4 %merge.1 = bf16[128,1152]{1,0:T(8,128)(2,1)} custom-call(bf16[128,1152]{1,0:T(8,128)(2,1)S(1)} %attend.2.a_ref, bf16[128,1152]{1,0:T(8,128)(2,1)S(1)} %collective-permute-done.2.b_ref), custom_call_target="tpu_custom_call" | custom-call | tf_op jit(solution)/shard_map/merge/pallas_call | solution.py:176
  46.7 0.0 copy-start
  46.7 6.7 %all-to-all-start.1 = ((bf16[16,8,1152]{2,1,0:T(8,128)(2,1)}), bf16[16,8,1152]{2,1,0:T(8,128)(2,1)S(1)}, u32[]{:S(2)}, u32[]{:S(2)}) async-start(bf16[16,8,1152]{2,1,0:T(8,128)(2,1)} %bitcast.2), calls=%async_computation.1 | async-start | bytes 589824 | tf_op jit(solution)/shard_map/all_to_all | solution.py:297
  53.4 0.0 copy-done
  53.4 3.0 %collective-permute-start.4 = (bf16[1024,128]{1,0:T(8,128)(2,1)S(1)}, bf16[1024,128]{1,0:T(8,128)(2,1)S(1)}, u32[]{:S(2)}, u32[]{:S(2)}) collective-permute-start(bf16[1024,128]{1,0:T(8,128)(2,1)S(1)} %copy-done), channel_id=1, source_target_pairs={{0,16},{16,0},{1,17},{17,1},{2,18},{18,2},{3,19},{19,3},{4,20},{20... | collective-permute-start | bytes 786440 | tf_op jit(solution)/shard_map/ppermute | solution.py:309
  56.4 7.7 %all-to-all-done.1 = bf16[16,8,1152]{2,1,0:T(8,128)(2,1)S(1)} async-done(((bf16[16,8,1152]{2,1,0:T(8,128)(2,1)}), bf16[16,8,1152]{2,1,0:T(8,128)(2,1)S(1)}, u32[]{:S(2)}, u32[]{:S(2)}) %all-to-all-start.1) | async-done | bytes 294944 | tf_op jit(solution)/shard_map/all_to_all | solution.py:297
  64.1 1.1 combine.1
  65.3 3.5 %all-to-all-start.2 = ((bf16[16,8,1024]{2,1,0:T(8,128)(2,1)}), bf16[16,8,1024]{2,1,0:T(8,128)(2,1)S(1)}, u32[]{:S(2)}, u32[]{:S(2)}) async-start(bf16[16,8,1024]{2,1,0:T(8,128)(2,1)} %bitcast.4), calls=%async_computation.2 | async-start | bytes 524288 | tf_op jit(solution)/shard_map/all_to_all | solution.py:297
  68.8 21.2 %collective-permute-start.3 = (bf16[1024,128]{1,0:T(8,128)(2,1)S(1)}, bf16[1024,128]{1,0:T(8,128)(2,1)S(1)}, u32[]{:S(2)}, u32[]{:S(2)}) collective-permute-start(bf16[1024,128]{1,0:T(8,128)(2,1)S(1)} %copy-done), channel_id=1, source_target_pairs={{0,8},{8,0},{1,9},{9,1},{2,10},{10,2},{3,11},{11,3},{4,12},{12,4},... | collective-permute-start | bytes 786440 | tf_op jit(solution)/shard_map/ppermute | solution.py:308
  90.0 0.0 collective-permute-done.4.w_chip
  90.1 1.9 %collective-permute-start.5 = (bf16[1024,128]{1,0:T(8,128)(2,1)S(1)}, bf16[1024,128]{1,0:T(8,128)(2,1)S(1)}, u32[]{:S(2)}, u32[]{:S(2)}) collective-permute-start(bf16[1024,128]{1,0:T(8,128)(2,1)S(1)} %collective-permute-done.4.w_chip), channel_id=1, source_target_pairs={{0,8},{8,0},{1,9},{9,1},{2,10},{10,2},{3,11},{11,3},{4,12},{12,4},... | collective-permute-start | bytes 786440 | tf_op jit(solution)/shard_map/ppermute | solution.py:310
  92.0 0.0 collective-permute-done.3.w_core
  92.0 1.5 %collective-permute-done.5.w_both = bf16[1024,128]{1,0:T(8,128)(2,1)S(1)} collective-permute-done((bf16[1024,128]{1,0:T(8,128)(2,1)S(1)}, bf16[1024,128]{1,0:T(8,128)(2,1)S(1)}, u32[]{:S(2)}, u32[]{:S(2)}) %collective-permute-start.5) | collective-permute-done | bytes 262176 | tf_op jit(solution)/shard_map/ppermute | solution.py:310
  93.5 0.0 all-to-all-done.2
  93.5 0.4 project.1
  93.9 26.2 %all_to_all.44 = bf16[32,16,128]{2,1,0:T(8,128)(2,1)S(1)} all-to-all(bf16[32,16,128]{2,1,0:T(8,128)(2,1)S(1)} %bitcast.13), channel_id=1, replica_groups=mesh['y'=8,'zh'=2,'zl'=2,'c'=2,'w'=2,'x'=4] {'zl','c','w','x'}, dimensions={0} | all-to-all | bytes 262144 | tf_op jit(solution)/shard_map/all_to_all | solution.py:297
  120.2 0.6 total.1
Async XLA Ops:
  1.7 13.6 %copy-start.1 = (bf16[2048,128]{1,0:T(8,128)(2,1)S(1)}, bf16[2048,128]{1,0:T(8,128)(2,1)}, u32[]{:S(2)}) copy-start(bf16[2048,128]{1,0:T(8,128)(2,1)} %k_mine.3) | copy-start | bytes 1572868
  1.7 16.5 %copy-start.2 = (bf16[2048,128]{1,0:T(8,128)(2,1)S(1)}, bf16[2048,128]{1,0:T(8,128)(2,1)}, u32[]{:S(2)}) copy-start(bf16[2048,128]{1,0:T(8,128)(2,1)} %v_mine.3) | copy-start | bytes 1572868
  1.7 30.8 %all-to-all-start = ((bf16[32,8,1152]{2,1,0:T(8,128)(2,1)}), bf16[32,8,1152]{2,1,0:T(8,128)(2,1)S(1)}, u32[]{:S(2)}, u32[]{:S(2)}) async-start(bf16[32,8,1152]{2,1,0:T(8,128)(2,1)} %bitcast.14), calls=%async_computation | async-start | bytes 1179648 | tf_op jit(solution)/shard_map/all_to_all | solution.py:297
  15.3 4.8 %collective-permute-start = (bf16[2048,128]{1,0:T(8,128)(2,1)S(1)}, bf16[2048,128]{1,0:T(8,128)(2,1)S(1)}, u32[]{:S(2)}, u32[]{:S(2)}) collective-permute-start(bf16[2048,128]{1,0:T(8,128)(2,1)S(1)} %copy-done.1), channel_id=1, source_target_pairs={{0,8},{8,0},{1,9},{9,1},{2,10},{10,2},{3,11},{11,3},{4,12},{12,4},... | collective-permute-start | bytes 1572872 | tf_op jit(solution)/shard_map/ppermute | solution.py:302
  18.2 3.8 %collective-permute-start.1 = (bf16[2048,128]{1,0:T(8,128)(2,1)S(1)}, bf16[2048,128]{1,0:T(8,128)(2,1)S(1)}, u32[]{:S(2)}, u32[]{:S(2)}) collective-permute-start(bf16[2048,128]{1,0:T(8,128)(2,1)S(1)} %copy-done.2), channel_id=1, source_target_pairs={{0,8},{8,0},{1,9},{9,1},{2,10},{10,2},{3,11},{11,3},{4,12},{12,4},... | collective-permute-start | bytes 1572872 | tf_op jit(solution)/shard_map/ppermute | solution.py:303
  37.8 7.5 %collective-permute-start.2 = (bf16[128,1152]{1,0:T(8,128)(2,1)S(1)}, bf16[128,1152]{1,0:T(8,128)(2,1)S(1)}, u32[]{:S(2)}, u32[]{:S(2)}) collective-permute-start(bf16[128,1152]{1,0:T(8,128)(2,1)S(1)} %attend.3), channel_id=1, source_target_pairs={{0,16},{16,0},{1,17},{17,1},{2,18},{18,2},{3,19},{19,3},{4,20},{20... | collective-permute-start | bytes 884744 | tf_op jit(solution)/shard_map/ppermute | solution.py:306
  46.7 6.7 %copy-start = (bf16[1024,128]{1,0:T(8,128)(2,1)S(1)}, bf16[1024,128]{1,0:T(8,128)(2,1)}, u32[]{:S(2)}) copy-start(bf16[1024,128]{1,0:T(8,128)(2,1)} %w_ref.1) | copy-start | bytes 786436
  46.7 17.5 %all-to-all-start.1 = ((bf16[16,8,1152]{2,1,0:T(8,128)(2,1)}), bf16[16,8,1152]{2,1,0:T(8,128)(2,1)S(1)}, u32[]{:S(2)}, u32[]{:S(2)}) async-start(bf16[16,8,1152]{2,1,0:T(8,128)(2,1)} %bitcast.2), calls=%async_computation.1 | async-start | bytes 589824 | tf_op jit(solution)/shard_map/all_to_all | solution.py:297
  53.4 36.7 %collective-permute-start.4 = (bf16[1024,128]{1,0:T(8,128)(2,1)S(1)}, bf16[1024,128]{1,0:T(8,128)(2,1)S(1)}, u32[]{:S(2)}, u32[]{:S(2)}) collective-permute-start(bf16[1024,128]{1,0:T(8,128)(2,1)S(1)} %copy-done), channel_id=1, source_target_pairs={{0,16},{16,0},{1,17},{17,1},{2,18},{18,2},{3,19},{19,3},{4,20},{20... | collective-permute-start | bytes 786440 | tf_op jit(solution)/shard_map/ppermute | solution.py:309
  65.3 28.2 %all-to-all-start.2 = ((bf16[16,8,1024]{2,1,0:T(8,128)(2,1)}), bf16[16,8,1024]{2,1,0:T(8,128)(2,1)S(1)}, u32[]{:S(2)}, u32[]{:S(2)}) async-start(bf16[16,8,1024]{2,1,0:T(8,128)(2,1)} %bitcast.4), calls=%async_computation.2 | async-start | bytes 524288 | tf_op jit(solution)/shard_map/all_to_all | solution.py:297
  68.8 23.2 %collective-permute-start.3 = (bf16[1024,128]{1,0:T(8,128)(2,1)S(1)}, bf16[1024,128]{1,0:T(8,128)(2,1)S(1)}, u32[]{:S(2)}, u32[]{:S(2)}) collective-permute-start(bf16[1024,128]{1,0:T(8,128)(2,1)S(1)} %copy-done), channel_id=1, source_target_pairs={{0,8},{8,0},{1,9},{9,1},{2,10},{10,2},{3,11},{11,3},{4,12},{12,4},... | collective-permute-start | bytes 786440 | tf_op jit(solution)/shard_map/ppermute | solution.py:308
  90.1 3.4 %collective-permute-start.5 = (bf16[1024,128]{1,0:T(8,128)(2,1)S(1)}, bf16[1024,128]{1,0:T(8,128)(2,1)S(1)}, u32[]{:S(2)}, u32[]{:S(2)}) collective-permute-start(bf16[1024,128]{1,0:T(8,128)(2,1)S(1)} %collective-permute-done.4.w_chip), channel_id=1, source_target_pairs={{0,8},{8,0},{1,9},{9,1},{2,10},{10,2},{3,11},{11,3},{4,12},{12,4},... | collective-permute-start | bytes 786440 | tf_op jit(solution)/shard_map/ppermute | solution.py:310

commit v5 on v4

--- a/solution.py
+++ b/solution.py
@@ -22,11 +22,12 @@
 VMEM = 24 * 2**20
 SMALL = 8 * 2**20
 
-AXES = ("y", "zh", "zl", "c", "w", "x")
-SIZES = (8, 2, 2, 2, 2, 4)
-BLK = ("y", "zh", "zl", "c")
+AXES = ("yc", "yb", "ya", "zh", "zl", "c", "w", "x")
+SIZES = (2, 2, 2, 2, 2, 2, 2, 4)
+BLK = ("yc", "yb", "ya", "zh", "zl", "c")
 HEAD = ("w", "x")
-FAR = ("y", "zh")
+QUERIES = ("zl", "yb", "yc", "ya", "zh")
+FAR = ("zh", "yc", "yb", "ya")
 NEAR = ("zl", "c")
 SWAP = ((0, 1), (1, 0))
 
@@ -44,7 +45,10 @@
     length = k_mine.shape[0]
     chip = lax.axis_index("zl")
     core = lax.axis_index("c")
-    me = lax.axis_index("y") * 8 + lax.axis_index("zh") * 4 + chip * 2
+    me = 0
+    for axis in ("yc", "yb", "ya", "zh"):
+        me = me * 2 + lax.axis_index(axis)
+    me = me * 4 + chip * 2
     starts = ((me + core) * length, (me + 1 - core) * length)
     base = (1 - chip if whose else chip) * rows
 
@@ -149,10 +153,18 @@
 
 
 def merge_kernel(a_ref, b_ref, o_ref):
-    rows = 64
+    rows = 32
     lane = lax.broadcasted_iota(jnp.int32, (rows, LANES), 1)
-    for at in range(0, o_ref.shape[0], rows):
-        here = slice(at, at + rows)
+    for n in range(o_ref.shape[0] // rows):
+        here = slice(n * rows, (n + 1) * rows)
+        yb, yc = n // 2, n % 2
+
+        def put(columns, block):
+            for zh in range(2):
+                at = ((zh * 2 + yc) * 2 + yb) * 16
+                pair = [block[8 * zh : 8 * zh + 8], block[16 + 8 * zh : 24 + 8 * zh]]
+                o_ref[at : at + 16, columns] = jnp.concatenate(pair, axis=0).astype(o_ref.dtype)
+
         levels = [level_of(ref[here, WIDTH:]) for ref in (a_ref, b_ref)]
         top = jnp.maximum(*levels)
         shares = [jnp.exp2(level - top) for level in levels]
@@ -162,14 +174,14 @@
             head = slice(h * HEAD_DIM, (h + 1) * HEAD_DIM)
             mixed = a_ref[here, head].astype(jnp.float32) * shares[0][:, h : h + 1]
             mixed = mixed + b_ref[here, head].astype(jnp.float32) * shares[1][:, h : h + 1]
-            o_ref[here, head] = mixed.astype(jnp.bfloat16)
+            put(head, mixed)
         high, middle, low = split(top + jnp.log2(total))
         stats = jnp.where(
             lane < 8,
             high,
             jnp.where(lane < 16, jnp.roll(middle, 8, axis=1), jnp.roll(low, 16, axis=1)),
         )
-        o_ref[here, WIDTH:] = jnp.where(lane < 24, stats, 0.0).astype(jnp.bfloat16)
+        put(slice(WIDTH, PACKED), jnp.where(lane < 24, stats, 0.0))
 
 
 def merge(a, b):
@@ -245,7 +257,7 @@
 
 
 def project_kernel(a_ref, w_ref, w_core, w_chip, w_both, o_ref):
-    rows = a_ref.shape[0]
+    half = a_ref.shape[0] // 2
     chip = lax.axis_index("zl")
     core = lax.axis_index("c")
     attended = a_ref[...]
@@ -255,9 +267,11 @@
         (1 - chip, core, w_chip),
         (1 - chip, 1 - core, w_both),
     ):
-        at = pl.multiple_of((there * 2 + that) * rows, rows)
         part = jnp.dot(attended, weight[...], preferred_element_type=jnp.float32)
-        o_ref[pl.ds(at, rows), :] = part.astype(o_ref.dtype)
+        for y in range(half // 8):
+            pair = [part[8 * y : 8 * y + 8], part[half + 8 * y : half + 8 * y + 8]]
+            at = pl.multiple_of((y * 4 + there * 2 + that) * 16, 16)
+            o_ref[pl.ds(at, 16), :] = jnp.concatenate(pair, axis=0).astype(o_ref.dtype)
 
 
 def project(attended, *weights):
@@ -275,7 +289,7 @@
     half = rows // 2
     for n in range(near):
         parts = [
-            s_ref[(n * heads + h) * rows : (n * heads + h + 1) * rows, :].astype(jnp.float32)
+            s_ref[(h * near + n) * rows : (h * near + n + 1) * rows, :].astype(jnp.float32)
             for h in range(heads)
         ]
         total = functools.reduce(jnp.add, parts)
@@ -298,10 +312,10 @@
 
 
 def shards(queries, keys, values, cutoffs, out_weight):
-    far = SIZES[0] * SIZES[1]
+    far = SIZES[0] * SIZES[1] * SIZES[2] * SIZES[3]
     k_other = lax.ppermute(keys, "c", SWAP)
     v_other = lax.ppermute(values, "c", SWAP)
-    packed = exchange(pack(queries, cutoffs, 2 * far), ("zl",) + FAR)
+    packed = exchange(pack(queries, cutoffs, 2 * far), QUERIES)
     pairs = (keys, values, k_other, v_other)
     away = lax.ppermute(attend(packed, 1, *pairs), "zl", SWAP)
     parts = exchange(merge(attend(packed, 0, *pairs), away), FAR)
@@ -310,7 +324,7 @@
     w_both = lax.ppermute(w_chip, "c", SWAP)
     attended = exchange(combine(parts, far), FAR)
     sums = project(attended, out_weight, w_core, w_chip, w_both)
-    return total_of(exchange(sums, NEAR + HEAD))
+    return total_of(exchange(sums, HEAD + NEAR))
 
 
 def solution(mesh):

time: 121 us -> 118 us (0.975)
  starting transfers between devices: 56.6 us -> 54.9 us
  blocking collectives: 26.2 us -> 24.5 us
    all_to_all x1, blocking collectives: 26.2 us -> 24.5 us  [exchange(): return lax.all_to_all(x, axis, 0, 0, tiled=True)]
    ppermute x1, starting transfers between devices: 21.2 us -> 19.9 us  [shards(): w_core = lax.ppermute(out_weight, 'c', SWAP)]
where the time goes in v5:
time: 118 us; the launch traced here: 117 us
  starting transfers between devices  54.9 us (47%)
  blocking collectives  24.5 us (21%)
  waiting for transfers between devices  21.5 us (18%)
  Pallas kernels  16.3 us (14%)
    all_to_all x1, blocking collectives, exchange(): return lax.all_to_all(x, axis, 0, 0, tiled=True)  24.5 us
    all_to_all x3, starting transfers between devices, exchange(): return lax.all_to_all(x, axis, 0, 0, tiled=True)  24.2 us
    ppermute x1, starting transfers between devices, shards(): w_core = lax.ppermute(out_weight, 'c', SWAP)  19.9 us
    all_to_all x3, waiting for transfers between devices, exchange(): return lax.all_to_all(x, axis, 0, 0, tiled=True)  18.1 us
    pallas_call x2, Pallas kernels, attend(): pl.pallas_call(functools.partial(attend_kernel, 256, whose), in_specs=[vm...  10.8 us
    ppermute x1, starting transfers between devices, shards(): k_other = lax.ppermute(keys, 'c', SWAP)  2.86 us
  transfers between devices with their start and end apart: 9, of which 4 were waited for; matrix products, arithmetic and copies ran while one was open for 0% of the time, Pallas kernels for 6%

profile of v5, /device:TPU:1, one launch (start us, length us, event | category | flops | bytes accessed | tf_op | source)
XLA Modules:
  0.0 117.3 jit_solution(10139686678261871079)
XLA Ops:
  0.0 1.7 %pack.1 = bf16[256,1152]{1,0:T(8,128)(2,1)} custom-call(bf16[8,1024]{1,0:T(8,128)(2,1)} %q_ref.1, s32[8]{0:T(128)} %cut_ref.1), custom_call_target="tpu_custom_call" | custom-call | tf_op jit(solution)/shard_map/pack/pallas_call | solution.py:217
  1.7 0.0 copy-start.1
  1.7 0.0 copy-start.2
  1.7 13.6 %all-to-all-start = ((bf16[32,8,1152]{2,1,0:T(8,128)(2,1)}), bf16[32,8,1152]{2,1,0:T(8,128)(2,1)S(1)}, u32[]{:S(2)}, u32[]{:S(2)}) async-start(bf16[32,8,1152]{2,1,0:T(8,128)(2,1)} %bitcast.14), calls=%async_computation | async-start | bytes 1179648 | tf_op jit(solution)/shard_map/all_to_all | solution.py:311
  15.3 0.0 copy-done.1
  15.3 2.9 %collective-permute-start = (bf16[2048,128]{1,0:T(8,128)(2,1)S(1)}, bf16[2048,128]{1,0:T(8,128)(2,1)S(1)}, u32[]{:S(2)}, u32[]{:S(2)}) collective-permute-start(bf16[2048,128]{1,0:T(8,128)(2,1)S(1)} %copy-done.1), channel_id=1, source_target_pairs={{0,8},{8,0},{1,9},{9,1},{2,10},{10,2},{3,11},{11,3},{4,12},{12,4},... | collective-permute-start | bytes 1572872 | tf_op jit(solution)/shard_map/ppermute | solution.py:316
  18.2 0.0 copy-done.2
  18.2 1.9 %collective-permute-start.1 = (bf16[2048,128]{1,0:T(8,128)(2,1)S(1)}, bf16[2048,128]{1,0:T(8,128)(2,1)S(1)}, u32[]{:S(2)}, u32[]{:S(2)}) collective-permute-start(bf16[2048,128]{1,0:T(8,128)(2,1)S(1)} %copy-done.2), channel_id=1, source_target_pairs={{0,8},{8,0},{1,9},{9,1},{2,10},{10,2},{3,11},{11,3},{4,12},{12,4},... | collective-permute-start | bytes 1572872 | tf_op jit(solution)/shard_map/ppermute | solution.py:317
  20.1 0.0 collective-permute-done.k_other
  20.1 1.9 %collective-permute-done.1.v_other = bf16[2048,128]{1,0:T(8,128)(2,1)S(1)} collective-permute-done((bf16[2048,128]{1,0:T(8,128)(2,1)S(1)}, bf16[2048,128]{1,0:T(8,128)(2,1)S(1)}, u32[]{:S(2)}, u32[]{:S(2)}) %collective-permute-start.1) | collective-permute-done | bytes 524320 | tf_op jit(solution)/shard_map/ppermute | solution.py:317
  22.0 11.2 %all-to-all-done = bf16[32,8,1152]{2,1,0:T(8,128)(2,1)S(1)} async-done(((bf16[32,8,1152]{2,1,0:T(8,128)(2,1)}), bf16[32,8,1152]{2,1,0:T(8,128)(2,1)S(1)}, u32[]{:S(2)}, u32[]{:S(2)}) %all-to-all-start) | async-done | bytes 589856 | tf_op jit(solution)/shard_map/all_to_all | solution.py:311
  33.2 5.3 %attend.3 = bf16[128,1152]{1,0:T(8,128)(2,1)S(1)} custom-call(bf16[256,1152]{1,0:T(8,128)(2,1)S(1)} %bitcast.10, bf16[2048,128]{1,0:T(8,128)(2,1)S(1)} %copy-done.1, bf16[2048,128]{1,0:T(8,128)(2,1)S(1)} %copy-done.2, bf16[2048,128]{1,0:T(8,128)(2,1)S(1)} %collective-permute-done.k_other, bf16[2048,128]{1,0:T(8,128)(2,1)S(1)} %collective-permute-done.1.v_other), custom_call_target="tpu_custom_call" | custom-call | flops 4294967296 | bytes 2097152 | tf_op jit(solution)/shard_map/attend/pallas_call | solution.py:137
  38.5 1.9 %collective-permute-start.2 = (bf16[128,1152]{1,0:T(8,128)(2,1)S(1)}, bf16[128,1152]{1,0:T(8,128)(2,1)S(1)}, u32[]{:S(2)}, u32[]{:S(2)}) collective-permute-start(bf16[128,1152]{1,0:T(8,128)(2,1)S(1)} %attend.3), channel_id=1, source_target_pairs={{0,16},{16,0},{1,17},{17,1},{2,18},{18,2},{3,19},{19,3},{4,20},{20... | collective-permute-start | bytes 884744 | tf_op jit(solution)/shard_map/ppermute | solution.py:320
  40.4 5.5 %attend.2.a_ref = bf16[128,1152]{1,0:T(8,128)(2,1)S(1)} custom-call(bf16[256,1152]{1,0:T(8,128)(2,1)S(1)} %bitcast.11, bf16[2048,128]{1,0:T(8,128)(2,1)S(1)} %copy-done.1, bf16[2048,128]{1,0:T(8,128)(2,1)S(1)} %copy-done.2, bf16[2048,128]{1,0:T(8,128)(2,1)S(1)} %collective-permute-done.k_other, bf16[2048,128]{1,0:T(8,128)(2,1)S(1)} %collective-permute-done.1.v_other), custom_call_target="tpu_custom_call" | custom-call | flops 4294967296 | bytes 2097152 | tf_op jit(solution)/shard_map/attend/pallas_call | solution.py:137
  46.0 0.0 collective-permute-done.2.b_ref
  46.0 1.6 %merge.1 = bf16[128,1152]{1,0:T(8,128)(2,1)} custom-call(bf16[128,1152]{1,0:T(8,128)(2,1)S(1)} %attend.2.a_ref, bf16[128,1152]{1,0:T(8,128)(2,1)S(1)} %collective-permute-done.2.b_ref), custom_call_target="tpu_custom_call" | custom-call | tf_op jit(solution)/shard_map/merge/pallas_call | solution.py:188
  47.6 0.0 copy-start
  47.6 6.6 %all-to-all-start.1 = ((bf16[16,8,1152]{2,1,0:T(8,128)(2,1)}), bf16[16,8,1152]{2,1,0:T(8,128)(2,1)S(1)}, u32[]{:S(2)}, u32[]{:S(2)}) async-start(bf16[16,8,1152]{2,1,0:T(8,128)(2,1)} %bitcast.2), calls=%async_computation.1 | async-start | bytes 589824 | tf_op jit(solution)/shard_map/all_to_all | solution.py:311
  54.2 0.0 copy-done
  54.2 2.1 %collective-permute-start.4 = (bf16[1024,128]{1,0:T(8,128)(2,1)S(1)}, bf16[1024,128]{1,0:T(8,128)(2,1)S(1)}, u32[]{:S(2)}, u32[]{:S(2)}) collective-permute-start(bf16[1024,128]{1,0:T(8,128)(2,1)S(1)} %copy-done), channel_id=1, source_target_pairs={{0,16},{16,0},{1,17},{17,1},{2,18},{18,2},{3,19},{19,3},{4,20},{20... | collective-permute-start | bytes 786440 | tf_op jit(solution)/shard_map/ppermute | solution.py:323
  56.3 6.9 %all-to-all-done.1 = bf16[16,8,1152]{2,1,0:T(8,128)(2,1)S(1)} async-done(((bf16[16,8,1152]{2,1,0:T(8,128)(2,1)}), bf16[16,8,1152]{2,1,0:T(8,128)(2,1)S(1)}, u32[]{:S(2)}, u32[]{:S(2)}) %all-to-all-start.1) | async-done | bytes 294944 | tf_op jit(solution)/shard_map/all_to_all | solution.py:311
  63.2 1.1 combine.1
  64.4 4.1 %all-to-all-start.2 = ((bf16[16,8,1024]{2,1,0:T(8,128)(2,1)}), bf16[16,8,1024]{2,1,0:T(8,128)(2,1)S(1)}, u32[]{:S(2)}, u32[]{:S(2)}) async-start(bf16[16,8,1024]{2,1,0:T(8,128)(2,1)} %bitcast.4), calls=%async_computation.2 | async-start | bytes 524288 | tf_op jit(solution)/shard_map/all_to_all | solution.py:311
  68.4 19.9 %collective-permute-start.3 = (bf16[1024,128]{1,0:T(8,128)(2,1)S(1)}, bf16[1024,128]{1,0:T(8,128)(2,1)S(1)}, u32[]{:S(2)}, u32[]{:S(2)}) collective-permute-start(bf16[1024,128]{1,0:T(8,128)(2,1)S(1)} %copy-done), channel_id=1, source_target_pairs={{0,8},{8,0},{1,9},{9,1},{2,10},{10,2},{3,11},{11,3},{4,12},{12,4},... | collective-permute-start | bytes 786440 | tf_op jit(solution)/shard_map/ppermute | solution.py:322
  88.3 0.0 collective-permute-done.4.w_chip
  88.4 1.9 %collective-permute-start.5 = (bf16[1024,128]{1,0:T(8,128)(2,1)S(1)}, bf16[1024,128]{1,0:T(8,128)(2,1)S(1)}, u32[]{:S(2)}, u32[]{:S(2)}) collective-permute-start(bf16[1024,128]{1,0:T(8,128)(2,1)S(1)} %collective-permute-done.4.w_chip), channel_id=1, source_target_pairs={{0,8},{8,0},{1,9},{9,1},{2,10},{10,2},{3,11},{11,3},{4,12},{12,4},... | collective-permute-start | bytes 786440 | tf_op jit(solution)/shard_map/ppermute | solution.py:324
  90.3 0.0 collective-permute-done.3.w_core
  90.3 1.5 %collective-permute-done.5.w_both = bf16[1024,128]{1,0:T(8,128)(2,1)S(1)} collective-permute-done((bf16[1024,128]{1,0:T(8,128)(2,1)S(1)}, bf16[1024,128]{1,0:T(8,128)(2,1)S(1)}, u32[]{:S(2)}, u32[]{:S(2)}) %collective-permute-start.5) | collective-permute-done | bytes 262176 | tf_op jit(solution)/shard_map/ppermute | solution.py:324
  91.8 0.0 all-to-all-done.2
  91.8 0.4 project.1
  92.2 24.5 %all_to_all.44 = bf16[32,16,128]{2,1,0:T(8,128)(2,1)S(1)} all-to-all(bf16[32,16,128]{2,1,0:T(8,128)(2,1)S(1)} %bitcast.13), channel_id=1, replica_groups=mesh['yc'=2,'yb'=2,'ya'=2,'zh'=2,'zl'=2,'c'=2,'w'=2,'x'=4] {'w','x','zl'..., dimensions={0} | all-to-all | bytes 262144 | tf_op jit(solution)/shard_map/all_to_all | solution.py:311
  116.7 0.6 total.1
Async XLA Ops:
  1.7 13.6 %copy-start.1 = (bf16[2048,128]{1,0:T(8,128)(2,1)S(1)}, bf16[2048,128]{1,0:T(8,128)(2,1)}, u32[]{:S(2)}) copy-start(bf16[2048,128]{1,0:T(8,128)(2,1)} %k_mine.3) | copy-start | bytes 1572868
  1.7 16.5 %copy-start.2 = (bf16[2048,128]{1,0:T(8,128)(2,1)S(1)}, bf16[2048,128]{1,0:T(8,128)(2,1)}, u32[]{:S(2)}) copy-start(bf16[2048,128]{1,0:T(8,128)(2,1)} %v_mine.3) | copy-start | bytes 1572868
  1.7 31.5 %all-to-all-start = ((bf16[32,8,1152]{2,1,0:T(8,128)(2,1)}), bf16[32,8,1152]{2,1,0:T(8,128)(2,1)S(1)}, u32[]{:S(2)}, u32[]{:S(2)}) async-start(bf16[32,8,1152]{2,1,0:T(8,128)(2,1)} %bitcast.14), calls=%async_computation | async-start | bytes 1179648 | tf_op jit(solution)/shard_map/all_to_all | solution.py:311
  15.3 4.8 %collective-permute-start = (bf16[2048,128]{1,0:T(8,128)(2,1)S(1)}, bf16[2048,128]{1,0:T(8,128)(2,1)S(1)}, u32[]{:S(2)}, u32[]{:S(2)}) collective-permute-start(bf16[2048,128]{1,0:T(8,128)(2,1)S(1)} %copy-done.1), channel_id=1, source_target_pairs={{0,8},{8,0},{1,9},{9,1},{2,10},{10,2},{3,11},{11,3},{4,12},{12,4},... | collective-permute-start | bytes 1572872 | tf_op jit(solution)/shard_map/ppermute | solution.py:316
  18.2 3.8 %collective-permute-start.1 = (bf16[2048,128]{1,0:T(8,128)(2,1)S(1)}, bf16[2048,128]{1,0:T(8,128)(2,1)S(1)}, u32[]{:S(2)}, u32[]{:S(2)}) collective-permute-start(bf16[2048,128]{1,0:T(8,128)(2,1)S(1)} %copy-done.2), channel_id=1, source_target_pairs={{0,8},{8,0},{1,9},{9,1},{2,10},{10,2},{3,11},{11,3},{4,12},{12,4},... | collective-permute-start | bytes 1572872 | tf_op jit(solution)/shard_map/ppermute | solution.py:317
  38.5 7.5 %collective-permute-start.2 = (bf16[128,1152]{1,0:T(8,128)(2,1)S(1)}, bf16[128,1152]{1,0:T(8,128)(2,1)S(1)}, u32[]{:S(2)}, u32[]{:S(2)}) collective-permute-start(bf16[128,1152]{1,0:T(8,128)(2,1)S(1)} %attend.3), channel_id=1, source_target_pairs={{0,16},{16,0},{1,17},{17,1},{2,18},{18,2},{3,19},{19,3},{4,20},{20... | collective-permute-start | bytes 884744 | tf_op jit(solution)/shard_map/ppermute | solution.py:320
  47.6 6.6 %copy-start = (bf16[1024,128]{1,0:T(8,128)(2,1)S(1)}, bf16[1024,128]{1,0:T(8,128)(2,1)}, u32[]{:S(2)}) copy-start(bf16[1024,128]{1,0:T(8,128)(2,1)} %w_ref.1) | copy-start | bytes 786436
  47.6 15.6 %all-to-all-start.1 = ((bf16[16,8,1152]{2,1,0:T(8,128)(2,1)}), bf16[16,8,1152]{2,1,0:T(8,128)(2,1)S(1)}, u32[]{:S(2)}, u32[]{:S(2)}) async-start(bf16[16,8,1152]{2,1,0:T(8,128)(2,1)} %bitcast.2), calls=%async_computation.1 | async-start | bytes 589824 | tf_op jit(solution)/shard_map/all_to_all | solution.py:311
  54.2 34.2 %collective-permute-start.4 = (bf16[1024,128]{1,0:T(8,128)(2,1)S(1)}, bf16[1024,128]{1,0:T(8,128)(2,1)S(1)}, u32[]{:S(2)}, u32[]{:S(2)}) collective-permute-start(bf16[1024,128]{1,0:T(8,128)(2,1)S(1)} %copy-done), channel_id=1, source_target_pairs={{0,16},{16,0},{1,17},{17,1},{2,18},{18,2},{3,19},{19,3},{4,20},{20... | collective-permute-start | bytes 786440 | tf_op jit(solution)/shard_map/ppermute | solution.py:323
  64.4 27.4 %all-to-all-start.2 = ((bf16[16,8,1024]{2,1,0:T(8,128)(2,1)}), bf16[16,8,1024]{2,1,0:T(8,128)(2,1)S(1)}, u32[]{:S(2)}, u32[]{:S(2)}) async-start(bf16[16,8,1024]{2,1,0:T(8,128)(2,1)} %bitcast.4), calls=%async_computation.2 | async-start | bytes 524288 | tf_op jit(solution)/shard_map/all_to_all | solution.py:311
  68.4 21.8 %collective-permute-start.3 = (bf16[1024,128]{1,0:T(8,128)(2,1)S(1)}, bf16[1024,128]{1,0:T(8,128)(2,1)S(1)}, u32[]{:S(2)}, u32[]{:S(2)}) collective-permute-start(bf16[1024,128]{1,0:T(8,128)(2,1)S(1)} %copy-done), channel_id=1, source_target_pairs={{0,8},{8,0},{1,9},{9,1},{2,10},{10,2},{3,11},{11,3},{4,12},{12,4},... | collective-permute-start | bytes 786440 | tf_op jit(solution)/shard_map/ppermute | solution.py:322
  88.4 3.4 %collective-permute-start.5 = (bf16[1024,128]{1,0:T(8,128)(2,1)S(1)}, bf16[1024,128]{1,0:T(8,128)(2,1)S(1)}, u32[]{:S(2)}, u32[]{:S(2)}) collective-permute-start(bf16[1024,128]{1,0:T(8,128)(2,1)S(1)} %collective-permute-done.4.w_chip), channel_id=1, source_target_pairs={{0,8},{8,0},{1,9},{9,1},{2,10},{10,2},{3,11},{11,3},{4,12},{12,4},... | collective-permute-start | bytes 786440 | tf_op jit(solution)/shard_map/ppermute | solution.py:324

commit v6 on v5

--- a/solution.py
+++ b/solution.py
@@ -26,8 +26,8 @@
 SIZES = (2, 2, 2, 2, 2, 2, 2, 4)
 BLK = ("yc", "yb", "ya", "zh", "zl", "c")
 HEAD = ("w", "x")
-QUERIES = ("zl", "yb", "yc", "ya", "zh")
 FAR = ("zh", "yc", "yb", "ya")
+QUERIES = ("zl",) + FAR
 NEAR = ("zl", "c")
 SWAP = ((0, 1), (1, 0))
 
@@ -153,18 +153,10 @@
 
 
 def merge_kernel(a_ref, b_ref, o_ref):
-    rows = 32
+    rows = 64
     lane = lax.broadcasted_iota(jnp.int32, (rows, LANES), 1)
-    for n in range(o_ref.shape[0] // rows):
-        here = slice(n * rows, (n + 1) * rows)
-        yb, yc = n // 2, n % 2
-
-        def put(columns, block):
-            for zh in range(2):
-                at = ((zh * 2 + yc) * 2 + yb) * 16
-                pair = [block[8 * zh : 8 * zh + 8], block[16 + 8 * zh : 24 + 8 * zh]]
-                o_ref[at : at + 16, columns] = jnp.concatenate(pair, axis=0).astype(o_ref.dtype)
-
+    for at in range(0, o_ref.shape[0], rows):
+        here = slice(at, at + rows)
         levels = [level_of(ref[here, WIDTH:]) for ref in (a_ref, b_ref)]
         top = jnp.maximum(*levels)
         shares = [jnp.exp2(level - top) for level in levels]
@@ -174,14 +166,14 @@
             head = slice(h * HEAD_DIM, (h + 1) * HEAD_DIM)
             mixed = a_ref[here, head].astype(jnp.float32) * shares[0][:, h : h + 1]
             mixed = mixed + b_ref[here, head].astype(jnp.float32) * shares[1][:, h : h + 1]
-            put(head, mixed)
+            o_ref[here, head] = mixed.astype(jnp.bfloat16)
         high, middle, low = split(top + jnp.log2(total))
         stats = jnp.where(
             lane < 8,
             high,
             jnp.where(lane < 16, jnp.roll(middle, 8, axis=1), jnp.roll(low, 16, axis=1)),
         )
-        put(slice(WIDTH, PACKED), jnp.where(lane < 24, stats, 0.0))
+        o_ref[here, WIDTH:] = jnp.where(lane < 24, stats, 0.0).astype(jnp.bfloat16)
 
 
 def merge(a, b):

time: 118 us -> 118 us (level)
  starting transfers between devices: 54.9 us -> 57.5 us
  waiting for transfers between devices: 21.5 us -> 19.2 us
    all_to_all x3, waiting for transfers between devices: 18.1 us -> 15.8 us  [exchange(): return lax.all_to_all(x, axis, 0, 0, tiled=True)]
    all_to_all x3, starting transfers between devices: 24.2 us -> 26.4 us  [exchange(): return lax.all_to_all(x, axis, 0, 0, tiled=True)]
where the time goes in v6:
time: 118 us; the launch traced here: 117 us
  starting transfers between devices  57.5 us (49%)
  blocking collectives  24.3 us (21%)
  waiting for transfers between devices  19.2 us (16%)
  Pallas kernels  16.1 us (14%)
    all_to_all x3, starting transfers between devices, exchange(): return lax.all_to_all(x, axis, 0, 0, tiled=True)  26.4 us
    all_to_all x1, blocking collectives, exchange(): return lax.all_to_all(x, axis, 0, 0, tiled=True)  24.3 us
    ppermute x1, starting transfers between devices, shards(): w_core = lax.ppermute(out_weight, 'c', SWAP)  19.9 us
    all_to_all x3, waiting for transfers between devices, exchange(): return lax.all_to_all(x, axis, 0, 0, tiled=True)  15.8 us
    pallas_call x2, Pallas kernels, attend(): pl.pallas_call(functools.partial(attend_kernel, 256, whose), in_specs=[vm...  10.8 us
    ppermute x1, starting transfers between devices, shards(): k_other = lax.ppermute(keys, 'c', SWAP)  2.86 us
    ppermute x1, starting transfers between devices, shards(): w_chip = lax.ppermute(out_weight, 'zl', SWAP)  2.56 us
  transfers between devices with their start and end apart: 9, of which 4 were waited for; matrix products, arithmetic and copies ran while one was open for 0% of the time, Pallas kernels for 6%

profile of v6, /device:TPU:1, one launch (start us, length us, event | category | flops | bytes accessed | tf_op | source)
XLA Modules:
  0.0 117.3 jit_solution(6929697369686000683)
XLA Ops:
  0.0 1.7 %pack.1 = bf16[256,1152]{1,0:T(8,128)(2,1)} custom-call(bf16[8,1024]{1,0:T(8,128)(2,1)} %q_ref.1, s32[8]{0:T(128)} %cut_ref.1), custom_call_target="tpu_custom_call" | custom-call | tf_op jit(solution)/shard_map/pack/pallas_call | solution.py:209
  1.7 0.0 copy-start.1
  1.7 0.0 copy-start.2
  1.7 13.6 %all-to-all-start = ((bf16[32,8,1152]{2,1,0:T(8,128)(2,1)}), bf16[32,8,1152]{2,1,0:T(8,128)(2,1)S(1)}, u32[]{:S(2)}, u32[]{:S(2)}) async-start(bf16[32,8,1152]{2,1,0:T(8,128)(2,1)} %bitcast.14), calls=%async_computation | async-start | bytes 1179648 | tf_op jit(solution)/shard_map/all_to_all | solution.py:303
  15.3 0.0 copy-done.1
  15.3 2.9 %collective-permute-start = (bf16[2048,128]{1,0:T(8,128)(2,1)S(1)}, bf16[2048,128]{1,0:T(8,128)(2,1)S(1)}, u32[]{:S(2)}, u32[]{:S(2)}) collective-permute-start(bf16[2048,128]{1,0:T(8,128)(2,1)S(1)} %copy-done.1), channel_id=1, source_target_pairs={{0,8},{8,0},{1,9},{9,1},{2,10},{10,2},{3,11},{11,3},{4,12},{12,4},... | collective-permute-start | bytes 1572872 | tf_op jit(solution)/shard_map/ppermute | solution.py:308
  18.2 0.0 copy-done.2
  18.2 1.9 %collective-permute-start.1 = (bf16[2048,128]{1,0:T(8,128)(2,1)S(1)}, bf16[2048,128]{1,0:T(8,128)(2,1)S(1)}, u32[]{:S(2)}, u32[]{:S(2)}) collective-permute-start(bf16[2048,128]{1,0:T(8,128)(2,1)S(1)} %copy-done.2), channel_id=1, source_target_pairs={{0,8},{8,0},{1,9},{9,1},{2,10},{10,2},{3,11},{11,3},{4,12},{12,4},... | collective-permute-start | bytes 1572872 | tf_op jit(solution)/shard_map/ppermute | solution.py:309
  20.1 0.0 collective-permute-done.k_other
  20.1 1.9 %collective-permute-done.1.v_other = bf16[2048,128]{1,0:T(8,128)(2,1)S(1)} collective-permute-done((bf16[2048,128]{1,0:T(8,128)(2,1)S(1)}, bf16[2048,128]{1,0:T(8,128)(2,1)S(1)}, u32[]{:S(2)}, u32[]{:S(2)}) %collective-permute-start.1) | collective-permute-done | bytes 524320 | tf_op jit(solution)/shard_map/ppermute | solution.py:309
  22.0 9.4 %all-to-all-done = bf16[32,8,1152]{2,1,0:T(8,128)(2,1)S(1)} async-done(((bf16[32,8,1152]{2,1,0:T(8,128)(2,1)}), bf16[32,8,1152]{2,1,0:T(8,128)(2,1)S(1)}, u32[]{:S(2)}, u32[]{:S(2)}) %all-to-all-start) | async-done | bytes 589856 | tf_op jit(solution)/shard_map/all_to_all | solution.py:303
  31.4 5.3 %attend.3 = bf16[128,1152]{1,0:T(8,128)(2,1)S(1)} custom-call(bf16[256,1152]{1,0:T(8,128)(2,1)S(1)} %bitcast.10, bf16[2048,128]{1,0:T(8,128)(2,1)S(1)} %copy-done.1, bf16[2048,128]{1,0:T(8,128)(2,1)S(1)} %copy-done.2, bf16[2048,128]{1,0:T(8,128)(2,1)S(1)} %collective-permute-done.k_other, bf16[2048,128]{1,0:T(8,128)(2,1)S(1)} %collective-permute-done.1.v_other), custom_call_target="tpu_custom_call" | custom-call | flops 4294967296 | bytes 2097152 | tf_op jit(solution)/shard_map/attend/pallas_call | solution.py:137
  36.7 2.0 %collective-permute-start.2 = (bf16[128,1152]{1,0:T(8,128)(2,1)S(1)}, bf16[128,1152]{1,0:T(8,128)(2,1)S(1)}, u32[]{:S(2)}, u32[]{:S(2)}) collective-permute-start(bf16[128,1152]{1,0:T(8,128)(2,1)S(1)} %attend.3), channel_id=1, source_target_pairs={{0,16},{16,0},{1,17},{17,1},{2,18},{18,2},{3,19},{19,3},{4,20},{20... | collective-permute-start | bytes 884744 | tf_op jit(solution)/shard_map/ppermute | solution.py:312
  38.7 5.5 %attend.2.a_ref = bf16[128,1152]{1,0:T(8,128)(2,1)S(1)} custom-call(bf16[256,1152]{1,0:T(8,128)(2,1)S(1)} %bitcast.11, bf16[2048,128]{1,0:T(8,128)(2,1)S(1)} %copy-done.1, bf16[2048,128]{1,0:T(8,128)(2,1)S(1)} %copy-done.2, bf16[2048,128]{1,0:T(8,128)(2,1)S(1)} %collective-permute-done.k_other, bf16[2048,128]{1,0:T(8,128)(2,1)S(1)} %collective-permute-done.1.v_other), custom_call_target="tpu_custom_call" | custom-call | flops 4294967296 | bytes 2097152 | tf_op jit(solution)/shard_map/attend/pallas_call | solution.py:137
  44.3 0.0 collective-permute-done.2.b_ref
  44.3 1.4 %merge.1 = bf16[128,1152]{1,0:T(8,128)(2,1)} custom-call(bf16[128,1152]{1,0:T(8,128)(2,1)S(1)} %attend.2.a_ref, bf16[128,1152]{1,0:T(8,128)(2,1)S(1)} %collective-permute-done.2.b_ref), custom_call_target="tpu_custom_call" | custom-call | tf_op jit(solution)/shard_map/merge/pallas_call | solution.py:180
  45.7 0.0 copy-start
  45.7 8.7 %all-to-all-start.1 = ((bf16[16,8,1152]{2,1,0:T(8,128)(2,1)}), bf16[16,8,1152]{2,1,0:T(8,128)(2,1)S(1)}, u32[]{:S(2)}, u32[]{:S(2)}) async-start(bf16[16,8,1152]{2,1,0:T(8,128)(2,1)} %bitcast.2), calls=%async_computation.1 | async-start | bytes 589824 | tf_op jit(solution)/shard_map/all_to_all | solution.py:303
  54.3 0.0 copy-done
  54.3 2.6 %collective-permute-start.4 = (bf16[1024,128]{1,0:T(8,128)(2,1)S(1)}, bf16[1024,128]{1,0:T(8,128)(2,1)S(1)}, u32[]{:S(2)}, u32[]{:S(2)}) collective-permute-start(bf16[1024,128]{1,0:T(8,128)(2,1)S(1)} %copy-done), channel_id=1, source_target_pairs={{0,16},{16,0},{1,17},{17,1},{2,18},{18,2},{3,19},{19,3},{4,20},{20... | collective-permute-start | bytes 786440 | tf_op jit(solution)/shard_map/ppermute | solution.py:315
  56.9 6.4 %all-to-all-done.1 = bf16[16,8,1152]{2,1,0:T(8,128)(2,1)S(1)} async-done(((bf16[16,8,1152]{2,1,0:T(8,128)(2,1)}), bf16[16,8,1152]{2,1,0:T(8,128)(2,1)S(1)}, u32[]{:S(2)}, u32[]{:S(2)}) %all-to-all-start.1) | async-done | bytes 294944 | tf_op jit(solution)/shard_map/all_to_all | solution.py:303
  63.3 1.1 combine.1
  64.4 4.1 %all-to-all-start.2 = ((bf16[16,8,1024]{2,1,0:T(8,128)(2,1)}), bf16[16,8,1024]{2,1,0:T(8,128)(2,1)S(1)}, u32[]{:S(2)}, u32[]{:S(2)}) async-start(bf16[16,8,1024]{2,1,0:T(8,128)(2,1)} %bitcast.4), calls=%async_computation.2 | async-start | bytes 524288 | tf_op jit(solution)/shard_map/all_to_all | solution.py:303
  68.5 19.9 %collective-permute-start.3 = (bf16[1024,128]{1,0:T(8,128)(2,1)S(1)}, bf16[1024,128]{1,0:T(8,128)(2,1)S(1)}, u32[]{:S(2)}, u32[]{:S(2)}) collective-permute-start(bf16[1024,128]{1,0:T(8,128)(2,1)S(1)} %copy-done), channel_id=1, source_target_pairs={{0,8},{8,0},{1,9},{9,1},{2,10},{10,2},{3,11},{11,3},{4,12},{12,4},... | collective-permute-start | bytes 786440 | tf_op jit(solution)/shard_map/ppermute | solution.py:314
  88.4 0.0 collective-permute-done.4.w_chip
  88.5 1.9 %collective-permute-start.5 = (bf16[1024,128]{1,0:T(8,128)(2,1)S(1)}, bf16[1024,128]{1,0:T(8,128)(2,1)S(1)}, u32[]{:S(2)}, u32[]{:S(2)}) collective-permute-start(bf16[1024,128]{1,0:T(8,128)(2,1)S(1)} %collective-permute-done.4.w_chip), channel_id=1, source_target_pairs={{0,8},{8,0},{1,9},{9,1},{2,10},{10,2},{3,11},{11,3},{4,12},{12,4},... | collective-permute-start | bytes 786440 | tf_op jit(solution)/shard_map/ppermute | solution.py:316
  90.4 0.0 collective-permute-done.3.w_core
  90.4 1.5 %collective-permute-done.5.w_both = bf16[1024,128]{1,0:T(8,128)(2,1)S(1)} collective-permute-done((bf16[1024,128]{1,0:T(8,128)(2,1)S(1)}, bf16[1024,128]{1,0:T(8,128)(2,1)S(1)}, u32[]{:S(2)}, u32[]{:S(2)}) %collective-permute-start.5) | collective-permute-done | bytes 262176 | tf_op jit(solution)/shard_map/ppermute | solution.py:316
  91.9 0.0 all-to-all-done.2
  91.9 0.4 project.1
  92.3 24.3 %all_to_all.44 = bf16[32,16,128]{2,1,0:T(8,128)(2,1)S(1)} all-to-all(bf16[32,16,128]{2,1,0:T(8,128)(2,1)S(1)} %bitcast.13), channel_id=1, replica_groups=mesh['yc'=2,'yb'=2,'ya'=2,'zh'=2,'zl'=2,'c'=2,'w'=2,'x'=4] {'w','x','zl'..., dimensions={0} | all-to-all | bytes 262144 | tf_op jit(solution)/shard_map/all_to_all | solution.py:303
  116.6 0.6 total.1
Async XLA Ops:
  1.7 13.6 %copy-start.1 = (bf16[2048,128]{1,0:T(8,128)(2,1)S(1)}, bf16[2048,128]{1,0:T(8,128)(2,1)}, u32[]{:S(2)}) copy-start(bf16[2048,128]{1,0:T(8,128)(2,1)} %k_mine.3) | copy-start | bytes 1572868
  1.7 16.5 %copy-start.2 = (bf16[2048,128]{1,0:T(8,128)(2,1)S(1)}, bf16[2048,128]{1,0:T(8,128)(2,1)}, u32[]{:S(2)}) copy-start(bf16[2048,128]{1,0:T(8,128)(2,1)} %v_mine.3) | copy-start | bytes 1572868
  1.7 29.7 %all-to-all-start = ((bf16[32,8,1152]{2,1,0:T(8,128)(2,1)}), bf16[32,8,1152]{2,1,0:T(8,128)(2,1)S(1)}, u32[]{:S(2)}, u32[]{:S(2)}) async-start(bf16[32,8,1152]{2,1,0:T(8,128)(2,1)} %bitcast.14), calls=%async_computation | async-start | bytes 1179648 | tf_op jit(solution)/shard_map/all_to_all | solution.py:303
  15.3 4.8 %collective-permute-start = (bf16[2048,128]{1,0:T(8,128)(2,1)S(1)}, bf16[2048,128]{1,0:T(8,128)(2,1)S(1)}, u32[]{:S(2)}, u32[]{:S(2)}) collective-permute-start(bf16[2048,128]{1,0:T(8,128)(2,1)S(1)} %copy-done.1), channel_id=1, source_target_pairs={{0,8},{8,0},{1,9},{9,1},{2,10},{10,2},{3,11},{11,3},{4,12},{12,4},... | collective-permute-start | bytes 1572872 | tf_op jit(solution)/shard_map/ppermute | solution.py:308
  18.2 3.8 %collective-permute-start.1 = (bf16[2048,128]{1,0:T(8,128)(2,1)S(1)}, bf16[2048,128]{1,0:T(8,128)(2,1)S(1)}, u32[]{:S(2)}, u32[]{:S(2)}) collective-permute-start(bf16[2048,128]{1,0:T(8,128)(2,1)S(1)} %copy-done.2), channel_id=1, source_target_pairs={{0,8},{8,0},{1,9},{9,1},{2,10},{10,2},{3,11},{11,3},{4,12},{12,4},... | collective-permute-start | bytes 1572872 | tf_op jit(solution)/shard_map/ppermute | solution.py:309
  36.7 7.5 %collective-permute-start.2 = (bf16[128,1152]{1,0:T(8,128)(2,1)S(1)}, bf16[128,1152]{1,0:T(8,128)(2,1)S(1)}, u32[]{:S(2)}, u32[]{:S(2)}) collective-permute-start(bf16[128,1152]{1,0:T(8,128)(2,1)S(1)} %attend.3), channel_id=1, source_target_pairs={{0,16},{16,0},{1,17},{17,1},{2,18},{18,2},{3,19},{19,3},{4,20},{20... | collective-permute-start | bytes 884744 | tf_op jit(solution)/shard_map/ppermute | solution.py:312
  45.7 8.7 %copy-start = (bf16[1024,128]{1,0:T(8,128)(2,1)S(1)}, bf16[1024,128]{1,0:T(8,128)(2,1)}, u32[]{:S(2)}) copy-start(bf16[1024,128]{1,0:T(8,128)(2,1)} %w_ref.1) | copy-start | bytes 786436
  45.7 17.6 %all-to-all-start.1 = ((bf16[16,8,1152]{2,1,0:T(8,128)(2,1)}), bf16[16,8,1152]{2,1,0:T(8,128)(2,1)S(1)}, u32[]{:S(2)}, u32[]{:S(2)}) async-start(bf16[16,8,1152]{2,1,0:T(8,128)(2,1)} %bitcast.2), calls=%async_computation.1 | async-start | bytes 589824 | tf_op jit(solution)/shard_map/all_to_all | solution.py:303
  54.3 34.1 %collective-permute-start.4 = (bf16[1024,128]{1,0:T(8,128)(2,1)S(1)}, bf16[1024,128]{1,0:T(8,128)(2,1)S(1)}, u32[]{:S(2)}, u32[]{:S(2)}) collective-permute-start(bf16[1024,128]{1,0:T(8,128)(2,1)S(1)} %copy-done), channel_id=1, source_target_pairs={{0,16},{16,0},{1,17},{17,1},{2,18},{18,2},{3,19},{19,3},{4,20},{20... | collective-permute-start | bytes 786440 | tf_op jit(solution)/shard_map/ppermute | solution.py:315
  64.4 27.5 %all-to-all-start.2 = ((bf16[16,8,1024]{2,1,0:T(8,128)(2,1)}), bf16[16,8,1024]{2,1,0:T(8,128)(2,1)S(1)}, u32[]{:S(2)}, u32[]{:S(2)}) async-start(bf16[16,8,1024]{2,1,0:T(8,128)(2,1)} %bitcast.4), calls=%async_computation.2 | async-start | bytes 524288 | tf_op jit(solution)/shard_map/all_to_all | solution.py:303
  68.5 21.9 %collective-permute-start.3 = (bf16[1024,128]{1,0:T(8,128)(2,1)S(1)}, bf16[1024,128]{1,0:T(8,128)(2,1)S(1)}, u32[]{:S(2)}, u32[]{:S(2)}) collective-permute-start(bf16[1024,128]{1,0:T(8,128)(2,1)S(1)} %copy-done), channel_id=1, source_target_pairs={{0,8},{8,0},{1,9},{9,1},{2,10},{10,2},{3,11},{11,3},{4,12},{12,4},... | collective-permute-start | bytes 786440 | tf_op jit(solution)/shard_map/ppermute | solution.py:314
  88.5 3.4 %collective-permute-start.5 = (bf16[1024,128]{1,0:T(8,128)(2,1)S(1)}, bf16[1024,128]{1,0:T(8,128)(2,1)S(1)}, u32[]{:S(2)}, u32[]{:S(2)}) collective-permute-start(bf16[1024,128]{1,0:T(8,128)(2,1)S(1)} %collective-permute-done.4.w_chip), channel_id=1, source_target_pairs={{0,8},{8,0},{1,9},{9,1},{2,10},{10,2},{3,11},{11,3},{4,12},{12,4},... | collective-permute-start | bytes 786440 | tf_op jit(solution)/shard_map/ppermute | solution.py:316

commit v7 on v5

--- a/solution.py
+++ b/solution.py
@@ -110,7 +110,7 @@
         return jnp.maximum(unsafe, far)
 
     unsafe = jnp.zeros((many, 1), jnp.float32)
-    unsafe = lax.fori_loop(0, rows // ROW_BLOCK, quick, unsafe)
+    unsafe = lax.fori_loop(0, rows // ROW_BLOCK, quick, unsafe, unroll=True)
 
     @pl.when(jnp.logical_not(jnp.max(unsafe) < REACH))
     def _():

time: 118 us -> 118 us (level)
  transfers between devices with their start and end apart: 9 -> 9, of which waited for: 4 -> 5; matrix products, arithmetic and copies ran while one was open for 0% -> 0% of each run, Pallas kernels for 6% -> 5%
where the time goes in v7:
time: 118 us; the launch traced here: 117 us
  starting transfers between devices  55.8 us (47%)
  blocking collectives  24.6 us (21%)
  waiting for transfers between devices  21.1 us (18%)
  Pallas kernels  15.4 us (13%)
    all_to_all x1, blocking collectives, exchange(): return lax.all_to_all(x, axis, 0, 0, tiled=True)  24.6 us
    all_to_all x3, starting transfers between devices, exchange(): return lax.all_to_all(x, axis, 0, 0, tiled=True)  24.3 us
    ppermute x1, starting transfers between devices, shards(): w_core = lax.ppermute(out_weight, 'c', SWAP)  19.9 us
    all_to_all x3, waiting for transfers between devices, exchange(): return lax.all_to_all(x, axis, 0, 0, tiled=True)  17.3 us
    pallas_call x2, Pallas kernels, attend(): pl.pallas_call(functools.partial(attend_kernel, 256, whose), in_specs=[vm...  9.97 us
    ppermute x1, starting transfers between devices, shards(): k_other = lax.ppermute(keys, 'c', SWAP)  2.86 us
    ppermute x1, starting transfers between devices, shards(): w_chip = lax.ppermute(out_weight, 'zl', SWAP)  2.75 us
  transfers between devices with their start and end apart: 9, of which 5 were waited for; matrix products, arithmetic and copies ran while one was open for 0% of the time, Pallas kernels for 5%

profile of v7, /device:TPU:1, one launch (start us, length us, event | category | flops | bytes accessed | tf_op | source)
XLA Modules:
  0.0 117.0 jit_solution(11898622381342098395)
XLA Ops:
  0.0 1.7 %pack.1 = bf16[256,1152]{1,0:T(8,128)(2,1)} custom-call(bf16[8,1024]{1,0:T(8,128)(2,1)} %q_ref.1, s32[8]{0:T(128)} %cut_ref.1), custom_call_target="tpu_custom_call" | custom-call | tf_op jit(solution)/shard_map/pack/pallas_call | solution.py:217
  1.7 0.0 copy-start.1
  1.7 0.0 copy-start.2
  1.7 13.6 %all-to-all-start = ((bf16[32,8,1152]{2,1,0:T(8,128)(2,1)}), bf16[32,8,1152]{2,1,0:T(8,128)(2,1)S(1)}, u32[]{:S(2)}, u32[]{:S(2)}) async-start(bf16[32,8,1152]{2,1,0:T(8,128)(2,1)} %bitcast.14), calls=%async_computation | async-start | bytes 1179648 | tf_op jit(solution)/shard_map/all_to_all | solution.py:311
  15.3 0.0 copy-done.1
  15.3 2.9 %collective-permute-start = (bf16[2048,128]{1,0:T(8,128)(2,1)S(1)}, bf16[2048,128]{1,0:T(8,128)(2,1)S(1)}, u32[]{:S(2)}, u32[]{:S(2)}) collective-permute-start(bf16[2048,128]{1,0:T(8,128)(2,1)S(1)} %copy-done.1), channel_id=1, source_target_pairs={{0,8},{8,0},{1,9},{9,1},{2,10},{10,2},{3,11},{11,3},{4,12},{12,4},... | collective-permute-start | bytes 1572872 | tf_op jit(solution)/shard_map/ppermute | solution.py:316
  18.2 0.0 copy-done.2
  18.2 1.9 %collective-permute-start.1 = (bf16[2048,128]{1,0:T(8,128)(2,1)S(1)}, bf16[2048,128]{1,0:T(8,128)(2,1)S(1)}, u32[]{:S(2)}, u32[]{:S(2)}) collective-permute-start(bf16[2048,128]{1,0:T(8,128)(2,1)S(1)} %copy-done.2), channel_id=1, source_target_pairs={{0,8},{8,0},{1,9},{9,1},{2,10},{10,2},{3,11},{11,3},{4,12},{12,4},... | collective-permute-start | bytes 1572872 | tf_op jit(solution)/shard_map/ppermute | solution.py:317
  20.1 0.0 collective-permute-done.k_other
  20.1 1.9 %collective-permute-done.1.v_other = bf16[2048,128]{1,0:T(8,128)(2,1)S(1)} collective-permute-done((bf16[2048,128]{1,0:T(8,128)(2,1)S(1)}, bf16[2048,128]{1,0:T(8,128)(2,1)S(1)}, u32[]{:S(2)}, u32[]{:S(2)}) %collective-permute-start.1) | collective-permute-done | bytes 524320 | tf_op jit(solution)/shard_map/ppermute | solution.py:317
  22.0 11.2 %all-to-all-done = bf16[32,8,1152]{2,1,0:T(8,128)(2,1)S(1)} async-done(((bf16[32,8,1152]{2,1,0:T(8,128)(2,1)}), bf16[32,8,1152]{2,1,0:T(8,128)(2,1)S(1)}, u32[]{:S(2)}, u32[]{:S(2)}) %all-to-all-start) | async-done | bytes 589856 | tf_op jit(solution)/shard_map/all_to_all | solution.py:311
  33.2 5.0 %attend.3 = bf16[128,1152]{1,0:T(8,128)(2,1)S(1)} custom-call(bf16[256,1152]{1,0:T(8,128)(2,1)S(1)} %bitcast.10, bf16[2048,128]{1,0:T(8,128)(2,1)S(1)} %copy-done.1, bf16[2048,128]{1,0:T(8,128)(2,1)S(1)} %copy-done.2, bf16[2048,128]{1,0:T(8,128)(2,1)S(1)} %collective-permute-done.k_other, bf16[2048,128]{1,0:T(8,128)(2,1)S(1)} %collective-permute-done.1.v_other), custom_call_target="tpu_custom_call" | custom-call | flops 4294967296 | bytes 2097152 | tf_op jit(solution)/shard_map/attend/pallas_call | solution.py:137
  38.2 2.1 %collective-permute-start.2 = (bf16[128,1152]{1,0:T(8,128)(2,1)S(1)}, bf16[128,1152]{1,0:T(8,128)(2,1)S(1)}, u32[]{:S(2)}, u32[]{:S(2)}) collective-permute-start(bf16[128,1152]{1,0:T(8,128)(2,1)S(1)} %attend.3), channel_id=1, source_target_pairs={{0,16},{16,0},{1,17},{17,1},{2,18},{18,2},{3,19},{19,3},{4,20},{20... | collective-permute-start | bytes 884744 | tf_op jit(solution)/shard_map/ppermute | solution.py:320
  40.3 5.0 %attend.2.a_ref = bf16[128,1152]{1,0:T(8,128)(2,1)S(1)} custom-call(bf16[256,1152]{1,0:T(8,128)(2,1)S(1)} %bitcast.11, bf16[2048,128]{1,0:T(8,128)(2,1)S(1)} %copy-done.1, bf16[2048,128]{1,0:T(8,128)(2,1)S(1)} %copy-done.2, bf16[2048,128]{1,0:T(8,128)(2,1)S(1)} %collective-permute-done.k_other, bf16[2048,128]{1,0:T(8,128)(2,1)S(1)} %collective-permute-done.1.v_other), custom_call_target="tpu_custom_call" | custom-call | flops 4294967296 | bytes 2097152 | tf_op jit(solution)/shard_map/attend/pallas_call | solution.py:137
  45.3 0.4 collective-permute-done.2.b_ref
  45.6 1.6 %merge.1 = bf16[128,1152]{1,0:T(8,128)(2,1)} custom-call(bf16[128,1152]{1,0:T(8,128)(2,1)S(1)} %attend.2.a_ref, bf16[128,1152]{1,0:T(8,128)(2,1)S(1)} %collective-permute-done.2.b_ref), custom_call_target="tpu_custom_call" | custom-call | tf_op jit(solution)/shard_map/merge/pallas_call | solution.py:188
  47.2 0.0 copy-start
  47.2 6.6 %all-to-all-start.1 = ((bf16[16,8,1152]{2,1,0:T(8,128)(2,1)}), bf16[16,8,1152]{2,1,0:T(8,128)(2,1)S(1)}, u32[]{:S(2)}, u32[]{:S(2)}) async-start(bf16[16,8,1152]{2,1,0:T(8,128)(2,1)} %bitcast.2), calls=%async_computation.1 | async-start | bytes 589824 | tf_op jit(solution)/shard_map/all_to_all | solution.py:311
  53.8 0.0 copy-done
  53.8 2.7 %collective-permute-start.4 = (bf16[1024,128]{1,0:T(8,128)(2,1)S(1)}, bf16[1024,128]{1,0:T(8,128)(2,1)S(1)}, u32[]{:S(2)}, u32[]{:S(2)}) collective-permute-start(bf16[1024,128]{1,0:T(8,128)(2,1)S(1)} %copy-done), channel_id=1, source_target_pairs={{0,16},{16,0},{1,17},{17,1},{2,18},{18,2},{3,19},{19,3},{4,20},{20... | collective-permute-start | bytes 786440 | tf_op jit(solution)/shard_map/ppermute | solution.py:323
  56.6 6.1 %all-to-all-done.1 = bf16[16,8,1152]{2,1,0:T(8,128)(2,1)S(1)} async-done(((bf16[16,8,1152]{2,1,0:T(8,128)(2,1)}), bf16[16,8,1152]{2,1,0:T(8,128)(2,1)S(1)}, u32[]{:S(2)}, u32[]{:S(2)}) %all-to-all-start.1) | async-done | bytes 294944 | tf_op jit(solution)/shard_map/all_to_all | solution.py:311
  62.7 1.1 combine.1
  63.8 4.2 %all-to-all-start.2 = ((bf16[16,8,1024]{2,1,0:T(8,128)(2,1)}), bf16[16,8,1024]{2,1,0:T(8,128)(2,1)S(1)}, u32[]{:S(2)}, u32[]{:S(2)}) async-start(bf16[16,8,1024]{2,1,0:T(8,128)(2,1)} %bitcast.4), calls=%async_computation.2 | async-start | bytes 524288 | tf_op jit(solution)/shard_map/all_to_all | solution.py:311
  68.0 19.9 %collective-permute-start.3 = (bf16[1024,128]{1,0:T(8,128)(2,1)S(1)}, bf16[1024,128]{1,0:T(8,128)(2,1)S(1)}, u32[]{:S(2)}, u32[]{:S(2)}) collective-permute-start(bf16[1024,128]{1,0:T(8,128)(2,1)S(1)} %copy-done), channel_id=1, source_target_pairs={{0,8},{8,0},{1,9},{9,1},{2,10},{10,2},{3,11},{11,3},{4,12},{12,4},... | collective-permute-start | bytes 786440 | tf_op jit(solution)/shard_map/ppermute | solution.py:322
  87.9 0.0 collective-permute-done.4.w_chip
  87.9 1.9 %collective-permute-start.5 = (bf16[1024,128]{1,0:T(8,128)(2,1)S(1)}, bf16[1024,128]{1,0:T(8,128)(2,1)S(1)}, u32[]{:S(2)}, u32[]{:S(2)}) collective-permute-start(bf16[1024,128]{1,0:T(8,128)(2,1)S(1)} %collective-permute-done.4.w_chip), channel_id=1, source_target_pairs={{0,8},{8,0},{1,9},{9,1},{2,10},{10,2},{3,11},{11,3},{4,12},{12,4},... | collective-permute-start | bytes 786440 | tf_op jit(solution)/shard_map/ppermute | solution.py:324
  89.8 0.0 collective-permute-done.3.w_core
  89.8 1.5 %collective-permute-done.5.w_both = bf16[1024,128]{1,0:T(8,128)(2,1)S(1)} collective-permute-done((bf16[1024,128]{1,0:T(8,128)(2,1)S(1)}, bf16[1024,128]{1,0:T(8,128)(2,1)S(1)}, u32[]{:S(2)}, u32[]{:S(2)}) %collective-permute-start.5) | collective-permute-done | bytes 262176 | tf_op jit(solution)/shard_map/ppermute | solution.py:324
  91.3 0.0 all-to-all-done.2
  91.3 0.4 project.1
  91.8 24.6 %all_to_all.44 = bf16[32,16,128]{2,1,0:T(8,128)(2,1)S(1)} all-to-all(bf16[32,16,128]{2,1,0:T(8,128)(2,1)S(1)} %bitcast.13), channel_id=1, replica_groups=mesh['yc'=2,'yb'=2,'ya'=2,'zh'=2,'zl'=2,'c'=2,'w'=2,'x'=4] {'w','x','zl'..., dimensions={0} | all-to-all | bytes 262144 | tf_op jit(solution)/shard_map/all_to_all | solution.py:311
  116.4 0.6 total.1
Async XLA Ops:
  1.7 13.6 %copy-start.1 = (bf16[2048,128]{1,0:T(8,128)(2,1)S(1)}, bf16[2048,128]{1,0:T(8,128)(2,1)}, u32[]{:S(2)}) copy-start(bf16[2048,128]{1,0:T(8,128)(2,1)} %k_mine.3) | copy-start | bytes 1572868
  1.7 16.5 %copy-start.2 = (bf16[2048,128]{1,0:T(8,128)(2,1)S(1)}, bf16[2048,128]{1,0:T(8,128)(2,1)}, u32[]{:S(2)}) copy-start(bf16[2048,128]{1,0:T(8,128)(2,1)} %v_mine.3) | copy-start | bytes 1572868
  1.7 31.5 %all-to-all-start = ((bf16[32,8,1152]{2,1,0:T(8,128)(2,1)}), bf16[32,8,1152]{2,1,0:T(8,128)(2,1)S(1)}, u32[]{:S(2)}, u32[]{:S(2)}) async-start(bf16[32,8,1152]{2,1,0:T(8,128)(2,1)} %bitcast.14), calls=%async_computation | async-start | bytes 1179648 | tf_op jit(solution)/shard_map/all_to_all | solution.py:311
  15.3 4.8 %collective-permute-start = (bf16[2048,128]{1,0:T(8,128)(2,1)S(1)}, bf16[2048,128]{1,0:T(8,128)(2,1)S(1)}, u32[]{:S(2)}, u32[]{:S(2)}) collective-permute-start(bf16[2048,128]{1,0:T(8,128)(2,1)S(1)} %copy-done.1), channel_id=1, source_target_pairs={{0,8},{8,0},{1,9},{9,1},{2,10},{10,2},{3,11},{11,3},{4,12},{12,4},... | collective-permute-start | bytes 1572872 | tf_op jit(solution)/shard_map/ppermute | solution.py:316
  18.2 3.8 %collective-permute-start.1 = (bf16[2048,128]{1,0:T(8,128)(2,1)S(1)}, bf16[2048,128]{1,0:T(8,128)(2,1)S(1)}, u32[]{:S(2)}, u32[]{:S(2)}) collective-permute-start(bf16[2048,128]{1,0:T(8,128)(2,1)S(1)} %copy-done.2), channel_id=1, source_target_pairs={{0,8},{8,0},{1,9},{9,1},{2,10},{10,2},{3,11},{11,3},{4,12},{12,4},... | collective-permute-start | bytes 1572872 | tf_op jit(solution)/shard_map/ppermute | solution.py:317
  38.2 7.5 %collective-permute-start.2 = (bf16[128,1152]{1,0:T(8,128)(2,1)S(1)}, bf16[128,1152]{1,0:T(8,128)(2,1)S(1)}, u32[]{:S(2)}, u32[]{:S(2)}) collective-permute-start(bf16[128,1152]{1,0:T(8,128)(2,1)S(1)} %attend.3), channel_id=1, source_target_pairs={{0,16},{16,0},{1,17},{17,1},{2,18},{18,2},{3,19},{19,3},{4,20},{20... | collective-permute-start | bytes 884744 | tf_op jit(solution)/shard_map/ppermute | solution.py:320
  47.2 6.6 %copy-start = (bf16[1024,128]{1,0:T(8,128)(2,1)S(1)}, bf16[1024,128]{1,0:T(8,128)(2,1)}, u32[]{:S(2)}) copy-start(bf16[1024,128]{1,0:T(8,128)(2,1)} %w_ref.1) | copy-start | bytes 786436
  47.2 15.4 %all-to-all-start.1 = ((bf16[16,8,1152]{2,1,0:T(8,128)(2,1)}), bf16[16,8,1152]{2,1,0:T(8,128)(2,1)S(1)}, u32[]{:S(2)}, u32[]{:S(2)}) async-start(bf16[16,8,1152]{2,1,0:T(8,128)(2,1)} %bitcast.2), calls=%async_computation.1 | async-start | bytes 589824 | tf_op jit(solution)/shard_map/all_to_all | solution.py:311
  53.8 34.1 %collective-permute-start.4 = (bf16[1024,128]{1,0:T(8,128)(2,1)S(1)}, bf16[1024,128]{1,0:T(8,128)(2,1)S(1)}, u32[]{:S(2)}, u32[]{:S(2)}) collective-permute-start(bf16[1024,128]{1,0:T(8,128)(2,1)S(1)} %copy-done), channel_id=1, source_target_pairs={{0,16},{16,0},{1,17},{17,1},{2,18},{18,2},{3,19},{19,3},{4,20},{20... | collective-permute-start | bytes 786440 | tf_op jit(solution)/shard_map/ppermute | solution.py:323
  63.8 27.5 %all-to-all-start.2 = ((bf16[16,8,1024]{2,1,0:T(8,128)(2,1)}), bf16[16,8,1024]{2,1,0:T(8,128)(2,1)S(1)}, u32[]{:S(2)}, u32[]{:S(2)}) async-start(bf16[16,8,1024]{2,1,0:T(8,128)(2,1)} %bitcast.4), calls=%async_computation.2 | async-start | bytes 524288 | tf_op jit(solution)/shard_map/all_to_all | solution.py:311
  68.0 21.8 %collective-permute-start.3 = (bf16[1024,128]{1,0:T(8,128)(2,1)S(1)}, bf16[1024,128]{1,0:T(8,128)(2,1)S(1)}, u32[]{:S(2)}, u32[]{:S(2)}) collective-permute-start(bf16[1024,128]{1,0:T(8,128)(2,1)S(1)} %copy-done), channel_id=1, source_target_pairs={{0,8},{8,0},{1,9},{9,1},{2,10},{10,2},{3,11},{11,3},{4,12},{12,4},... | collective-permute-start | bytes 786440 | tf_op jit(solution)/shard_map/ppermute | solution.py:322
  87.9 3.4 %collective-permute-start.5 = (bf16[1024,128]{1,0:T(8,128)(2,1)S(1)}, bf16[1024,128]{1,0:T(8,128)(2,1)S(1)}, u32[]{:S(2)}, u32[]{:S(2)}) collective-permute-start(bf16[1024,128]{1,0:T(8,128)(2,1)S(1)} %collective-permute-done.4.w_chip), channel_id=1, source_target_pairs={{0,8},{8,0},{1,9},{9,1},{2,10},{10,2},{3,11},{11,3},{4,12},{12,4},... | collective-permute-start | bytes 786440 | tf_op jit(solution)/shard_map/ppermute | solution.py:324

commit v8 on v7

--- a/solution.py
+++ b/solution.py
@@ -270,7 +270,7 @@
         part = jnp.dot(attended, weight[...], preferred_element_type=jnp.float32)
         for y in range(half // 8):
             pair = [part[8 * y : 8 * y + 8], part[half + 8 * y : half + 8 * y + 8]]
-            at = pl.multiple_of((y * 4 + there * 2 + that) * 16, 16)
+            at = pl.multiple_of(((y % 4 * 2 + y // 4) * 4 + there * 2 + that) * 16, 16)
             o_ref[pl.ds(at, 16), :] = jnp.concatenate(pair, axis=0).astype(o_ref.dtype)
 
 
@@ -324,7 +324,7 @@
     w_both = lax.ppermute(w_chip, "c", SWAP)
     attended = exchange(combine(parts, far), FAR)
     sums = project(attended, out_weight, w_core, w_chip, w_both)
-    return total_of(exchange(sums, HEAD + NEAR))
+    return total_of(exchange(sums, ("x", "w") + NEAR))
 
 
 def solution(mesh):

time: 118 us -> 118 us (level)
  no operation moved by 1% of the time
where the time goes in v8:
time: 118 us; the launch traced here: 117 us
  starting transfers between devices  55.3 us (47%)
  blocking collectives  24.3 us (21%)
  waiting for transfers between devices  21.5 us (18%)
  Pallas kernels  15.4 us (13%)
    all_to_all x1, blocking collectives, exchange(): return lax.all_to_all(x, axis, 0, 0, tiled=True)  24.3 us
    all_to_all x3, starting transfers between devices, exchange(): return lax.all_to_all(x, axis, 0, 0, tiled=True)  24.3 us
    ppermute x1, starting transfers between devices, shards(): w_core = lax.ppermute(out_weight, 'c', SWAP)  19.9 us
    all_to_all x3, waiting for transfers between devices, exchange(): return lax.all_to_all(x, axis, 0, 0, tiled=True)  17.8 us
    pallas_call x2, Pallas kernels, attend(): pl.pallas_call(functools.partial(attend_kernel, 256, whose), in_specs=[vm...  9.97 us
    ppermute x1, starting transfers between devices, shards(): k_other = lax.ppermute(keys, 'c', SWAP)  2.86 us
    ppermute x1, starting transfers between devices, shards(): w_chip = lax.ppermute(out_weight, 'zl', SWAP)  2.38 us
  transfers between devices with their start and end apart: 9, of which 5 were waited for; matrix products, arithmetic and copies ran while one was open for 0% of the time, Pallas kernels for 5%

profile of v8, /device:TPU:1, one launch (start us, length us, event | category | flops | bytes accessed | tf_op | source)
XLA Modules:
  0.0 116.7 jit_solution(4234483908418628331)
XLA Ops:
  0.0 1.7 %pack.1 = bf16[256,1152]{1,0:T(8,128)(2,1)} custom-call(bf16[8,1024]{1,0:T(8,128)(2,1)} %q_ref.1, s32[8]{0:T(128)} %cut_ref.1), custom_call_target="tpu_custom_call" | custom-call | tf_op jit(solution)/shard_map/pack/pallas_call | solution.py:217
  1.7 0.0 copy-start.1
  1.7 0.0 copy-start.2
  1.7 13.6 %all-to-all-start = ((bf16[32,8,1152]{2,1,0:T(8,128)(2,1)}), bf16[32,8,1152]{2,1,0:T(8,128)(2,1)S(1)}, u32[]{:S(2)}, u32[]{:S(2)}) async-start(bf16[32,8,1152]{2,1,0:T(8,128)(2,1)} %bitcast.14), calls=%async_computation | async-start | bytes 1179648 | tf_op jit(solution)/shard_map/all_to_all | solution.py:311
  15.3 0.0 copy-done.1
  15.3 2.9 %collective-permute-start = (bf16[2048,128]{1,0:T(8,128)(2,1)S(1)}, bf16[2048,128]{1,0:T(8,128)(2,1)S(1)}, u32[]{:S(2)}, u32[]{:S(2)}) collective-permute-start(bf16[2048,128]{1,0:T(8,128)(2,1)S(1)} %copy-done.1), channel_id=1, source_target_pairs={{0,8},{8,0},{1,9},{9,1},{2,10},{10,2},{3,11},{11,3},{4,12},{12,4},... | collective-permute-start | bytes 1572872 | tf_op jit(solution)/shard_map/ppermute | solution.py:316
  18.2 0.0 copy-done.2
  18.2 1.9 %collective-permute-start.1 = (bf16[2048,128]{1,0:T(8,128)(2,1)S(1)}, bf16[2048,128]{1,0:T(8,128)(2,1)S(1)}, u32[]{:S(2)}, u32[]{:S(2)}) collective-permute-start(bf16[2048,128]{1,0:T(8,128)(2,1)S(1)} %copy-done.2), channel_id=1, source_target_pairs={{0,8},{8,0},{1,9},{9,1},{2,10},{10,2},{3,11},{11,3},{4,12},{12,4},... | collective-permute-start | bytes 1572872 | tf_op jit(solution)/shard_map/ppermute | solution.py:317
  20.1 0.0 collective-permute-done.k_other
  20.1 1.9 %collective-permute-done.1.v_other = bf16[2048,128]{1,0:T(8,128)(2,1)S(1)} collective-permute-done((bf16[2048,128]{1,0:T(8,128)(2,1)S(1)}, bf16[2048,128]{1,0:T(8,128)(2,1)S(1)}, u32[]{:S(2)}, u32[]{:S(2)}) %collective-permute-start.1) | collective-permute-done | bytes 524320 | tf_op jit(solution)/shard_map/ppermute | solution.py:317
  22.0 11.2 %all-to-all-done = bf16[32,8,1152]{2,1,0:T(8,128)(2,1)S(1)} async-done(((bf16[32,8,1152]{2,1,0:T(8,128)(2,1)}), bf16[32,8,1152]{2,1,0:T(8,128)(2,1)S(1)}, u32[]{:S(2)}, u32[]{:S(2)}) %all-to-all-start) | async-done | bytes 589856 | tf_op jit(solution)/shard_map/all_to_all | solution.py:311
  33.2 5.0 %attend.3 = bf16[128,1152]{1,0:T(8,128)(2,1)S(1)} custom-call(bf16[256,1152]{1,0:T(8,128)(2,1)S(1)} %bitcast.10, bf16[2048,128]{1,0:T(8,128)(2,1)S(1)} %copy-done.1, bf16[2048,128]{1,0:T(8,128)(2,1)S(1)} %copy-done.2, bf16[2048,128]{1,0:T(8,128)(2,1)S(1)} %collective-permute-done.k_other, bf16[2048,128]{1,0:T(8,128)(2,1)S(1)} %collective-permute-done.1.v_other), custom_call_target="tpu_custom_call" | custom-call | flops 4294967296 | bytes 2097152 | tf_op jit(solution)/shard_map/attend/pallas_call | solution.py:137
  38.2 2.1 %collective-permute-start.2 = (bf16[128,1152]{1,0:T(8,128)(2,1)S(1)}, bf16[128,1152]{1,0:T(8,128)(2,1)S(1)}, u32[]{:S(2)}, u32[]{:S(2)}) collective-permute-start(bf16[128,1152]{1,0:T(8,128)(2,1)S(1)} %attend.3), channel_id=1, source_target_pairs={{0,16},{16,0},{1,17},{17,1},{2,18},{18,2},{3,19},{19,3},{4,20},{20... | collective-permute-start | bytes 884744 | tf_op jit(solution)/shard_map/ppermute | solution.py:320
  40.3 5.0 %attend.2.a_ref = bf16[128,1152]{1,0:T(8,128)(2,1)S(1)} custom-call(bf16[256,1152]{1,0:T(8,128)(2,1)S(1)} %bitcast.11, bf16[2048,128]{1,0:T(8,128)(2,1)S(1)} %copy-done.1, bf16[2048,128]{1,0:T(8,128)(2,1)S(1)} %copy-done.2, bf16[2048,128]{1,0:T(8,128)(2,1)S(1)} %collective-permute-done.k_other, bf16[2048,128]{1,0:T(8,128)(2,1)S(1)} %collective-permute-done.1.v_other), custom_call_target="tpu_custom_call" | custom-call | flops 4294967296 | bytes 2097152 | tf_op jit(solution)/shard_map/attend/pallas_call | solution.py:137
  45.3 0.4 collective-permute-done.2.b_ref
  45.6 1.6 %merge.1 = bf16[128,1152]{1,0:T(8,128)(2,1)} custom-call(bf16[128,1152]{1,0:T(8,128)(2,1)S(1)} %attend.2.a_ref, bf16[128,1152]{1,0:T(8,128)(2,1)S(1)} %collective-permute-done.2.b_ref), custom_call_target="tpu_custom_call" | custom-call | tf_op jit(solution)/shard_map/merge/pallas_call | solution.py:188
  47.2 0.0 copy-start
  47.2 6.6 %all-to-all-start.1 = ((bf16[16,8,1152]{2,1,0:T(8,128)(2,1)}), bf16[16,8,1152]{2,1,0:T(8,128)(2,1)S(1)}, u32[]{:S(2)}, u32[]{:S(2)}) async-start(bf16[16,8,1152]{2,1,0:T(8,128)(2,1)} %bitcast.2), calls=%async_computation.1 | async-start | bytes 589824 | tf_op jit(solution)/shard_map/all_to_all | solution.py:311
  53.8 0.0 copy-done
  53.8 2.4 %collective-permute-start.4 = (bf16[1024,128]{1,0:T(8,128)(2,1)S(1)}, bf16[1024,128]{1,0:T(8,128)(2,1)S(1)}, u32[]{:S(2)}, u32[]{:S(2)}) collective-permute-start(bf16[1024,128]{1,0:T(8,128)(2,1)S(1)} %copy-done), channel_id=1, source_target_pairs={{0,16},{16,0},{1,17},{17,1},{2,18},{18,2},{3,19},{19,3},{4,20},{20... | collective-permute-start | bytes 786440 | tf_op jit(solution)/shard_map/ppermute | solution.py:323
  56.2 6.5 %all-to-all-done.1 = bf16[16,8,1152]{2,1,0:T(8,128)(2,1)S(1)} async-done(((bf16[16,8,1152]{2,1,0:T(8,128)(2,1)}), bf16[16,8,1152]{2,1,0:T(8,128)(2,1)S(1)}, u32[]{:S(2)}, u32[]{:S(2)}) %all-to-all-start.1) | async-done | bytes 294944 | tf_op jit(solution)/shard_map/all_to_all | solution.py:311
  62.7 1.1 combine.1
  63.9 4.1 %all-to-all-start.2 = ((bf16[16,8,1024]{2,1,0:T(8,128)(2,1)}), bf16[16,8,1024]{2,1,0:T(8,128)(2,1)S(1)}, u32[]{:S(2)}, u32[]{:S(2)}) async-start(bf16[16,8,1024]{2,1,0:T(8,128)(2,1)} %bitcast.4), calls=%async_computation.2 | async-start | bytes 524288 | tf_op jit(solution)/shard_map/all_to_all | solution.py:311
  68.0 19.9 %collective-permute-start.3 = (bf16[1024,128]{1,0:T(8,128)(2,1)S(1)}, bf16[1024,128]{1,0:T(8,128)(2,1)S(1)}, u32[]{:S(2)}, u32[]{:S(2)}) collective-permute-start(bf16[1024,128]{1,0:T(8,128)(2,1)S(1)} %copy-done), channel_id=1, source_target_pairs={{0,8},{8,0},{1,9},{9,1},{2,10},{10,2},{3,11},{11,3},{4,12},{12,4},... | collective-permute-start | bytes 786440 | tf_op jit(solution)/shard_map/ppermute | solution.py:322
  87.9 0.0 collective-permute-done.4.w_chip
  87.9 1.9 %collective-permute-start.5 = (bf16[1024,128]{1,0:T(8,128)(2,1)S(1)}, bf16[1024,128]{1,0:T(8,128)(2,1)S(1)}, u32[]{:S(2)}, u32[]{:S(2)}) collective-permute-start(bf16[1024,128]{1,0:T(8,128)(2,1)S(1)} %collective-permute-done.4.w_chip), channel_id=1, source_target_pairs={{0,8},{8,0},{1,9},{9,1},{2,10},{10,2},{3,11},{11,3},{4,12},{12,4},... | collective-permute-start | bytes 786440 | tf_op jit(solution)/shard_map/ppermute | solution.py:324
  89.8 0.0 collective-permute-done.3.w_core
  89.8 1.5 %collective-permute-done.5.w_both = bf16[1024,128]{1,0:T(8,128)(2,1)S(1)} collective-permute-done((bf16[1024,128]{1,0:T(8,128)(2,1)S(1)}, bf16[1024,128]{1,0:T(8,128)(2,1)S(1)}, u32[]{:S(2)}, u32[]{:S(2)}) %collective-permute-start.5) | collective-permute-done | bytes 262176 | tf_op jit(solution)/shard_map/ppermute | solution.py:324
  91.3 0.0 all-to-all-done.2
  91.3 0.4 project.1
  91.8 24.3 %all_to_all.44 = bf16[32,16,128]{2,1,0:T(8,128)(2,1)S(1)} all-to-all(bf16[32,16,128]{2,1,0:T(8,128)(2,1)S(1)} %bitcast.13), channel_id=1, replica_groups=mesh['yc'=2,'yb'=2,'ya'=2,'zh'=2,'zl'=2,'c'=2,'w'=2,'x'=4] {'x','w','zl'..., dimensions={0} | all-to-all | bytes 262144 | tf_op jit(solution)/shard_map/all_to_all | solution.py:311
  116.0 0.6 total.1
Async XLA Ops:
  1.7 13.6 %copy-start.1 = (bf16[2048,128]{1,0:T(8,128)(2,1)S(1)}, bf16[2048,128]{1,0:T(8,128)(2,1)}, u32[]{:S(2)}) copy-start(bf16[2048,128]{1,0:T(8,128)(2,1)} %k_mine.3) | copy-start | bytes 1572868
  1.7 16.5 %copy-start.2 = (bf16[2048,128]{1,0:T(8,128)(2,1)S(1)}, bf16[2048,128]{1,0:T(8,128)(2,1)}, u32[]{:S(2)}) copy-start(bf16[2048,128]{1,0:T(8,128)(2,1)} %v_mine.3) | copy-start | bytes 1572868
  1.7 31.5 %all-to-all-start = ((bf16[32,8,1152]{2,1,0:T(8,128)(2,1)}), bf16[32,8,1152]{2,1,0:T(8,128)(2,1)S(1)}, u32[]{:S(2)}, u32[]{:S(2)}) async-start(bf16[32,8,1152]{2,1,0:T(8,128)(2,1)} %bitcast.14), calls=%async_computation | async-start | bytes 1179648 | tf_op jit(solution)/shard_map/all_to_all | solution.py:311
  15.3 4.8 %collective-permute-start = (bf16[2048,128]{1,0:T(8,128)(2,1)S(1)}, bf16[2048,128]{1,0:T(8,128)(2,1)S(1)}, u32[]{:S(2)}, u32[]{:S(2)}) collective-permute-start(bf16[2048,128]{1,0:T(8,128)(2,1)S(1)} %copy-done.1), channel_id=1, source_target_pairs={{0,8},{8,0},{1,9},{9,1},{2,10},{10,2},{3,11},{11,3},{4,12},{12,4},... | collective-permute-start | bytes 1572872 | tf_op jit(solution)/shard_map/ppermute | solution.py:316
  18.2 3.8 %collective-permute-start.1 = (bf16[2048,128]{1,0:T(8,128)(2,1)S(1)}, bf16[2048,128]{1,0:T(8,128)(2,1)S(1)}, u32[]{:S(2)}, u32[]{:S(2)}) collective-permute-start(bf16[2048,128]{1,0:T(8,128)(2,1)S(1)} %copy-done.2), channel_id=1, source_target_pairs={{0,8},{8,0},{1,9},{9,1},{2,10},{10,2},{3,11},{11,3},{4,12},{12,4},... | collective-permute-start | bytes 1572872 | tf_op jit(solution)/shard_map/ppermute | solution.py:317
  38.2 7.5 %collective-permute-start.2 = (bf16[128,1152]{1,0:T(8,128)(2,1)S(1)}, bf16[128,1152]{1,0:T(8,128)(2,1)S(1)}, u32[]{:S(2)}, u32[]{:S(2)}) collective-permute-start(bf16[128,1152]{1,0:T(8,128)(2,1)S(1)} %attend.3), channel_id=1, source_target_pairs={{0,16},{16,0},{1,17},{17,1},{2,18},{18,2},{3,19},{19,3},{4,20},{20... | collective-permute-start | bytes 884744 | tf_op jit(solution)/shard_map/ppermute | solution.py:320
  47.2 6.6 %copy-start = (bf16[1024,128]{1,0:T(8,128)(2,1)S(1)}, bf16[1024,128]{1,0:T(8,128)(2,1)}, u32[]{:S(2)}) copy-start(bf16[1024,128]{1,0:T(8,128)(2,1)} %w_ref.1) | copy-start | bytes 786436
  47.2 15.5 %all-to-all-start.1 = ((bf16[16,8,1152]{2,1,0:T(8,128)(2,1)}), bf16[16,8,1152]{2,1,0:T(8,128)(2,1)S(1)}, u32[]{:S(2)}, u32[]{:S(2)}) async-start(bf16[16,8,1152]{2,1,0:T(8,128)(2,1)} %bitcast.2), calls=%async_computation.1 | async-start | bytes 589824 | tf_op jit(solution)/shard_map/all_to_all | solution.py:311
  53.8 34.1 %collective-permute-start.4 = (bf16[1024,128]{1,0:T(8,128)(2,1)S(1)}, bf16[1024,128]{1,0:T(8,128)(2,1)S(1)}, u32[]{:S(2)}, u32[]{:S(2)}) collective-permute-start(bf16[1024,128]{1,0:T(8,128)(2,1)S(1)} %copy-done), channel_id=1, source_target_pairs={{0,16},{16,0},{1,17},{17,1},{2,18},{18,2},{3,19},{19,3},{4,20},{20... | collective-permute-start | bytes 786440 | tf_op jit(solution)/shard_map/ppermute | solution.py:323
  63.9 27.5 %all-to-all-start.2 = ((bf16[16,8,1024]{2,1,0:T(8,128)(2,1)}), bf16[16,8,1024]{2,1,0:T(8,128)(2,1)S(1)}, u32[]{:S(2)}, u32[]{:S(2)}) async-start(bf16[16,8,1024]{2,1,0:T(8,128)(2,1)} %bitcast.4), calls=%async_computation.2 | async-start | bytes 524288 | tf_op jit(solution)/shard_map/all_to_all | solution.py:311
  68.0 21.8 %collective-permute-start.3 = (bf16[1024,128]{1,0:T(8,128)(2,1)S(1)}, bf16[1024,128]{1,0:T(8,128)(2,1)S(1)}, u32[]{:S(2)}, u32[]{:S(2)}) collective-permute-start(bf16[1024,128]{1,0:T(8,128)(2,1)S(1)} %copy-done), channel_id=1, source_target_pairs={{0,8},{8,0},{1,9},{9,1},{2,10},{10,2},{3,11},{11,3},{4,12},{12,4},... | collective-permute-start | bytes 786440 | tf_op jit(solution)/shard_map/ppermute | solution.py:322
  87.9 3.4 %collective-permute-start.5 = (bf16[1024,128]{1,0:T(8,128)(2,1)S(1)}, bf16[1024,128]{1,0:T(8,128)(2,1)S(1)}, u32[]{:S(2)}, u32[]{:S(2)}) collective-permute-start(bf16[1024,128]{1,0:T(8,128)(2,1)S(1)} %collective-permute-done.4.w_chip), channel_id=1, source_target_pairs={{0,8},{8,0},{1,9},{9,1},{2,10},{10,2},{3,11},{11,3},{4,12},{12,4},... | collective-permute-start | bytes 786440 | tf_op jit(solution)/shard_map/ppermute | solution.py:324
